TPU v7x, 32 devices: a whole 2x2x4 slice. The times are simulated.
32 devices in a mesh: seq: 2 (over x), fsdp: 16 (over z, y, core).
Axes of the slice: x: 2, y: 2, z: 4, core: 2. Of those that a mesh axis runs over, the one named last changes fastest.
Arguments:
- inputs: bfloat16 [48, 1296, 768], P('fsdp', 'seq'), may hold values from -6 to 6
- cotangent: bfloat16 [48, 1296, 768], P('fsdp', 'seq'), may hold values from -6 to 6
- first_gain: bfloat16 [768], P('fsdp'), may hold values from 0.5 to 1.5
- first_shift: bfloat16 [768], P('fsdp'), may hold values from -3 to 3
- qkv_weight: bfloat16 [768, 2304], P('fsdp'), may hold values from -0.3125 to 0.3125
- query_bias: bfloat16 [768], P('fsdp'), may hold values from -3 to 3
- value_bias: bfloat16 [768], P('fsdp'), may hold values from -3 to 3
- proj_weight: bfloat16 [768, 768], P('fsdp'), may hold values from -3.5 to 3.5
- proj_bias: bfloat16 [768], P('fsdp'), may hold values from -3 to 3
- second_gain: bfloat16 [768], P('fsdp'), may hold values from 0.5 to 1.5
- second_shift: bfloat16 [768], P('fsdp'), may hold values from -3 to 3
- hidden_weight: bfloat16 [768, 3072], P('fsdp'), may hold values from -0.21875 to 0.21875
- hidden_bias: bfloat16 [3072], P('fsdp'), may hold values from -3 to 3
- output_weight: bfloat16 [3072, 768], P('fsdp'), may hold values from -0.109375 to 0.109375
- output_bias: bfloat16 [768], P('fsdp'), may hold values from -3 to 3
Outputs:
- block_out: bfloat16 [48, 1296, 768], P('fsdp', 'seq')
- input_grad: bfloat16 [48, 1296, 768], P('fsdp', 'seq')
- grad_first_gain: float32 [768], P('fsdp')
- grad_first_shift: float32 [768], P('fsdp')
- grad_qkv_weight: float32 [768, 2304], P('fsdp')
- grad_query_bias: float32 [768], P('fsdp')
- grad_value_bias: float32 [768], P('fsdp')
- grad_proj_weight: float32 [768, 768], P('fsdp')
- grad_proj_bias: float32 [768], P('fsdp')
- grad_second_gain: float32 [768], P('fsdp')
- grad_second_shift: float32 [768], P('fsdp')
- grad_hidden_weight: float32 [768, 3072], P('fsdp')
- grad_hidden_bias: float32 [3072], P('fsdp')
- grad_output_weight: float32 [3072, 768], P('fsdp')
- grad_output_bias: float32 [768], P('fsdp')
All inputs are finite; a program needn't handle non-finite values.
Results may differ from a plain program's by a relative error of at most 0.02.
Values may be sent and summed in bfloat16 or wider, within the bound.
No kernel may reach another device: no remote copies, remote signals or barrier semaphores. Data moves between devices by JAX's collectives and lax.ppermute only.
A program may use at most 384 MiB of HBM per device.

v0:
```python
import functools

import jax
import jax.numpy as jnp
from jax import lax
from jax.experimental import pallas as pl
from jax.experimental.pallas import tpu as pltpu
from jax.sharding import PartitionSpec as P

HEADS = 12
HEAD_DIM = 64


EPS = 1e-06


def normalize(rows, gain, shift):
    row_mean = jnp.mean(rows, -1, keepdims=True)
    centred = rows - row_mean
    variance = jnp.mean(centred * centred, -1, keepdims=True)
    scaled = lax.rsqrt(variance + EPS)
    unit = centred * scaled
    return (unit * gain + shift, unit, scaled)


def norm_back(grad_out, unit, scaled, gain):
    grad_unit = grad_out * gain
    first_mean = jnp.mean(grad_unit, -1, keepdims=True)
    second_mean = jnp.mean(grad_unit * unit, -1, keepdims=True)
    return scaled * (grad_unit - first_mean - unit * second_mean)


def gelu_exact(value):
    return jax.nn.gelu(value, approximate=False)


def column_sum(values):
    return jnp.sum(values.astype(jnp.float32), 0)


def general_body(
    inputs,
    cotangent,
    first_gain,
    first_shift,
    qkv_weight,
    query_bias,
    value_bias,
    proj_weight,
    proj_bias,
    second_gain,
    second_shift,
    hidden_weight,
    hidden_bias,
    output_weight,
    output_bias,
):
    images, local_len, width = inputs.shape
    row_count = images * local_len
    factor = HEAD_DIM ** (-0.5)
    (
        gain_one,
        shift_one,
        full_qkv,
        bias_query,
        bias_value,
        full_proj,
        bias_proj,
        gain_two,
        shift_two,
        full_hidden,
        bias_hidden,
        full_output,
        bias_output,
    ) = (
        lax.all_gather(first_gain, "fsdp", axis=0, tiled=True),
        lax.all_gather(first_shift, "fsdp", axis=0, tiled=True),
        lax.all_gather(qkv_weight, "fsdp", axis=0, tiled=True),
        lax.all_gather(query_bias, "fsdp", axis=0, tiled=True),
        lax.all_gather(value_bias, "fsdp", axis=0, tiled=True),
        lax.all_gather(proj_weight, "fsdp", axis=0, tiled=True),
        lax.all_gather(proj_bias, "fsdp", axis=0, tiled=True),
        lax.all_gather(second_gain, "fsdp", axis=0, tiled=True),
        lax.all_gather(second_shift, "fsdp", axis=0, tiled=True),
        lax.all_gather(hidden_weight, "fsdp", axis=0, tiled=True),
        lax.all_gather(hidden_bias, "fsdp", axis=0, tiled=True),
        lax.all_gather(output_weight, "fsdp", axis=0, tiled=True),
        lax.all_gather(output_bias, "fsdp", axis=0, tiled=True),
    )
    rows = inputs.reshape(row_count, width).astype(jnp.float32)
    normed, unit_one, scale_one = normalize(
        rows, gain_one.astype(jnp.float32), shift_one.astype(jnp.float32)
    )
    normed_low = normed.astype(jnp.bfloat16)
    projected = jnp.dot(normed_low, full_qkv, preferred_element_type=jnp.float32)
    head_shape = (images, local_len, HEADS, HEAD_DIM)
    query = (
        (projected[:, :width] + bias_query.astype(jnp.float32))
        .astype(jnp.bfloat16)
        .reshape(head_shape)
    )
    keys = projected[:, width : 2 * width].astype(jnp.bfloat16).reshape(head_shape)
    values = (
        (projected[:, 2 * width :] + bias_value.astype(jnp.float32))
        .astype(jnp.bfloat16)
        .reshape(head_shape)
    )
    all_keys, all_values = (
        lax.all_gather(keys, "seq", axis=1, tiled=True),
        lax.all_gather(values, "seq", axis=1, tiled=True),
    )

    def attend(items):
        query_one, key_one, value_one = items
        scores = (
            jnp.einsum("qhd,khd->hqk", query_one, key_one, preferred_element_type=jnp.float32)
            * factor
        )
        row_max = jnp.max(scores, -1, keepdims=True)
        exponent = jnp.exp(scores - row_max)
        row_total = jnp.sum(exponent, -1, keepdims=True)
        weights = (exponent / row_total).astype(jnp.bfloat16)
        mixed_one = jnp.einsum(
            "hqk,khd->qhd", weights, value_one, preferred_element_type=jnp.float32
        )
        return (mixed_one, (row_max + jnp.log(row_total))[..., 0])

    mixed, log_total = lax.map(attend, (query, all_keys, all_values))
    mixed_low = mixed.reshape(row_count, width).astype(jnp.bfloat16)
    attended = jnp.dot(mixed_low, full_proj, preferred_element_type=jnp.float32) + bias_proj.astype(
        jnp.float32
    )
    middle = rows + attended
    normed_two, unit_two, scale_two = normalize(
        middle, gain_two.astype(jnp.float32), shift_two.astype(jnp.float32)
    )
    normed_two_low = normed_two.astype(jnp.bfloat16)
    hidden_pre = jnp.dot(
        normed_two_low, full_hidden, preferred_element_type=jnp.float32
    ) + bias_hidden.astype(jnp.float32)
    activated = gelu_exact(hidden_pre).astype(jnp.bfloat16)
    branch = jnp.dot(
        activated, full_output, preferred_element_type=jnp.float32
    ) + bias_output.astype(jnp.float32)
    block_out = (middle + branch).astype(jnp.bfloat16).reshape(inputs.shape)
    upstream = cotangent.reshape(row_count, width).astype(jnp.float32)
    grad_branch = upstream.astype(jnp.bfloat16)
    grad_output_w = jnp.einsum(
        "rf,rd->fd", activated, grad_branch, preferred_element_type=jnp.float32
    )
    grad_output_b = column_sum(grad_branch)
    grad_act = jnp.einsum("rd,fd->rf", grad_branch, full_output, preferred_element_type=jnp.float32)
    unused_value, pull_gelu = jax.vjp(gelu_exact, hidden_pre)
    grad_hidden = pull_gelu(grad_act)[0].astype(jnp.bfloat16)
    grad_hidden_w = jnp.einsum(
        "rd,rf->df", normed_two_low, grad_hidden, preferred_element_type=jnp.float32
    )
    grad_hidden_b = column_sum(grad_hidden)
    grad_normed_two = jnp.einsum(
        "rf,df->rd", grad_hidden, full_hidden, preferred_element_type=jnp.float32
    )
    grad_gain_two = jnp.sum(grad_normed_two * unit_two, 0)
    grad_shift_two = jnp.sum(grad_normed_two, 0)
    grad_middle = upstream + norm_back(
        grad_normed_two, unit_two, scale_two, gain_two.astype(jnp.float32)
    )
    grad_attended = grad_middle.astype(jnp.bfloat16)
    grad_proj_w = jnp.einsum(
        "re,rd->ed", mixed_low, grad_attended, preferred_element_type=jnp.float32
    )
    grad_proj_b = column_sum(grad_attended)
    grad_mixed = jnp.einsum(
        "rd,ed->re", grad_attended, full_proj, preferred_element_type=jnp.float32
    )
    grad_mixed = grad_mixed.astype(jnp.bfloat16).reshape(head_shape)

    def attend_back(items):
        query_one, key_one, value_one, grad_one, log_one = items
        scores = (
            jnp.einsum("qhd,khd->hqk", query_one, key_one, preferred_element_type=jnp.float32)
            * factor
        )
        probs = jnp.exp(scores - log_one[..., None])
        grad_value = jnp.einsum(
            "hqk,qhd->khd", probs.astype(jnp.bfloat16), grad_one, preferred_element_type=jnp.float32
        )
        grad_probs = jnp.einsum(
            "qhd,khd->hqk", grad_one, value_one, preferred_element_type=jnp.float32
        )
        inner = jnp.sum(probs * grad_probs, -1, keepdims=True)
        grad_scores = (probs * (grad_probs - inner)).astype(jnp.bfloat16)
        grad_query = (
            jnp.einsum("hqk,khd->qhd", grad_scores, key_one, preferred_element_type=jnp.float32)
            * factor
        )
        grad_key = (
            jnp.einsum("hqk,qhd->khd", grad_scores, query_one, preferred_element_type=jnp.float32)
            * factor
        )
        return (grad_query, grad_key, grad_value)

    grad_query, grad_keys, grad_values = lax.map(
        attend_back, (query, all_keys, all_values, grad_mixed, log_total)
    )
    grad_keys, grad_values = (
        lax.psum_scatter(
            grad_keys.astype(jnp.bfloat16), "seq", scatter_dimension=1, tiled=True
        ).astype(jnp.float32),
        lax.psum_scatter(
            grad_values.astype(jnp.bfloat16), "seq", scatter_dimension=1, tiled=True
        ).astype(jnp.float32),
    )
    grad_qkv = jnp.concatenate(
        [
            grad_query.reshape(row_count, width),
            grad_keys.reshape(row_count, width),
            grad_values.reshape(row_count, width),
        ],
        -1,
    ).astype(jnp.bfloat16)
    grad_qkv_w = jnp.einsum("rd,rc->dc", normed_low, grad_qkv, preferred_element_type=jnp.float32)
    grad_query_b = column_sum(grad_qkv[:, :width])
    grad_value_b = column_sum(grad_qkv[:, 2 * width :])
    grad_normed = jnp.einsum("rc,dc->rd", grad_qkv, full_qkv, preferred_element_type=jnp.float32)
    grad_gain_one = jnp.sum(grad_normed * unit_one, 0)
    grad_shift_one = jnp.sum(grad_normed, 0)
    grad_rows = grad_middle + norm_back(
        grad_normed, unit_one, scale_one, gain_one.astype(jnp.float32)
    )
    input_grad = grad_rows.astype(jnp.bfloat16).reshape(inputs.shape)
    parts = (
        lax.psum_scatter(
            grad_gain_one.astype(jnp.bfloat16), "fsdp", scatter_dimension=0, tiled=True
        ).astype(jnp.float32),
        lax.psum_scatter(
            grad_shift_one.astype(jnp.bfloat16), "fsdp", scatter_dimension=0, tiled=True
        ).astype(jnp.float32),
        lax.psum_scatter(
            grad_qkv_w.astype(jnp.bfloat16), "fsdp", scatter_dimension=0, tiled=True
        ).astype(jnp.float32),
        lax.psum_scatter(
            grad_query_b.astype(jnp.bfloat16), "fsdp", scatter_dimension=0, tiled=True
        ).astype(jnp.float32),
        lax.psum_scatter(
            grad_value_b.astype(jnp.bfloat16), "fsdp", scatter_dimension=0, tiled=True
        ).astype(jnp.float32),
        lax.psum_scatter(
            grad_proj_w.astype(jnp.bfloat16), "fsdp", scatter_dimension=0, tiled=True
        ).astype(jnp.float32),
        lax.psum_scatter(
            grad_proj_b.astype(jnp.bfloat16), "fsdp", scatter_dimension=0, tiled=True
        ).astype(jnp.float32),
        lax.psum_scatter(
            grad_gain_two.astype(jnp.bfloat16), "fsdp", scatter_dimension=0, tiled=True
        ).astype(jnp.float32),
        lax.psum_scatter(
            grad_shift_two.astype(jnp.bfloat16), "fsdp", scatter_dimension=0, tiled=True
        ).astype(jnp.float32),
        lax.psum_scatter(
            grad_hidden_w.astype(jnp.bfloat16), "fsdp", scatter_dimension=0, tiled=True
        ).astype(jnp.float32),
        lax.psum_scatter(
            grad_hidden_b.astype(jnp.bfloat16), "fsdp", scatter_dimension=0, tiled=True
        ).astype(jnp.float32),
        lax.psum_scatter(
            grad_output_w.astype(jnp.bfloat16), "fsdp", scatter_dimension=0, tiled=True
        ).astype(jnp.float32),
        lax.psum_scatter(
            grad_output_b.astype(jnp.bfloat16), "fsdp", scatter_dimension=0, tiled=True
        ).astype(jnp.float32),
    )
    shares = (
        lax.psum(parts[0].astype(jnp.bfloat16), "seq").astype(jnp.float32),
        lax.psum(parts[1].astype(jnp.bfloat16), "seq").astype(jnp.float32),
        lax.psum(parts[2].astype(jnp.bfloat16), "seq").astype(jnp.float32),
        lax.psum(parts[3].astype(jnp.bfloat16), "seq").astype(jnp.float32),
        lax.psum(parts[4].astype(jnp.bfloat16), "seq").astype(jnp.float32),
        lax.psum(parts[5].astype(jnp.bfloat16), "seq").astype(jnp.float32),
        lax.psum(parts[6].astype(jnp.bfloat16), "seq").astype(jnp.float32),
        lax.psum(parts[7].astype(jnp.bfloat16), "seq").astype(jnp.float32),
        lax.psum(parts[8].astype(jnp.bfloat16), "seq").astype(jnp.float32),
        lax.psum(parts[9].astype(jnp.bfloat16), "seq").astype(jnp.float32),
        lax.psum(parts[10].astype(jnp.bfloat16), "seq").astype(jnp.float32),
        lax.psum(parts[11].astype(jnp.bfloat16), "seq").astype(jnp.float32),
        lax.psum(parts[12].astype(jnp.bfloat16), "seq").astype(jnp.float32),
    )
    return (
        block_out,
        input_grad,
        shares[0],
        shares[1],
        shares[2],
        shares[3],
        shares[4],
        shares[5],
        shares[6],
        shares[7],
        shares[8],
        shares[9],
        shares[10],
        shares[11],
        shares[12],
    )


F32 = jnp.float32
BF16 = jnp.bfloat16
VMEM_BYTES = 60 * 1024 * 1024
NT = (((1,), (1,)), ((), ()))
LATE = pl.CostEstimate(flops=1000, bytes_accessed=1000, transcendentals=0)


def mul(left, right):
    return jnp.dot(left, right, preferred_element_type=F32)


def mul_nt(left, right):
    return lax.dot_general(left, right, NT, preferred_element_type=F32)


def params(count):
    return pltpu.CompilerParams(
        dimension_semantics=("arbitrary",) * count, vmem_limit_bytes=VMEM_BYTES
    )


def whole(shape):
    return pl.BlockSpec(shape, lambda *ids: (0,) * len(shape), pipeline_mode=pl.Buffered(1))


def shaped(shape, dtype):
    return jax.ShapeDtypeStruct(shape, dtype)


def qkv_part(weight_ref, part):
    width = weight_ref.shape[-1] // 3
    rows = width // weight_ref.shape[0]
    return weight_ref[:, :rows, part * width : (part + 1) * width].reshape(width, width)


def project_kernel(x_ref, weight_ref, gain_ref, shift_ref, bias_ref, qkv_ref, normed_ref):
    width = x_ref.shape[-1]
    normed, unused_unit, unused_scale = normalize(
        x_ref[0].astype(F32), gain_ref[...], shift_ref[...]
    )
    low = normed.astype(BF16)
    normed_ref[0] = low
    for part in range(3):
        value = mul(low, qkv_part(weight_ref, part)) + bias_ref[part : part + 1]
        if part == 0:
            value = value * HEAD_DIM ** (-0.5)
        qkv_ref[part, 0] = value.astype(BF16)


def project(units, weight, gain, shift, bias):
    count, size, width = units.shape
    return pl.pallas_call(
        project_kernel,
        grid=(count,),
        in_specs=[
            pl.BlockSpec((1, size, width), lambda u: (u, 0, 0)),
            whole(weight.shape),
            whole(gain.shape),
            whole(shift.shape),
            whole(bias.shape),
        ],
        out_specs=[
            pl.BlockSpec((3, 1, size, width), lambda u: (0, u, 0, 0)),
            pl.BlockSpec((1, size, width), lambda u: (u, 0, 0)),
        ],
        out_shape=[shaped((3, count, size, width), BF16), shaped((count, size, width), BF16)],
        compiler_params=params(1),
        cost_estimate=pl.CostEstimate(
            flops=2 * count * size * width * 3 * width,
            bytes_accessed=count * size * width * 10 + 6 * width * width,
            transcendentals=0,
        ),
        name="project",
    )(units, weight, gain, shift, bias)


def head_mask(size):
    return lax.broadcasted_iota(jnp.int32, (size, 2 * HEAD_DIM), 1) // HEAD_DIM


def mix_kernel(q_ref, ka_ref, va_ref, kb_ref, vb_ref, *rest):
    o_ref, lse_ref = rest[-2:]
    query = q_ref[0, 0]
    lanes = head_mask(query.shape[0])
    keys = (ka_ref[0, 0], kb_ref[0, 0])
    turned = (va_ref[0, 0].T, vb_ref[0, 0].T)
    outs = []
    for head in range(2):
        one = jnp.where(lanes == head, query, jnp.zeros_like(query))
        scores = [mul_nt(key, one) for key in keys]
        top = jnp.maximum(
            jnp.max(scores[0], 0, keepdims=True), jnp.max(scores[1], 0, keepdims=True)
        )
        grown = [jnp.exp(score - top) for score in scores]
        total = jnp.sum(grown[0], 0, keepdims=True) + jnp.sum(grown[1], 0, keepdims=True)
        span = slice(head * HEAD_DIM, (head + 1) * HEAD_DIM)
        mixed = mul(turned[0][span], grown[0].astype(BF16)) + mul(
            turned[1][span], grown[1].astype(BF16)
        )
        outs.append(mixed / total)
        lse_ref[0, 0, head : head + 1] = top + jnp.log(total)
    o_ref[0] = jnp.concatenate(outs, 0).T.astype(BF16)


def attend_specs(size, key_places):
    lanes = 2 * HEAD_DIM
    specs = []
    for source, part, unit in key_places:
        specs.append(
            pl.BlockSpec((1, 1, size, lanes), lambda h, u, part=part, unit=unit: (part, unit, 0, h))
        )
    return specs


def mix(qkv, first_unit, unit_count, key_places, earlier=None):
    size, width = qkv.shape[2:]
    lanes = 2 * HEAD_DIM
    pairs = width // lanes
    flops = 4 * unit_count * size * 2 * size * width
    return pl.pallas_call(
        mix_kernel,
        grid=(pairs, unit_count),
        in_specs=[pl.BlockSpec((1, 1, size, lanes), lambda h, u: (0, first_unit + u, 0, h))]
        + attend_specs(size, key_places)
        + [pl.BlockSpec(memory_space=pl.ANY)] * (earlier is not None),
        out_specs=[
            pl.BlockSpec((1, size, lanes), lambda h, u: (first_unit + u, 0, h)),
            pl.BlockSpec((1, 1, 8, size), lambda h, u: (u, h, 0, 0)),
        ],
        out_shape=[
            shaped((qkv.shape[1], size, width), BF16),
            shaped((unit_count, pairs, 8, size), F32),
        ],
        input_output_aliases={} if earlier is None else {5: 0},
        compiler_params=params(2),
        cost_estimate=pl.CostEstimate(
            flops=4 * flops,
            bytes_accessed=unit_count * size * width * 8,
            transcendentals=unit_count * size * 2 * size * width // HEAD_DIM,
        ),
        name="mix",
    )(qkv, *[place[0] for place in key_places], *([] if earlier is None else [earlier]))


def mix_back_kernel(
    unit_count,
    q_ref,
    ka_ref,
    va_ref,
    kb_ref,
    vb_ref,
    o_ref,
    do_ref,
    lse_ref,
    *rest,
):
    dq_ref, dkv_ref, dk_acc, dv_acc = rest[-4:]
    step = pl.program_id(1)
    query = q_ref[0, 0]
    grad = do_ref[0]
    size = query.shape[0]
    lanes = head_mask(size)
    keys = (ka_ref[0, 0], kb_ref[0, 0])
    values = (va_ref[0, 0], vb_ref[0, 0])
    turned = (keys[0].T, keys[1].T)
    product = grad.astype(F32) * o_ref[0].astype(F32)
    high = product.astype(BF16)
    rest = (product - high.astype(F32)).astype(BF16)
    chosen = (
        lax.broadcasted_iota(jnp.int32, (8, 2 * HEAD_DIM), 1) // HEAD_DIM
        == lax.broadcasted_iota(jnp.int32, (8, 2 * HEAD_DIM), 0)
    ).astype(BF16)
    inner = mul_nt(chosen, high) + mul_nt(chosen, rest)
    dks, dvs, dqs = [None, None], [None, None], []
    for head in range(2):
        mine = lanes == head
        one_query = jnp.where(mine, query, jnp.zeros_like(query))
        one_grad = jnp.where(mine, grad, jnp.zeros_like(grad))
        span = slice(head * HEAD_DIM, (head + 1) * HEAD_DIM)
        log_row = lse_ref[0, 0, head : head + 1]
        inner_row = inner[head : head + 1]
        dq = None
        for side in range(2):
            probs = jnp.exp(mul_nt(keys[side], one_query) - log_row)
            dv = mul(probs.astype(BF16), one_grad)
            change = mul_nt(values[side], one_grad)
            scored = (probs * (change - inner_row)).astype(BF16)
            dk = mul(scored, one_query)
            part = mul(turned[side][span], scored)
            dq = part if dq is None else dq + part
            dks[side] = dk if head == 0 else dks[side] + dk
            dvs[side] = dv if head == 0 else dvs[side] + dv
        dqs.append(dq)
    dq_ref[0] = (jnp.concatenate(dqs, 0).T * HEAD_DIM ** (-0.5)).astype(BF16)
    if unit_count == 1:
        for side in range(2):
            dkv_ref[0, side] = dks[side].astype(BF16)
            dkv_ref[1, side] = dvs[side].astype(BF16)
        return

    @pl.when(step == 0)
    def first():
        for side in range(2):
            dk_acc[side] = dks[side]
            dv_acc[side] = dvs[side]

    @pl.when(jnp.logical_and(step > 0, step < unit_count - 1))
    def between():
        for side in range(2):
            dk_acc[side] += dks[side]
            dv_acc[side] += dvs[side]

    @pl.when(step == unit_count - 1)
    def last():
        for side in range(2):
            dkv_ref[0, side] = (dk_acc[side] + dks[side]).astype(BF16)
            dkv_ref[1, side] = (dv_acc[side] + dvs[side]).astype(BF16)


def mix_back(qkv, first_unit, unit_count, key_places, mixed, grad_mixed, lse, earlier=None):
    size, width = qkv.shape[2:]
    lanes = 2 * HEAD_DIM
    pairs = width // lanes
    units = qkv.shape[1]
    return pl.pallas_call(
        functools.partial(mix_back_kernel, unit_count),
        grid=(pairs, unit_count),
        in_specs=[pl.BlockSpec((1, 1, size, lanes), lambda h, u: (0, first_unit + u, 0, h))]
        + attend_specs(size, key_places)
        + [
            pl.BlockSpec((1, size, lanes), lambda h, u: (first_unit + u, 0, h)),
            pl.BlockSpec((1, size, lanes), lambda h, u: (first_unit + u, 0, h)),
            pl.BlockSpec((1, 1, 8, size), lambda h, u: (u, h, 0, 0)),
        ]
        + [pl.BlockSpec(memory_space=pl.ANY)] * (earlier is not None),
        out_specs=[
            pl.BlockSpec((1, size, lanes), lambda h, u: (first_unit + u, 0, h)),
            pl.BlockSpec((2, 2, size, lanes), lambda h, u: (0, 0, 0, h)),
        ],
        out_shape=[
            shaped((units, size, width), BF16),
            shaped((2, 2 if earlier is None else units, size, width), BF16),
        ],
        input_output_aliases={} if earlier is None else {8: 0},
        scratch_shapes=[pltpu.VMEM((2, size, lanes), F32)] * 2,
        compiler_params=params(2),
        cost_estimate=LATE,
        name="mix_back",
    )(
        qkv,
        *[place[0] for place in key_places],
        mixed,
        grad_mixed,
        lse,
        *([] if earlier is None else [earlier]),
    )


def gelu_pair(value):
    size = jnp.abs(value) * 0.5**0.5
    turn = 1.0 / (1.0 + 0.3275911 * size)
    bell = jnp.exp(-size * size)
    series = turn * (
        0.254829592
        + turn * (-0.284496736 + turn * (1.421413741 + turn * (-1.453152027 + turn * 1.061405429)))
    )
    tail = 0.5 * series * bell
    share = jnp.where(value >= 0, 1.0 - tail, tail)
    return value * share, share + value * (bell * 0.3989422804014327)


def column(values):
    return jnp.sum(values, 0, keepdims=True)


def feed_kernel(
    x_ref,
    o_ref,
    cot_ref,
    weights_ref,
    gain_ref,
    shift_ref,
    proj_bias_ref,
    hidden_bias_ref,
    output_bias_ref,
    out_ref,
    dx_ref,
    do_ref,
    normed_ref,
    act_ref,
    dh_ref,
    dp_ref,
    sums_ref,
    hidden_sum_ref,
):
    step = pl.program_id(0)
    width = x_ref.shape[-1]
    shards, shard_rows = weights_ref.shape[:2]
    rows = width // shards
    parts = hidden_bias_ref.shape[-1] // width
    per_part = shards // parts

    @pl.when(step == 0)
    def clear():
        sums_ref[...] = jnp.zeros_like(sums_ref)
        hidden_sum_ref[...] = jnp.zeros_like(hidden_sum_ref)

    proj = weights_ref[:, 2 * parts * rows :, :].reshape(width, width)
    middle = x_ref[0].astype(F32) + (mul(o_ref[0], proj) + proj_bias_ref[...])
    gain = gain_ref[...]
    normed, unit, scale = normalize(middle, gain, shift_ref[...])
    low = normed.astype(BF16)
    normed_ref[0] = low
    upstream = cot_ref[0]
    branch = middle + output_bias_ref[...]
    grad_normed = None
    for part in range(parts):
        first = weights_ref[:, part * rows : (part + 1) * rows, :].reshape(width, width)
        second = weights_ref[
            part * per_part : (part + 1) * per_part, parts * rows : 2 * parts * rows, :
        ].reshape(width, width)
        span = slice(part * width, (part + 1) * width)
        hidden = mul(low, first) + hidden_bias_ref[:, span]
        active, slope = gelu_pair(hidden)
        active = active.astype(BF16)
        act_ref[0, :, span] = active
        branch = branch + mul(active, second)
        grad_hidden = mul_nt(upstream, second) * slope
        low_grad = grad_hidden.astype(BF16)
        dh_ref[0, :, span] = low_grad
        hidden_sum_ref[0:1, span] += column(low_grad.astype(F32))
        back = mul_nt(low_grad, first)
        grad_normed = back if grad_normed is None else grad_normed + back
    out_ref[0] = branch.astype(BF16)
    wide = upstream.astype(F32)
    grad_middle = wide + norm_back(grad_normed, unit, scale, gain)
    dx_ref[0] = grad_middle
    low_middle = grad_middle.astype(BF16)
    dp_ref[0] = low_middle
    do_ref[0] = mul_nt(low_middle, proj).astype(BF16)
    sums_ref[0:1] += column(wide)
    sums_ref[1:2] += column(grad_normed * unit)
    sums_ref[2:3] += column(grad_normed)
    sums_ref[3:4] += column(low_middle.astype(F32))


def feed(units, mixed, cotangent, weights, gain, shift, proj_bias, hidden_bias, output_bias):
    count, size, width = units.shape
    inner = hidden_bias.shape[-1]

    def rows(columns):
        return pl.BlockSpec((1, size, columns), lambda u: (u, 0, 0))

    return pl.pallas_call(
        feed_kernel,
        grid=(count,),
        in_specs=[
            rows(width),
            rows(width),
            rows(width),
            whole(weights.shape),
            whole(gain.shape),
            whole(shift.shape),
            whole(proj_bias.shape),
            whole(hidden_bias.shape),
            whole(output_bias.shape),
        ],
        out_specs=[
            rows(width),
            rows(width),
            rows(width),
            rows(width),
            rows(inner),
            rows(inner),
            rows(width),
            pl.BlockSpec((8, width), lambda u: (0, 0)),
            pl.BlockSpec((8, inner), lambda u: (0, 0)),
        ],
        out_shape=[
            shaped((count, size, width), BF16),
            shaped((count, size, width), F32),
            shaped((count, size, width), BF16),
            shaped((count, size, width), BF16),
            shaped((count, size, inner), BF16),
            shaped((count, size, inner), BF16),
            shaped((count, size, width), BF16),
            shaped((8, width), F32),
            shaped((8, inner), F32),
        ],
        compiler_params=params(1),
        cost_estimate=pl.CostEstimate(
            flops=2 * count * size * width * (4 * inner + 2 * width),
            bytes_accessed=count * size * (width * 20 + inner * 4),
            transcendentals=2 * count * size * inner,
        ),
        name="feed",
    )(units, mixed, cotangent, weights, gain, shift, proj_bias, hidden_bias, output_bias)


def weight_kernel(parts, shards, normed_ref, dh_ref, act_ref, dz_ref, o_ref, dp_ref, out_ref, left, right):
    step = pl.program_id(0)
    width = normed_ref.shape[-1]
    rows = width // shards
    per_part = shards // parts

    @pl.when(step == 0)
    def turn():
        left[...] = normed_ref[...].T
        right[...] = dz_ref[...].T

    for part in range(parts):

        @pl.when(step == part)
        def first():
            grad = mul(left[...], dh_ref[...])
            out_ref[:, part * rows : (part + 1) * rows, :] = grad.astype(BF16).reshape(
                shards, rows, width
            )

        @pl.when(step == parts + part)
        def second():
            grad = mul(right[...], act_ref[...]).T
            out_ref[
                part * per_part : (part + 1) * per_part, parts * rows : 2 * parts * rows, :
            ] = grad.astype(BF16).reshape(per_part, parts * rows, width)

    @pl.when(step == 2 * parts)
    def third():
        grad = mul(o_ref[...].T, dp_ref[...])
        out_ref[:, 2 * parts * rows :, :] = grad.astype(BF16).reshape(shards, rows, width)


def weight_grads(normed, grad_hidden, active, grad_branch, mixed, grad_attended, shards):
    count, width = normed.shape
    inner = active.shape[-1]
    parts = inner // width
    shard_rows = (2 * parts + 1) * (width // shards)
    return pl.pallas_call(
        functools.partial(weight_kernel, parts, shards),
        grid=(2 * parts + 1,),
        in_specs=[
            whole(normed.shape),
            pl.BlockSpec((count, width), lambda s: (0, jnp.minimum(s, parts - 1))),
            pl.BlockSpec((count, width), lambda s: (0, jnp.clip(s - parts, 0, parts - 1))),
            whole(grad_branch.shape),
            whole(mixed.shape),
            whole(grad_attended.shape),
        ],
        out_specs=whole((shards, shard_rows, width)),
        out_shape=shaped((shards, shard_rows, width), BF16),
        scratch_shapes=[pltpu.VMEM((width, count), BF16)] * 2,
        compiler_params=params(1),
        cost_estimate=pl.CostEstimate(
            flops=2 * count * width * (2 * inner + width),
            bytes_accessed=count * (8 * width + 4 * inner),
            transcendentals=0,
        ),
        name="weight_grads",
    )(normed, grad_hidden, active, grad_branch, mixed, grad_attended)


def halving_orders(shards):
    reaches = [1 << bit for bit in range(shards.bit_length() - 1)]
    return reaches, reaches[:1] + reaches[2:] + reaches[1:2]


def slot_of(shard, order):
    slot = 0
    for reach in order:
        slot = 2 * slot + (shard // reach) % 2
    return slot


def qkv_weight_kernel(shards, normed_ref, dq_ref, dkv_ref, low_ref, high_ref, left):
    step = pl.program_id(0)
    width = normed_ref.shape[-1]
    rows = width // shards
    half = width // 2
    low_order, high_order = halving_orders(shards)

    def keep(ref, order, start, grad):
        for shard in range(shards):
            ref[slot_of(shard, order), :, start : start + grad.shape[1]] = grad[
                shard * rows : (shard + 1) * rows
            ]

    @pl.when(step == 0)
    def query_part():
        left[...] = normed_ref[...].T
        keep(low_ref, low_order, 0, mul(left[...], dq_ref[...]).astype(BF16))

    @pl.when(step == 1)
    def key_part():
        grad = mul(left[...], dkv_ref[0]).astype(BF16)
        keep(low_ref, low_order, width, grad[:, :half])
        keep(high_ref, high_order, 0, grad[:, half:])

    @pl.when(step == 2)
    def value_part():
        keep(high_ref, high_order, half, mul(left[...], dkv_ref[0]).astype(BF16))


def qkv_weight_grad(normed, dq, dkv, shards):
    count, width = normed.shape
    half = (shards, width // shards, 3 * width // 2)
    return pl.pallas_call(
        functools.partial(qkv_weight_kernel, shards),
        grid=(3,),
        in_specs=[
            whole(normed.shape),
            whole(dq.shape),
            pl.BlockSpec((1, count, width), lambda s: (jnp.maximum(s - 1, 0), 0, 0)),
        ],
        out_specs=[whole(half), whole(half)],
        out_shape=[shaped(half, BF16), shaped(half, BF16)],
        scratch_shapes=[pltpu.VMEM((width, count), BF16)],
        compiler_params=params(1),
        cost_estimate=LATE,
        name="qkv_weight_grad",
    )(normed, dq, dkv)


def input_kernel(x_ref, dx_ref, dq_ref, dkv_ref, weight_ref, gain_ref, shift_ref, out_ref, sums_ref):
    step = pl.program_id(0)
    width = x_ref.shape[-1]

    @pl.when(step == 0)
    def clear():
        sums_ref[...] = jnp.zeros_like(sums_ref)

    gain = gain_ref[...]
    unused, unit, scale = normalize(x_ref[0].astype(F32), gain, shift_ref[...])
    grad = mul_nt(dq_ref[0], qkv_part(weight_ref, 0))
    grad = grad + mul_nt(dkv_ref[0, 0], qkv_part(weight_ref, 1))
    grad = grad + mul_nt(dkv_ref[1, 0], qkv_part(weight_ref, 2))
    out_ref[0] = (dx_ref[0] + norm_back(grad, unit, scale, gain)).astype(BF16)
    sums_ref[0:1] += column(grad * unit)
    sums_ref[1:2] += column(grad)
    sums_ref[2:3] += column(dq_ref[0].astype(F32))
    sums_ref[3:4] += column(dkv_ref[1, 0].astype(F32))


def input_grads(units, grad_middle, dq, dkv, weight, gain, shift):
    count, size, width = units.shape
    rows = pl.BlockSpec((1, size, width), lambda u: (u, 0, 0))
    return pl.pallas_call(
        input_kernel,
        grid=(count,),
        in_specs=[
            rows,
            rows,
            rows,
            pl.BlockSpec((2, 1, size, width), lambda u: (0, u, 0, 0)),
            whole(weight.shape),
            whole(gain.shape),
            whole(shift.shape),
        ],
        out_specs=[rows, pl.BlockSpec((8, width), lambda u: (0, 0))],
        out_shape=[shaped((count, size, width), BF16), shaped((8, width), F32)],
        compiler_params=params(1),
        cost_estimate=LATE,
        name="input_grads",
    )(units, grad_middle, dq, dkv, weight, gain, shift)


def tree_sum(value, axes):
    for axis, size in axes:
        reach = 1
        while reach < size:
            pairs = [(index, index ^ reach) for index in range(size)]
            value = value + lax.ppermute(value, axis, pairs)
            reach *= 2
    return value


def halving_sum(value, axis, size, place, order):
    for reach in order:
        pairs = [(index, index ^ reach) for index in range(size)]
        halves = value.reshape((2, value.shape[0] // 2) + value.shape[1:])
        bit = (place // reach) % 2
        got = lax.ppermute(lax.dynamic_index_in_dim(halves, 1 - bit, 0, False), axis, pairs)
        kept = lax.dynamic_index_in_dim(halves, bit, 0, False)
        value = (kept.astype(F32) + got.astype(F32)).astype(BF16)
    return value


def fast_body(fsdp_size, *args):
    (
        inputs,
        cotangent,
        first_gain,
        first_shift,
        qkv_weight,
        query_bias,
        value_bias,
        proj_weight,
        proj_bias,
        second_gain,
        second_shift,
        hidden_weight,
        hidden_bias,
        output_weight,
        output_bias,
    ) = args
    images, size, width = inputs.shape
    row_count = images * size
    side = lax.axis_index("seq")
    place = lax.axis_index("fsdp")
    swap_sides = [(0, 1), (1, 0)]
    swap_cores = [(index, index ^ 1) for index in range(fsdp_size)]
    swap_middle = []
    for index in range(0, fsdp_size, 2):
        swap_middle += [(fsdp_size + index, index + 1), (index + 1, fsdp_size + index)]
    stays = side == place % 2

    def middle_swap(value):
        return jnp.where(stays, value, lax.ppermute(value, ("seq", "fsdp"), swap_middle))

    def gather_units(values):
        got = lax.ppermute(
            lax.dynamic_index_in_dim(values, 2 * (1 - side), 0, False), "seq", swap_sides
        )
        kept = lax.dynamic_index_in_dim(values, 2 * side, 0, False)
        return jnp.stack([kept, got, middle_swap(values[1])])

    def return_units(values, after=None):
        got = lax.ppermute(values[1], "seq", swap_sides)
        centre = lax.ppermute(values[2], ("seq", "fsdp"), swap_middle)
        if after is not None:
            got, centre, after = lax.optimization_barrier((got, centre, after))
        centre = jnp.where(stays, values[2], centre)
        first = jnp.where(side == 0, values[0], got)
        last = jnp.where(side == 0, got, values[0])
        value = jnp.stack([first, centre, last])
        return value if after is None else (value, after)

    def both(value):
        return value.astype(F32) + lax.ppermute(value, "seq", swap_sides).astype(F32)

    parts = hidden_weight.shape[1] // width
    rows = hidden_weight.shape[0]
    small = [
        first_gain,
        first_shift,
        query_bias,
        value_bias,
        proj_bias,
        second_gain,
        second_shift,
        output_bias,
        hidden_bias,
    ]
    sizes = [value.shape[0] for value in small]
    starts = [sum(sizes[:index]) for index in range(len(sizes))]
    lines = [jnp.pad(value[None], ((0, 0), (0, 3 * width - value.shape[0]))) for value in small]
    lines.append(jnp.zeros((16 - len(small), 3 * width), BF16))
    full_head = lax.all_gather(jnp.concatenate([qkv_weight] + lines, 0), "fsdp", axis=0)
    units = gather_units(inputs)
    hidden_weight, output_weight, proj_weight, units = lax.optimization_barrier(
        (hidden_weight, output_weight, proj_weight, units)
    )
    pack = jnp.concatenate(
        [hidden_weight[:, part * width : (part + 1) * width] for part in range(parts)]
        + [output_weight, proj_weight],
        0,
    )
    full_pack = lax.all_gather(pack, "fsdp", axis=0)
    all_small = full_head[:, rows:].astype(F32)
    (
        gain_one,
        shift_one,
        bias_query,
        bias_value,
        bias_proj,
        gain_two,
        shift_two,
        bias_output,
        bias_hidden,
    ) = [
        all_small[:, index, :count].reshape(1, fsdp_size * count)
        for index, count in enumerate(sizes)
    ]

    bias_qkv = jnp.concatenate([bias_query, jnp.zeros_like(bias_query), bias_value], 0)
    qkv, normed = project(units, full_head, gain_one, shift_one, bias_qkv)
    to_other, cotangent = lax.optimization_barrier((qkv[1:, 2], cotangent))
    other = lax.ppermute(to_other, "fsdp", swap_cores)[:, None]
    grads_up = gather_units(cotangent)
    places_pair = [(qkv, 1, 0), (qkv, 2, 0), (qkv, 1, 1), (qkv, 2, 1)]
    places_one = [(qkv, 1, 2), (qkv, 2, 2), (other, 0, 0), (other, 1, 0)]
    mixed_pair, lse_pair = mix(qkv, 0, 2, places_pair)
    mixed, lse_one = mix(qkv, 2, 1, places_one, mixed_pair)
    (
        out,
        grad_middle,
        grad_mixed,
        normed_two,
        active,
        grad_hidden,
        grad_attended,
        sums_two,
        sum_hidden,
    ) = feed(
        units,
        mixed,
        grads_up,
        full_pack,
        gain_two,
        shift_two,
        bias_proj,
        bias_hidden,
        bias_output,
    )
    block_out = return_units(out)

    def flat(value):
        return value.reshape(row_count, value.shape[-1])

    grad_pack = weight_grads(
        flat(normed_two),
        flat(grad_hidden),
        flat(active),
        flat(grads_up),
        flat(mixed),
        flat(grad_attended),
        fsdp_size,
    )
    grad_mixed, grad_pack = lax.optimization_barrier((grad_mixed, grad_pack))
    shard_pack = lax.psum_scatter(grad_pack, "fsdp", scatter_dimension=0, tiled=False)
    dq_one, dkv_one = mix_back(qkv, 2, 1, places_one, mixed, grad_mixed, lse_one)
    dkv_got = lax.ppermute(dkv_one[:, 1], "fsdp", swap_cores)
    dq, dkv = mix_back(qkv, 0, 2, places_pair, mixed, grad_mixed, lse_pair, dq_one)
    dkv = dkv.at[:, 2].set((dkv_one[:, 0].astype(F32) + dkv_got.astype(F32)).astype(BF16))
    sides = qkv_weight_grad(flat(normed), flat(dq), dkv.reshape(2, row_count, width), fsdp_size)
    orders = halving_orders(fsdp_size)
    sides = [
        halving_sum(value, "fsdp", fsdp_size, place, order[:1])
        for value, order in zip(sides, orders)
    ]
    sides, shard_pack, dq, dkv = lax.optimization_barrier((sides, shard_pack, dq, dkv))
    shard_pack = both(shard_pack)
    sides = [
        halving_sum(value, "fsdp", fsdp_size, place, order[1:2])
        for value, order in zip(sides, orders)
    ]
    grad_units, sums_one = input_grads(units, grad_middle, dq, dkv, full_head, gain_one, shift_one)
    sides, grad_units, sums_one = lax.optimization_barrier((sides, grad_units, sums_one))
    shard_sides = [
        halving_sum(value, "fsdp", fsdp_size, place, order[2:])[0]
        for value, order in zip(sides, orders)
    ]
    input_grad, shard_sides = return_units(grad_units, shard_sides)

    small_grads = [
        sums_one[0],
        sums_one[1],
        sums_one[2],
        sums_one[3],
        sums_two[3],
        sums_two[1],
        sums_two[2],
        sums_two[0],
        sum_hidden[0],
    ]
    packed = jnp.concatenate([value.reshape(fsdp_size, -1) for value in small_grads], 1)
    packed = tree_sum(packed, [("seq", 2), ("fsdp", fsdp_size)])
    mine = lax.dynamic_index_in_dim(packed, place, 0, False)
    (
        grad_gain_one,
        grad_shift_one,
        grad_query_b,
        grad_value_b,
        grad_proj_b,
        grad_gain_two,
        grad_shift_two,
        grad_output_b,
        grad_hidden_b,
    ) = [mine[start : start + count] for start, count in zip(starts, sizes)]

    grad_hidden_w = jnp.concatenate(
        [shard_pack[part * rows : (part + 1) * rows] for part in range(parts)], 1
    )
    grad_output_w = shard_pack[parts * rows : 2 * parts * rows]
    grad_proj_w = shard_pack[2 * parts * rows :]
    grad_qkv_w = jnp.concatenate([both(value) for value in shard_sides], 1)
    return (
        block_out,
        input_grad,
        grad_gain_one,
        grad_shift_one,
        grad_qkv_w,
        grad_query_b,
        grad_value_b,
        grad_proj_w,
        grad_proj_b,
        grad_gain_two,
        grad_shift_two,
        grad_hidden_w,
        grad_hidden_b,
        grad_output_w,
        grad_output_b,
    )


def pick_body(seq_size, fsdp_size):
    def body(*args):
        images, size, width = args[0].shape
        inner = args[11].shape[1]
        fits = (
            seq_size == 2
            and images == 3
            and fsdp_size > 1
            and fsdp_size & (fsdp_size - 1) == 0
            and size % 8 == 0
            and width % 128 == 0
            and (width // fsdp_size) % 16 == 0
            and inner % width == 0
            and fsdp_size % (inner // width) == 0
        )
        if fits:
            return fast_body(fsdp_size, *args)
        return general_body(*args)

    return body


def solution(mesh):
    shape = mesh.shape
    body = pick_body(shape["seq"], shape["fsdp"])
    return jax.shard_map(
        body,
        mesh=mesh,
        in_specs=(
            P("fsdp", "seq", None),
            P("fsdp", "seq", None),
            P("fsdp"),
            P("fsdp"),
            P("fsdp", None),
            P("fsdp"),
            P("fsdp"),
            P("fsdp", None),
            P("fsdp"),
            P("fsdp"),
            P("fsdp"),
            P("fsdp", None),
            P("fsdp"),
            P("fsdp", None),
            P("fsdp"),
        ),
        out_specs=(
            P("fsdp", "seq", None),
            P("fsdp", "seq", None),
            P("fsdp"),
            P("fsdp"),
            P("fsdp", None),
            P("fsdp"),
            P("fsdp"),
            P("fsdp", None),
            P("fsdp"),
            P("fsdp"),
            P("fsdp"),
            P("fsdp", None),
            P("fsdp"),
            P("fsdp", None),
            P("fsdp"),
        ),
        check_vma=False,
    )
```

profile of v0, /device:TPU:0, one launch (start us, length us, event | category | flops | bytes accessed | tf_op | source)
XLA Modules:
  0.0 527.3 jit_solution(4610845302150304230)
XLA Ops:
  13.2 3.0 concatenate.20
  16.3 3.0 constant_dynamic-slice_fusion.5
  19.2 1.6 collective-permute-start.1
  20.8 3.3 collective-permute-start
  25.5 32.3 %collective-permute-done = bf16[648,768]{1,0:T(8,128)(2,1)S(1)} collective-permute-done((bf16[648,768]{1,0:T(8,128)(2,1)S(1)}, bf16[648,768]{1,0:T(8,128)(2,1)S(1)}, u32[]{:S(2)}, u32[]{:S(2)}) %collective-permute-start) | collective-permute-done | bytes 995360 | tf_op jit(solution)/shard_map/ppermute | solution.py:925
  57.8 1.9 pad_maximum_fusion.x_ref
  60.9 11.6 %all-gather.5.cloned.1.call-done = bf16[1024,2304]{1,0:T(8,128)(2,1)} async-done(((bf16[64,2304]{1,0:T(8,128)(2,1)}), bf16[1024,2304]{1,0:T(8,128)(2,1)}) %all-gather.5.cloned.1.call-update) | async-done | bytes 4718608 | tf_op jit(solution)/shard_map/all_gather | solution.py:962
  72.5 1.5 slice_convert_fusion
  77.7 13.8 %project.1 = (bf16[3,3,648,768]{3,2,1,0:T(8,128)(2,1)}, bf16[3,648,768]{2,1,0:T(8,128)(2,1)}) custom-call(bf16[3,648,768]{2,1,0:T(8,128)(2,1)} %pad_maximum_fusion.x_ref, bf16[16,64,2304]{2,1,0:T(8,128)(2,1)} %bitcast.156, f32[1,768]{1,0:T(1,128)} %reshape_squeeze.54.gain_ref, f32[1,768]{1,0:T(1,128)} %reshape_squeeze.55.shift_ref, ...), custom_call_target="tpu_custom_call" | custom-call | flops 6879707136 | bytes 18468864 | tf_op jit(solution)/shard_map/project/pallas_call | solution.py:357
  91.5 3.2 slice_bitcast_fusion.2
  94.7 1.5 constant_dynamic-slice_fusion.4
  96.2 1.6 collective-permute-start.4
  97.8 2.2 collective-permute-start.3
  100.0 38.0 %mix.2 = (bf16[3,648,768]{2,1,0:T(8,128)(2,1)}, f32[2,6,8,648]{3,2,1,0:T(8,128)}) custom-call(bf16[3,3,648,768]{3,2,1,0:T(8,128)(2,1)} %get-tuple-element.72.q_ref.ka_ref.va_ref.kb_ref.vb_ref, bf16[3,3,648,768]{3,2,1,0:T(8,128)(2,1)} %get-tuple-element.72.q_ref.ka_ref.va_ref.kb_ref.vb_ref, ...), custom_call_target="tpu_custom_call" | custom-call | flops 20639121408 | bytes 7962624 | tf_op jit(solution)/shard_map/mix/pallas_call | solution.py:425
  143.7 3.1 pad_maximum_fusion.1.cot_ref
  148.2 19.9 %mix.3 = (bf16[3,648,768]{2,1,0:T(8,128)(2,1)}, f32[1,6,8,648]{3,2,1,0:T(8,128)}) custom-call(bf16[3,3,648,768]{3,2,1,0:T(8,128)(2,1)} %get-tuple-element.72.q_ref.ka_ref.va_ref.kb_ref.vb_ref, bf16[3,3,648,768]{3,2,1,0:T(8,128)(2,1)} %get-tuple-element.72.q_ref.ka_ref.va_ref.kb_ref.vb_ref, ...), custom_call_target="tpu_custom_call", output_to_operand_aliasing={{0}: (5, {})} | custom-call | flops 10319560704 | bytes 3981312 | tf_op jit(solution)/shard_map/mix/pallas_call | solution.py:425
  168.0 83.8 %feed.1 = (bf16[3,648,768]{2,1,0:T(8,128)(2,1)}, f32[3,648,768]{2,1,0:T(8,128)}, bf16[3,648,768]{2,1,0:T(8,128)(2,1)}, bf16[3,648,768]{2,1,0:T(8,128)(2,1)}, bf1...) custom-call(bf16[3,648,768]{2,1,0:T(8,128)(2,1)} %pad_maximum_fusion, ...), custom_call_target="tpu_custom_call" | custom-call | flops 41278242816 | bytes 53747712 | tf_op jit(solution)/shard_map/feed/pallas_call | solution.py:659
  251.8 34.9 %weight_grads.1 = bf16[16,432,768]{2,1,0:T(8,128)(2,1)} custom-call(bf16[1944,768]{1,0:T(8,128)(2,1)} %bitcast.187, bf16[1944,3072]{1,0:T(8,128)(2,1)} %bitcast.186, bf16[1944,3072]{1,0:T(8,128)(2,1)} %bitcast.185, bf16[1944,768]{1,0:T(8,128)(2,1)} %bitcast.163, bf16[1944,768]{1,0:T(8,128)(2,1)} %bitcast.150, bf16[1944,768]{1,0:T(8,128)(2,1)} %bitcast.188), custom_call_target="tpu_custom_call" | custom-call | flops 20639121408 | bytes 35831808 | tf_op jit(solution)/shard_map/weight_grads/pallas_call | solution.py:743
  286.7 33.9 %mix_back.2 = (bf16[3,648,768]{2,1,0:T(8,128)(2,1)}, bf16[2,2,648,768]{3,2,1,0:T(8,128)(2,1)}) custom-call(bf16[3,3,648,768]{3,2,1,0:T(8,128)(2,1)} %get-tuple-element.72.q_ref.ka_ref.va_ref.kb_ref.vb_ref, bf16[3,3,648,768]{3,2,1,0:T(8,128)(2,1)} %get-tuple-element.72.q_ref.ka_ref.va_ref.kb_ref.vb_ref, ...), custom_call_target="tpu_custom_call" | custom-call | flops 1000 | bytes 1000 | tf_op jit(solution)/shard_map/mix_back/pallas_call | solution.py:530
  320.6 3.0 slice_bitcast_fusion
  324.5 67.1 %mix_back.3 = (bf16[3,648,768]{2,1,0:T(8,128)(2,1)}, bf16[2,3,648,768]{3,2,1,0:T(8,128)(2,1)}) custom-call(bf16[3,3,648,768]{3,2,1,0:T(8,128)(2,1)} %get-tuple-element.72.q_ref.ka_ref.va_ref.kb_ref.vb_ref, bf16[3,3,648,768]{3,2,1,0:T(8,128)(2,1)} %get-tuple-element.72.q_ref.ka_ref.va_ref.kb_ref.vb_ref, ...), custom_call_target="tpu_custom_call", output_to_operand_aliasing={{0}: (8, {})} | custom-call | flops 1000 | bytes 1000 | tf_op jit(solution)/shard_map/mix_back/pallas_call | solution.py:530
  391.6 3.4 fusion.2.dkv_ref
  395.0 13.9 %qkv_weight_grad.1 = (bf16[16,48,1152]{2,1,0:T(8,128)(2,1)}, bf16[16,48,1152]{2,1,0:T(8,128)(2,1)}) custom-call(bf16[1944,768]{1,0:T(8,128)(2,1)} %bitcast.162, bf16[1944,768]{1,0:T(8,128)(2,1)} %bitcast.148, bf16[2,1944,768]{2,1,0:T(8,128)(2,1)} %bitcast.149), custom_call_target="tpu_custom_call" | custom-call | flops 1000 | bytes 1000 | tf_op jit(solution)/shard_map/qkv_weight_grad/pallas_call | solution.py:811
  408.9 2.2 dynamic-slice_bitcast_fusion.2
  411.0 2.2 dynamic-slice_bitcast_fusion.3
  415.1 2.7 fusion.3
  417.8 2.6 fusion.4
  421.5 1.6 collective-permute-start.11
  425.7 1.6 collective-permute-start.6
  428.7 16.3 %input_grads.1 = (bf16[3,648,768]{2,1,0:T(8,128)(2,1)}, f32[8,768]{1,0:T(8,128)}) custom-call(bf16[3,648,768]{2,1,0:T(8,128)(2,1)} %pad_maximum_fusion.x_ref, f32[3,648,768]{2,1,0:T(8,128)} %get-tuple-element.99.dx_ref, bf16[3,648,768]{2,1,0:T(8,128)(2,1)} %get-tuple-element.100.dq_ref, bf16[2,3,648,768]{3,2,1,0:T(8,128)(2,1)} %fusion.2.dkv_ref, ...), custom_call_target="tpu_custom_call" | custom-call | flops 1000 | bytes 1000 | tf_op jit(solution)/shard_map/input_grads/pallas_call | solution.py:851
  445.0 1.9 fusion.9
  449.4 1.9 collective-permute-start.18
  451.3 1.4 fusion.7
  452.8 7.1 %collective-permute-done.18 = f32[16,576]{1,0:T(8,128)S(1)} collective-permute-done((f32[16,576]{1,0:T(8,128)S(1)}, f32[16,576]{1,0:T(8,128)S(1)}, u32[]{:S(2)}, u32[]{:S(2)}) %collective-permute-start.18) | collective-permute-done | bytes 36896 | tf_op jit(solution)/shard_map/ppermute | solution.py:876
  461.2 1.9 pad_maximum_fusion.2
  463.2 1.9 collective-permute-start.25
  467.0 2.1 collective-permute-done.20
  469.6 1.6 collective-permute-start.14
  471.2 3.1 collective-permute-done.21
  474.4 2.0 collective-permute-start.22
  476.8 3.2 collective-permute-done.22
  482.9 1.5 collective-permute-start.17
  488.3 6.7 %collective-permute-done.15 = bf16[1,48,1152]{2,1,0:T(8,128)(2,1)S(1)} collective-permute-done((bf16[1,48,1152]{2,1,0:T(8,128)(2,1)S(1)}, bf16[1,48,1152]{2,1,0:T(8,128)(2,1)S(1)}, u32[]{:S(2)}, u32[]{:S(2)}) %collective-permute-start.15) | collective-permute-done | bytes 110624 | tf_op jit(solution)/shard_map/ppermute | solution.py:886
  495.1 6.8 %collective-permute-done.12 = bf16[648,768]{1,0:T(8,128)(2,1)S(1)} collective-permute-done((bf16[648,768]{1,0:T(8,128)(2,1)S(1)}, bf16[648,768]{1,0:T(8,128)(2,1)S(1)}, u32[]{:S(2)}, u32[]{:S(2)}) %collective-permute-start.12) | collective-permute-done | bytes 995360 | tf_op jit(solution)/shard_map/ppermute | solution.py:932
  501.9 12.4 %collective-permute-start.23 = (bf16[48,1152]{1,0:T(8,128)(2,1)S(1)}, bf16[48,1152]{1,0:T(8,128)(2,1)S(1)}, u32[]{:S(2)}, u32[]{:S(2)}) collective-permute-start(bf16[48,1152]{1,0:T(8,128)(2,1)S(1)} %fusion.13), channel_id=1, source_target_pairs={{0,16},{16,0},{1,17},{17,1},{2,18},{18,2},{3,19},{19,3},{4,20},{20... | collective-permute-start | bytes 331784 | tf_op jit(solution)/shard_map/ppermute | solution.py:943
  514.6 1.9 pad_maximum_fusion.3
  516.5 1.7 collective-permute-done.23
  518.2 1.5 collective-permute-done.24
  (140 shorter events, 41.7 us)
Async XLA Ops:
  7.2 65.3 %all-gather.5.cloned.1.call-start = ((), (), s32[]{:S(2)}) async-start(), calls=%async_computation.2 | async-start | bytes 5013504 | tf_op jit(solution)/shard_map/all_gather | solution.py:962
  16.2 151.8 %all-gather.7.cloned.1.call-start = ((), (), s32[]{:S(2)}) async-start(), calls=%async_computation.3 | async-start | bytes 11280384 | tf_op jit(solution)/shard_map/all_gather | solution.py:972
  19.2 4.9 collective-permute-start.1
  20.8 37.0 %collective-permute-start = (bf16[648,768]{1,0:T(8,128)(2,1)S(1)}, bf16[648,768]{1,0:T(8,128)(2,1)S(1)}, u32[]{:S(2)}, u32[]{:S(2)}) collective-permute-start(bf16[648,768]{1,0:T(8,128)(2,1)S(1)} %get-tuple-element.146), channel_id=1, source_target_pairs={{0,16},{16,0},{1,17},{17,1},{2,18},{18,2},{3,19},{19,3},{4,20},{20... | collective-permute-start | bytes 2985992 | tf_op jit(solution)/shard_map/ppermute | solution.py:925
  57.8 1.9 copy-start.10
  57.8 2.0 copy-start.11
  57.8 2.0 copy-start.12
  59.9 0.8 copy-start.8
  60.7 359.7 %reduce-scatter.2.cloned.1.call-start = ((), (), s32[]{:S(2)}) async-start(), calls=%async_computation.1 | async-start | bytes 11280384 | tf_op jit(solution)/shard_map/reduce_scatter | solution.py:1034
  74.0 1.4 copy-start.6
  91.5 3.2 copy-start.1
  96.2 46.2 %collective-permute-start.4 = (bf16[648,768]{1,0:T(8,128)(2,1)}, bf16[648,768]{1,0:T(8,128)(2,1)}, u32[]{:S(2)}, u32[]{:S(2)}) collective-permute-start(bf16[648,768]{1,0:T(8,128)(2,1)} %get-tuple-element.142), channel_id=1, source_target_pairs={{16,1},{1,16},{18,3},{3,18},{20,5},{5,20},{22,7},{7,22},{24,9},{9,... | collective-permute-start | bytes 2985992 | tf_op jit(solution)/shard_map/ppermute | solution.py:922
  97.8 45.8 %collective-permute-start.3 = (bf16[648,768]{1,0:T(8,128)(2,1)}, bf16[648,768]{1,0:T(8,128)(2,1)}, u32[]{:S(2)}, u32[]{:S(2)}) collective-permute-start(bf16[648,768]{1,0:T(8,128)(2,1)} %get-tuple-element.143), channel_id=1, source_target_pairs={{0,16},{16,0},{1,17},{17,1},{2,18},{18,2},{3,19},{19,3},{4,20},{20... | collective-permute-start | bytes 2985992 | tf_op jit(solution)/shard_map/ppermute | solution.py:925
  100.0 46.8 %collective-permute-start.2 = (bf16[2,648,768]{2,1,0:T(8,128)(2,1)}, bf16[2,648,768]{2,1,0:T(8,128)(2,1)S(1)}, u32[]{:S(2)}, u32[]{:S(2)}) collective-permute-start(bf16[2,648,768]{2,1,0:T(8,128)(2,1)} %slice_bitcast_fusion.2), channel_id=1, source_target_pairs={{0,1},{1,0},{2,3},{3,2},{4,5},{5,4},{6,7},{7,6},{8,9},{9,8},{10,11... | collective-permute-start | bytes 5971976 | tf_op jit(solution)/shard_map/ppermute | solution.py:992
  146.8 1.3 copy-start
  323.6 68.0 %collective-permute-start.7 = (bf16[2,648,768]{2,1,0:T(8,128)(2,1)}, bf16[2,648,768]{2,1,0:T(8,128)(2,1)}, u32[]{:S(2)}, u32[]{:S(2)}) collective-permute-start(bf16[2,648,768]{2,1,0:T(8,128)(2,1)} %slice_bitcast_fusion), channel_id=1, source_target_pairs={{0,1},{1,0},{2,3},{3,2},{4,5},{5,4},{6,7},{7,6},{8,9},{9,8},{10,11... | collective-permute-start | bytes 5971976 | tf_op jit(solution)/shard_map/ppermute | solution.py:1036
  324.5 67.1 %copy-start.4 = (bf16[2,2,648,768]{3,2,1,0:T(8,128)(2,1)S(1)}, bf16[2,2,648,768]{3,2,1,0:T(8,128)(2,1)}, u32[]{:S(2)}) copy-start(bf16[2,2,648,768]{3,2,1,0:T(8,128)(2,1)} %get-tuple-element.93) | copy-start | bytes 11943940
  408.9 5.8 %copy-start.13 = (f32[8,768]{1,0:T(8,128)S(1)}, f32[8,768]{1,0:T(8,128)}, u32[]{:S(2)}) copy-start(f32[8,768]{1,0:T(8,128)} %get-tuple-element.110) | copy-start | bytes 73732
  411.0 4.0 collective-permute-start.9
  413.2 4.6 collective-permute-start.8
  415.1 8.0 %copy-start.2 = (bf16[3,648,768]{2,1,0:T(8,128)(2,1)S(1)}, bf16[3,648,768]{2,1,0:T(8,128)(2,1)}, u32[]{:S(2)}) copy-start(bf16[3,648,768]{2,1,0:T(8,128)(2,1)} %get-tuple-element.80) | copy-start | bytes 8957956
  420.4 6.9 %copy-start.5 = (bf16[8,48,1152]{2,1,0:T(8,128)(2,1)S(1)}, bf16[8,48,1152]{2,1,0:T(8,128)(2,1)}, u32[]{:S(2)}) copy-start(bf16[8,48,1152]{2,1,0:T(8,128)(2,1)} %fusion.4) | copy-start | bytes 2654212
  421.5 23.4 %collective-permute-start.11 = (bf16[4,48,1152]{2,1,0:T(8,128)(2,1)S(1)}, bf16[4,48,1152]{2,1,0:T(8,128)(2,1)S(1)}, u32[]{:S(2)}, u32[]{:S(2)}) collective-permute-start(bf16[4,48,1152]{2,1,0:T(8,128)(2,1)S(1)} %dynamic-slice_bitcast_fusion.4), channel_id=1, source_target_pairs={{0,4},{1,5},{2,6},{3,7},{4,0},{5,1},{6,2},{7,3},{8,12},{9,13},{10,... | collective-permute-start | bytes 1327112 | tf_op jit(solution)/shard_map/ppermute | solution.py:886
  424.5 26.8 %collective-permute-start.5 = (bf16[648,768]{1,0:T(8,128)(2,1)}, bf16[648,768]{1,0:T(8,128)(2,1)}, u32[]{:S(2)}, u32[]{:S(2)}) collective-permute-start(bf16[648,768]{1,0:T(8,128)(2,1)} %get-tuple-element.140), channel_id=1, source_target_pairs={{0,16},{16,0},{1,17},{17,1},{2,18},{18,2},{3,19},{19,3},{4,20},{20... | collective-permute-start | bytes 2985992 | tf_op jit(solution)/shard_map/ppermute | solution.py:932
  425.7 25.7 %collective-permute-start.6 = (bf16[648,768]{1,0:T(8,128)(2,1)}, bf16[648,768]{1,0:T(8,128)(2,1)}, u32[]{:S(2)}, u32[]{:S(2)}) collective-permute-start(bf16[648,768]{1,0:T(8,128)(2,1)} %get-tuple-element.139), channel_id=1, source_target_pairs={{16,1},{1,16},{18,3},{3,18},{20,5},{5,20},{22,7},{7,22},{24,9},{9,... | collective-permute-start | bytes 2985992 | tf_op jit(solution)/shard_map/ppermute | solution.py:933
  428.1 18.7 %collective-permute-start.10 = (bf16[4,48,1152]{2,1,0:T(8,128)(2,1)}, bf16[4,48,1152]{2,1,0:T(8,128)(2,1)}, u32[]{:S(2)}, u32[]{:S(2)}) collective-permute-start(bf16[4,48,1152]{2,1,0:T(8,128)(2,1)} %dynamic-slice_bitcast_fusion.5), channel_id=1, source_target_pairs={{0,2},{1,3},{2,0},{3,1},{4,6},{5,7},{6,4},{7,5},{8,10},{9,11},{10,... | collective-permute-start | bytes 1327112 | tf_op jit(solution)/shard_map/ppermute | solution.py:886
  449.4 10.5 %collective-permute-start.18 = (f32[16,576]{1,0:T(8,128)S(1)}, f32[16,576]{1,0:T(8,128)S(1)}, u32[]{:S(2)}, u32[]{:S(2)}) collective-permute-start(f32[16,576]{1,0:T(8,128)S(1)} %concatenate.23), channel_id=1, source_target_pairs={{0,16},{16,0},{1,17},{17,1},{2,18},{18,2},{3,19},{19,3},{4,20},{20... | collective-permute-start | bytes 110600 | tf_op jit(solution)/shard_map/ppermute | solution.py:876
  459.9 5.1 collective-permute-start.19
  461.2 1.9 copy-start.9
  461.2 4.5 copy-start.7
  461.2 15.1 %copy-start.3 = (bf16[3,648,768]{2,1,0:T(8,128)(2,1)S(1)}, bf16[3,648,768]{2,1,0:T(8,128)(2,1)}, u32[]{:S(2)}) copy-start(bf16[3,648,768]{2,1,0:T(8,128)(2,1)} %get-tuple-element.104) | copy-start | bytes 8957956
  463.2 18.7 %collective-permute-start.25 = (bf16[432,768]{1,0:T(8,128)(2,1)S(1)}, bf16[432,768]{1,0:T(8,128)(2,1)S(1)}, u32[]{:S(2)}, u32[]{:S(2)}) collective-permute-start(bf16[432,768]{1,0:T(8,128)(2,1)S(1)} %bitcast.173), channel_id=1, source_target_pairs={{0,16},{16,0},{1,17},{17,1},{2,18},{18,2},{3,19},{19,3},{4,20},{20... | collective-permute-start | bytes 1990664 | tf_op jit(solution)/shard_map/ppermute | solution.py:943
  465.1 4.1 collective-permute-start.20
  465.7 17.1 %collective-permute-start.16 = (bf16[2,48,1152]{2,1,0:T(8,128)(2,1)S(1)}, bf16[2,48,1152]{2,1,0:T(8,128)(2,1)S(1)}, u32[]{:S(2)}, u32[]{:S(2)}) collective-permute-start(bf16[2,48,1152]{2,1,0:T(8,128)(2,1)S(1)} %dynamic-slice_bitcast_fusion.6), channel_id=1, source_target_pairs={{0,8},{1,9},{2,10},{3,11},{4,12},{5,13},{6,14},{7,15},{8,0},{9,1},... | collective-permute-start | bytes 663560 | tf_op jit(solution)/shard_map/ppermute | solution.py:886
  469.1 5.2 collective-permute-start.21
  469.6 15.6 %collective-permute-start.14 = (bf16[2,48,1152]{2,1,0:T(8,128)(2,1)S(1)}, bf16[2,48,1152]{2,1,0:T(8,128)(2,1)S(1)}, u32[]{:S(2)}, u32[]{:S(2)}) collective-permute-start(bf16[2,48,1152]{2,1,0:T(8,128)(2,1)S(1)} %dynamic-slice_bitcast_fusion.7), channel_id=1, source_target_pairs={{0,4},{1,5},{2,6},{3,7},{4,0},{5,1},{6,2},{7,3},{8,12},{9,13},{10,... | collective-permute-start | bytes 663560 | tf_op jit(solution)/shard_map/ppermute | solution.py:886
  474.4 5.6 %collective-permute-start.22 = (f32[16,576]{1,0:T(8,128)S(1)}, f32[16,576]{1,0:T(8,128)S(1)}, u32[]{:S(2)}, u32[]{:S(2)}) collective-permute-start(f32[16,576]{1,0:T(8,128)S(1)} %add.174), channel_id=1, source_target_pairs={{0,8},{1,9},{2,10},{3,11},{4,12},{5,13},{6,14},{7,15},{8,0},{9,1},... | collective-permute-start | bytes 110600 | tf_op jit(solution)/shard_map/ppermute | solution.py:876
  476.5 25.4 %collective-permute-start.12 = (bf16[648,768]{1,0:T(8,128)(2,1)S(1)}, bf16[648,768]{1,0:T(8,128)(2,1)S(1)}, u32[]{:S(2)}, u32[]{:S(2)}) collective-permute-start(bf16[648,768]{1,0:T(8,128)(2,1)S(1)} %get-tuple-element.137), channel_id=1, source_target_pairs={{0,16},{16,0},{1,17},{17,1},{2,18},{18,2},{3,19},{19,3},{4,20},{20... | collective-permute-start | bytes 2985992 | tf_op jit(solution)/shard_map/ppermute | solution.py:932
  480.0 21.9 %collective-permute-start.13 = (bf16[648,768]{1,0:T(8,128)(2,1)S(1)}, bf16[648,768]{1,0:T(8,128)(2,1)S(1)}, u32[]{:S(2)}, u32[]{:S(2)}) collective-permute-start(bf16[648,768]{1,0:T(8,128)(2,1)S(1)} %get-tuple-element.136), channel_id=1, source_target_pairs={{16,1},{1,16},{18,3},{3,18},{20,5},{5,20},{22,7},{7,22},{24,9},{9,... | collective-permute-start | bytes 2985992 | tf_op jit(solution)/shard_map/ppermute | solution.py:933
  482.9 5.4 %collective-permute-start.17 = (bf16[1,48,1152]{2,1,0:T(8,128)(2,1)S(1)}, bf16[1,48,1152]{2,1,0:T(8,128)(2,1)S(1)}, u32[]{:S(2)}, u32[]{:S(2)}) collective-permute-start(bf16[1,48,1152]{2,1,0:T(8,128)(2,1)S(1)} %constant_dynamic-slice_fusion.2), channel_id=1, source_target_pairs={{0,2},{1,3},{2,0},{3,1},{4,6},{5,7},{6,4},{7,5},{8,10},{9,11},{10,... | collective-permute-start | bytes 331784 | tf_op jit(solution)/shard_map/ppermute | solution.py:886
  486.2 8.9 %collective-permute-start.15 = (bf16[1,48,1152]{2,1,0:T(8,128)(2,1)S(1)}, bf16[1,48,1152]{2,1,0:T(8,128)(2,1)S(1)}, u32[]{:S(2)}, u32[]{:S(2)}) collective-permute-start(bf16[1,48,1152]{2,1,0:T(8,128)(2,1)S(1)} %constant_dynamic-slice_fusion.3), channel_id=1, source_target_pairs={{0,8},{1,9},{2,10},{3,11},{4,12},{5,13},{6,14},{7,15},{8,0},{9,1},... | collective-permute-start | bytes 331784 | tf_op jit(solution)/shard_map/ppermute | solution.py:886
  501.9 16.3 %collective-permute-start.23 = (bf16[48,1152]{1,0:T(8,128)(2,1)S(1)}, bf16[48,1152]{1,0:T(8,128)(2,1)S(1)}, u32[]{:S(2)}, u32[]{:S(2)}) collective-permute-start(bf16[48,1152]{1,0:T(8,128)(2,1)S(1)} %fusion.13), channel_id=1, source_target_pairs={{0,16},{16,0},{1,17},{17,1},{2,18},{18,2},{3,19},{19,3},{4,20},{20... | collective-permute-start | bytes 331784 | tf_op jit(solution)/shard_map/ppermute | solution.py:943
  514.3 5.4 %collective-permute-start.24 = (bf16[48,1152]{1,0:T(8,128)(2,1)S(1)}, bf16[48,1152]{1,0:T(8,128)(2,1)S(1)}, u32[]{:S(2)}, u32[]{:S(2)}) collective-permute-start(bf16[48,1152]{1,0:T(8,128)(2,1)S(1)} %fusion.14), channel_id=1, source_target_pairs={{0,16},{16,0},{1,17},{17,1},{2,18},{18,2},{3,19},{19,3},{4,20},{20... | collective-permute-start | bytes 331784 | tf_op jit(solution)/shard_map/ppermute | solution.py:943
Sparse Core Ops, SparseCore 0:
  16.4 56.0 all-gather.4
  74.8 87.2 all-gather.6
  286.9 119.1 reduce-scatter.1
where the time goes:
time: 537 us; the launch traced here: 527 us
  Pallas kernels  321 us (60%)
  waiting for transfers between devices  77 us (14%)
  starting transfers between devices  42.6 us (8%)
  local copies, waits for them, and re-layouts  42.6 us (8%)
  other arithmetic  29.3 us (5%)
  between operations  14.3 us (3%)
    pallas_call x2, Pallas kernels, mix_back(): pl.pallas_call(functools.partial(mix_back_kernel, unit_count), grid=(pair...  101 us
    pallas_call x1, Pallas kernels, feed(): pl.pallas_call(feed_kernel, grid=(count,), in_specs=[rows(width), rows(wi...  83.8 us
    pallas_call x2, Pallas kernels, mix(): pl.pallas_call(mix_kernel, grid=(pairs, unit_count), in_specs=[pl.BlockSp...  57.9 us
    pallas_call x1, Pallas kernels, weight_grads(): pl.pallas_call(functools.partial(weight_kernel, parts, shards), grid=(2 *...  34.9 us
    ppermute x2, waiting for transfers between devices, gather_units(): lax.ppermute(lax.dynamic_index_in_dim(values, 2 * (1 - side), 0, False),...  32.3 us
    pallas_call x1, Pallas kernels, input_grads(): pl.pallas_call(input_kernel, grid=(count,), in_specs=[rows, rows, rows, p...  16.3 us
    ppermute x5, waiting for transfers between devices, tree_sum(): value = value + lax.ppermute(value, axis, pairs)  15.5 us
    ppermute x3, starting transfers between devices, both(): lax.ppermute(value, 'seq', swap_sides).astype(F32)  14.3 us
  transfers between devices with their start and end apart: 29, of which 11 were waited for; matrix products, arithmetic and copies ran while one was open for 11% of the time, Pallas kernels for 38%

commit v1 on v0

--- a/solution.py
+++ b/solution.py
@@ -338,21 +338,27 @@
     return weight_ref[:, :rows, part * width : (part + 1) * width].reshape(width, width)
 
 
-def project_kernel(x_ref, weight_ref, gain_ref, shift_ref, bias_ref, qkv_ref, normed_ref):
-    width = x_ref.shape[-1]
+def project_kernel(x_ref, weight_ref, vectors_ref, qkv_ref, normed_ref, other_ref):
+    step = pl.program_id(0)
     normed, unused_unit, unused_scale = normalize(
-        x_ref[0].astype(F32), gain_ref[...], shift_ref[...]
+        x_ref[0].astype(F32), vectors_ref[0:1], vectors_ref[1:2]
     )
     low = normed.astype(BF16)
     normed_ref[0] = low
     for part in range(3):
-        value = mul(low, qkv_part(weight_ref, part)) + bias_ref[part : part + 1]
+        value = mul(low, qkv_part(weight_ref, part))
         if part == 0:
-            value = value * HEAD_DIM ** (-0.5)
+            value = (value + vectors_ref[2:3]) * HEAD_DIM ** (-0.5)
+        elif part == 2:
+            value = value + vectors_ref[3:4]
         qkv_ref[part, 0] = value.astype(BF16)
 
-
-def project(units, weight, gain, shift, bias):
+    @pl.when(step == pl.num_programs(0) - 1)
+    def last():
+        other_ref[...] = qkv_ref[1:, 0]
+
+
+def project(units, weight, vectors):
     count, size, width = units.shape
     return pl.pallas_call(
         project_kernel,
@@ -360,15 +366,18 @@
         in_specs=[
             pl.BlockSpec((1, size, width), lambda u: (u, 0, 0)),
             whole(weight.shape),
-            whole(gain.shape),
-            whole(shift.shape),
-            whole(bias.shape),
+            whole(vectors.shape),
         ],
         out_specs=[
             pl.BlockSpec((3, 1, size, width), lambda u: (0, u, 0, 0)),
             pl.BlockSpec((1, size, width), lambda u: (u, 0, 0)),
-        ],
-        out_shape=[shaped((3, count, size, width), BF16), shaped((count, size, width), BF16)],
+            whole((2, size, width)),
+        ],
+        out_shape=[
+            shaped((3, count, size, width), BF16),
+            shaped((count, size, width), BF16),
+            shaped((2, size, width), BF16),
+        ],
         compiler_params=params(1),
         cost_estimate=pl.CostEstimate(
             flops=2 * count * size * width * 3 * width,
@@ -376,7 +385,36 @@
             transcendentals=0,
         ),
         name="project",
-    )(units, weight, gain, shift, bias)
+    )(units, weight, vectors)
+
+
+def head_kernel(weight_ref, hidden_ref, *rest):
+    out_ref = rest[-1]
+    short = jnp.concatenate([ref[...].astype(F32) for ref in rest[:-1]], 0)
+    count, length = short.shape
+    columns = weight_ref.shape[1]
+    hidden = hidden_ref[...].astype(F32)
+    wide = hidden.shape[1]
+    hidden = jnp.concatenate([hidden, jnp.zeros((count - 1, wide), F32)], 0)
+    lines = jnp.concatenate(
+        [
+            short,
+            jnp.zeros((count, 128 - length), F32),
+            hidden,
+            jnp.zeros((count, columns - 128 - wide), F32),
+        ],
+        1,
+    )
+    out_ref[...] = jnp.concatenate([weight_ref[...].astype(F32), lines], 0).astype(BF16)
+
+
+def head_pack(weight, hidden, short):
+    rows, columns = weight.shape
+    return pl.pallas_call(
+        head_kernel,
+        out_shape=shaped((rows + len(short), columns), BF16),
+        name="head_pack",
+    )(weight, hidden[None], *[value[None] for value in short])
 
 
 def head_mask(size):
@@ -459,7 +497,7 @@
     lse_ref,
     *rest,
 ):
-    dq_ref, dkv_ref, dk_acc, dv_acc = rest[-4:]
+    dq_ref, dkv_ref, last_ref, dk_acc, dv_acc = rest[-5:]
     step = pl.program_id(1)
     query = q_ref[0, 0]
     grad = do_ref[0]
@@ -498,10 +536,12 @@
         dqs.append(dq)
     dq_ref[0] = (jnp.concatenate(dqs, 0).T * HEAD_DIM ** (-0.5)).astype(BF16)
     if unit_count == 1:
-        for side in range(2):
-            dkv_ref[0, side] = dks[side].astype(BF16)
-            dkv_ref[1, side] = dvs[side].astype(BF16)
+        for side, ref in enumerate((dkv_ref, last_ref)):
+            ref[0, 0] = dks[side].astype(BF16)
+            ref[1, 0] = dvs[side].astype(BF16)
         return
+
+    last_ref[...] = jnp.zeros_like(last_ref)
 
     @pl.when(step == 0)
     def first():
@@ -527,6 +567,15 @@
     lanes = 2 * HEAD_DIM
     pairs = width // lanes
     units = qkv.shape[1]
+    if unit_count == 1:
+        key_outs = [pl.BlockSpec((2, 1, size, lanes), lambda h, u: (0, 0, 0, h))] * 2
+        key_shapes = [shaped((2, 1, size, width), BF16)] * 2
+    else:
+        key_outs = [
+            pl.BlockSpec((2, 2, size, lanes), lambda h, u: (0, 0, 0, h)),
+            pl.BlockSpec((8, lanes), lambda h, u: (0, 0)),
+        ]
+        key_shapes = [shaped((2, units, size, width), BF16), shaped((8, lanes), F32)]
     return pl.pallas_call(
         functools.partial(mix_back_kernel, unit_count),
         grid=(pairs, unit_count),
@@ -540,12 +589,9 @@
         + [pl.BlockSpec(memory_space=pl.ANY)] * (earlier is not None),
         out_specs=[
             pl.BlockSpec((1, size, lanes), lambda h, u: (first_unit + u, 0, h)),
-            pl.BlockSpec((2, 2, size, lanes), lambda h, u: (0, 0, 0, h)),
-        ],
-        out_shape=[
-            shaped((units, size, width), BF16),
-            shaped((2, 2 if earlier is None else units, size, width), BF16),
-        ],
+            *key_outs,
+        ],
+        out_shape=[shaped((units, size, width), BF16), *key_shapes],
         input_output_aliases={} if earlier is None else {8: 0},
         scratch_shapes=[pltpu.VMEM((2, size, lanes), F32)] * 2,
         compiler_params=params(2),
@@ -562,16 +608,9 @@
 
 
 def gelu_pair(value):
-    size = jnp.abs(value) * 0.5**0.5
-    turn = 1.0 / (1.0 + 0.3275911 * size)
-    bell = jnp.exp(-size * size)
-    series = turn * (
-        0.254829592
-        + turn * (-0.284496736 + turn * (1.421413741 + turn * (-1.453152027 + turn * 1.061405429)))
-    )
-    tail = 0.5 * series * bell
-    share = jnp.where(value >= 0, 1.0 - tail, tail)
-    return value * share, share + value * (bell * 0.3989422804014327)
+    share = 0.5 + 0.5 * lax.erf(value * 0.5**0.5)
+    density = jnp.exp(value * value * -0.5) * 0.3989422804014327
+    return value * share, share + value * density
 
 
 def column(values):
@@ -583,13 +622,9 @@
     o_ref,
     cot_ref,
     weights_ref,
-    gain_ref,
-    shift_ref,
-    proj_bias_ref,
+    vectors_ref,
     hidden_bias_ref,
-    output_bias_ref,
     out_ref,
-    dx_ref,
     do_ref,
     normed_ref,
     act_ref,
@@ -611,13 +646,13 @@
         hidden_sum_ref[...] = jnp.zeros_like(hidden_sum_ref)
 
     proj = weights_ref[:, 2 * parts * rows :, :].reshape(width, width)
-    middle = x_ref[0].astype(F32) + (mul(o_ref[0], proj) + proj_bias_ref[...])
-    gain = gain_ref[...]
-    normed, unit, scale = normalize(middle, gain, shift_ref[...])
+    middle = x_ref[0].astype(F32) + (mul(o_ref[0], proj) + vectors_ref[4:5])
+    gain = vectors_ref[5:6]
+    normed, unit, scale = normalize(middle, gain, vectors_ref[6:7])
     low = normed.astype(BF16)
     normed_ref[0] = low
     upstream = cot_ref[0]
-    branch = middle + output_bias_ref[...]
+    branch = middle + vectors_ref[7:8]
     grad_normed = None
     for part in range(parts):
         first = weights_ref[:, part * rows : (part + 1) * rows, :].reshape(width, width)
@@ -639,7 +674,6 @@
     out_ref[0] = branch.astype(BF16)
     wide = upstream.astype(F32)
     grad_middle = wide + norm_back(grad_normed, unit, scale, gain)
-    dx_ref[0] = grad_middle
     low_middle = grad_middle.astype(BF16)
     dp_ref[0] = low_middle
     do_ref[0] = mul_nt(low_middle, proj).astype(BF16)
@@ -649,7 +683,7 @@
     sums_ref[3:4] += column(low_middle.astype(F32))
 
 
-def feed(units, mixed, cotangent, weights, gain, shift, proj_bias, hidden_bias, output_bias):
+def feed(units, mixed, cotangent, weights, vectors, hidden_bias):
     count, size, width = units.shape
     inner = hidden_bias.shape[-1]
 
@@ -664,14 +698,10 @@
             rows(width),
             rows(width),
             whole(weights.shape),
-            whole(gain.shape),
-            whole(shift.shape),
-            whole(proj_bias.shape),
+            whole(vectors.shape),
             whole(hidden_bias.shape),
-            whole(output_bias.shape),
         ],
         out_specs=[
-            rows(width),
             rows(width),
             rows(width),
             rows(width),
@@ -683,7 +713,6 @@
         ],
         out_shape=[
             shaped((count, size, width), BF16),
-            shaped((count, size, width), F32),
             shaped((count, size, width), BF16),
             shaped((count, size, width), BF16),
             shaped((count, size, inner), BF16),
@@ -699,7 +728,7 @@
             transcendentals=2 * count * size * inner,
         ),
         name="feed",
-    )(units, mixed, cotangent, weights, gain, shift, proj_bias, hidden_bias, output_bias)
+    )(units, mixed, cotangent, weights, vectors, hidden_bias)
 
 
 def weight_kernel(parts, shards, normed_ref, dh_ref, act_ref, dz_ref, o_ref, dp_ref, out_ref, left, right):
@@ -724,10 +753,10 @@
 
         @pl.when(step == parts + part)
         def second():
-            grad = mul(right[...], act_ref[...]).T
+            grad = mul(right[...], act_ref[...]).astype(BF16).T
             out_ref[
                 part * per_part : (part + 1) * per_part, parts * rows : 2 * parts * rows, :
-            ] = grad.astype(BF16).reshape(per_part, parts * rows, width)
+            ] = grad.reshape(per_part, parts * rows, width)
 
     @pl.when(step == 2 * parts)
     def third():
@@ -825,27 +854,34 @@
     )(normed, dq, dkv)
 
 
-def input_kernel(x_ref, dx_ref, dq_ref, dkv_ref, weight_ref, gain_ref, shift_ref, out_ref, sums_ref):
+def input_kernel(
+    x_ref, dx_ref, dq_ref, dkv_ref, weight_ref, vectors_ref, first_ref, second_ref, third_ref, sums_ref
+):
     step = pl.program_id(0)
-    width = x_ref.shape[-1]
 
     @pl.when(step == 0)
     def clear():
         sums_ref[...] = jnp.zeros_like(sums_ref)
 
-    gain = gain_ref[...]
-    unused, unit, scale = normalize(x_ref[0].astype(F32), gain, shift_ref[...])
+    gain = vectors_ref[0:1]
+    unused, unit, scale = normalize(x_ref[0].astype(F32), gain, vectors_ref[1:2])
     grad = mul_nt(dq_ref[0], qkv_part(weight_ref, 0))
     grad = grad + mul_nt(dkv_ref[0, 0], qkv_part(weight_ref, 1))
     grad = grad + mul_nt(dkv_ref[1, 0], qkv_part(weight_ref, 2))
-    out_ref[0] = (dx_ref[0] + norm_back(grad, unit, scale, gain)).astype(BF16)
+    value = (dx_ref[0].astype(F32) + norm_back(grad, unit, scale, gain)).astype(BF16)
+    for place, ref in enumerate((first_ref, second_ref, third_ref)):
+
+        @pl.when(step == place)
+        def keep():
+            ref[...] = value
+
     sums_ref[0:1] += column(grad * unit)
     sums_ref[1:2] += column(grad)
     sums_ref[2:3] += column(dq_ref[0].astype(F32))
     sums_ref[3:4] += column(dkv_ref[1, 0].astype(F32))
 
 
-def input_grads(units, grad_middle, dq, dkv, weight, gain, shift):
+def input_grads(units, grad_middle, dq, dkv, weight, vectors):
     count, size, width = units.shape
     rows = pl.BlockSpec((1, size, width), lambda u: (u, 0, 0))
     return pl.pallas_call(
@@ -857,25 +893,14 @@
             rows,
             pl.BlockSpec((2, 1, size, width), lambda u: (0, u, 0, 0)),
             whole(weight.shape),
-            whole(gain.shape),
-            whole(shift.shape),
-        ],
-        out_specs=[rows, pl.BlockSpec((8, width), lambda u: (0, 0))],
-        out_shape=[shaped((count, size, width), BF16), shaped((8, width), F32)],
+            whole(vectors.shape),
+        ],
+        out_specs=[whole((size, width))] * 3 + [pl.BlockSpec((8, width), lambda u: (0, 0))],
+        out_shape=[shaped((size, width), BF16)] * 3 + [shaped((8, width), F32)],
         compiler_params=params(1),
         cost_estimate=LATE,
         name="input_grads",
-    )(units, grad_middle, dq, dkv, weight, gain, shift)
-
-
-def tree_sum(value, axes):
-    for axis, size in axes:
-        reach = 1
-        while reach < size:
-            pairs = [(index, index ^ reach) for index in range(size)]
-            value = value + lax.ppermute(value, axis, pairs)
-            reach *= 2
-    return value
+    )(units, grad_middle, dq, dkv, weight, vectors)
 
 
 def halving_sum(value, axis, size, place, order):
@@ -944,7 +969,7 @@
 
     parts = hidden_weight.shape[1] // width
     rows = hidden_weight.shape[0]
-    small = [
+    short = [
         first_gain,
         first_shift,
         query_bias,
@@ -953,13 +978,9 @@
         second_gain,
         second_shift,
         output_bias,
-        hidden_bias,
     ]
-    sizes = [value.shape[0] for value in small]
-    starts = [sum(sizes[:index]) for index in range(len(sizes))]
-    lines = [jnp.pad(value[None], ((0, 0), (0, 3 * width - value.shape[0]))) for value in small]
-    lines.append(jnp.zeros((16 - len(small), 3 * width), BF16))
-    full_head = lax.all_gather(jnp.concatenate([qkv_weight] + lines, 0), "fsdp", axis=0)
+    count = first_gain.shape[0]
+    full_head = lax.all_gather(head_pack(qkv_weight, hidden_bias, short), "fsdp", axis=0)
     units = gather_units(inputs)
     hidden_weight, output_weight, proj_weight, units = lax.optimization_barrier(
         (hidden_weight, output_weight, proj_weight, units)
@@ -970,25 +991,12 @@
         0,
     )
     full_pack = lax.all_gather(pack, "fsdp", axis=0)
-    all_small = full_head[:, rows:].astype(F32)
-    (
-        gain_one,
-        shift_one,
-        bias_query,
-        bias_value,
-        bias_proj,
-        gain_two,
-        shift_two,
-        bias_output,
-        bias_hidden,
-    ) = [
-        all_small[:, index, :count].reshape(1, fsdp_size * count)
-        for index, count in enumerate(sizes)
-    ]
-
-    bias_qkv = jnp.concatenate([bias_query, jnp.zeros_like(bias_query), bias_value], 0)
-    qkv, normed = project(units, full_head, gain_one, shift_one, bias_qkv)
-    to_other, cotangent = lax.optimization_barrier((qkv[1:, 2], cotangent))
+    vectors = full_head[:, rows:, :count].astype(F32).transpose(1, 0, 2)
+    vectors = vectors.reshape(len(short), width)
+    bias_hidden = full_head[:, rows, 128 : 128 + hidden_bias.shape[0]].astype(F32)
+    bias_hidden = bias_hidden.reshape(1, parts * width)
+    qkv, normed, to_other = project(units, full_head, vectors)
+    to_other, cotangent = lax.optimization_barrier((to_other, cotangent))
     other = lax.ppermute(to_other, "fsdp", swap_cores)[:, None]
     grads_up = gather_units(cotangent)
     places_pair = [(qkv, 1, 0), (qkv, 2, 0), (qkv, 1, 1), (qkv, 2, 1)]
@@ -997,7 +1005,6 @@
     mixed, lse_one = mix(qkv, 2, 1, places_one, mixed_pair)
     (
         out,
-        grad_middle,
         grad_mixed,
         normed_two,
         active,
@@ -1005,17 +1012,7 @@
         grad_attended,
         sums_two,
         sum_hidden,
-    ) = feed(
-        units,
-        mixed,
-        grads_up,
-        full_pack,
-        gain_two,
-        shift_two,
-        bias_proj,
-        bias_hidden,
-        bias_output,
-    )
+    ) = feed(units, mixed, grads_up, full_pack, vectors, bias_hidden)
     block_out = return_units(out)
 
     def flat(value):
@@ -1032,10 +1029,10 @@
     )
     grad_mixed, grad_pack = lax.optimization_barrier((grad_mixed, grad_pack))
     shard_pack = lax.psum_scatter(grad_pack, "fsdp", scatter_dimension=0, tiled=False)
-    dq_one, dkv_one = mix_back(qkv, 2, 1, places_one, mixed, grad_mixed, lse_one)
-    dkv_got = lax.ppermute(dkv_one[:, 1], "fsdp", swap_cores)
-    dq, dkv = mix_back(qkv, 0, 2, places_pair, mixed, grad_mixed, lse_pair, dq_one)
-    dkv = dkv.at[:, 2].set((dkv_one[:, 0].astype(F32) + dkv_got.astype(F32)).astype(BF16))
+    dq_one, dkv_one, dkv_other = mix_back(qkv, 2, 1, places_one, mixed, grad_mixed, lse_one)
+    dkv_got = lax.ppermute(dkv_other, "fsdp", swap_cores)
+    dq, dkv, unused = mix_back(qkv, 0, 2, places_pair, mixed, grad_mixed, lse_pair, dq_one)
+    dkv = dkv.at[:, 2].set((dkv_one.astype(F32) + dkv_got.astype(F32)).astype(BF16)[:, 0])
     sides = qkv_weight_grad(flat(normed), flat(dq), dkv.reshape(2, row_count, width), fsdp_size)
     orders = halving_orders(fsdp_size)
     sides = [
@@ -1048,14 +1045,12 @@
         halving_sum(value, "fsdp", fsdp_size, place, order[1:2])
         for value, order in zip(sides, orders)
     ]
-    grad_units, sums_one = input_grads(units, grad_middle, dq, dkv, full_head, gain_one, shift_one)
+    *grad_units, sums_one = input_grads(units, grad_attended, dq, dkv, full_head, vectors)
     sides, grad_units, sums_one = lax.optimization_barrier((sides, grad_units, sums_one))
     shard_sides = [
         halving_sum(value, "fsdp", fsdp_size, place, order[2:])[0]
         for value, order in zip(sides, orders)
     ]
-    input_grad, shard_sides = return_units(grad_units, shard_sides)
-
     small_grads = [
         sums_one[0],
         sums_one[1],
@@ -1068,8 +1063,15 @@
         sum_hidden[0],
     ]
     packed = jnp.concatenate([value.reshape(fsdp_size, -1) for value in small_grads], 1)
-    packed = tree_sum(packed, [("seq", 2), ("fsdp", fsdp_size)])
-    mine = lax.dynamic_index_in_dim(packed, place, 0, False)
+    packed = jnp.pad(packed, ((0, 0), (0, -packed.shape[1] % 1024)))
+    packed = packed.reshape(-1, 128)
+    mine = lax.psum_scatter(packed, "fsdp", scatter_dimension=0, tiled=True)
+    shard_sides = [both(value) for value in shard_sides]
+    input_grad, shard_sides = return_units(grad_units, shard_sides)
+    mine = both(mine).reshape(-1)
+    pieces = []
+    for index in range(len(short)):
+        pieces.append(mine[index * count : (index + 1) * count])
     (
         grad_gain_one,
         grad_shift_one,
@@ -1079,15 +1081,14 @@
         grad_gain_two,
         grad_shift_two,
         grad_output_b,
-        grad_hidden_b,
-    ) = [mine[start : start + count] for start, count in zip(starts, sizes)]
-
+    ) = pieces
+    grad_hidden_b = mine[len(short) * count :][: hidden_bias.shape[0]]
     grad_hidden_w = jnp.concatenate(
         [shard_pack[part * rows : (part + 1) * rows] for part in range(parts)], 1
     )
     grad_output_w = shard_pack[parts * rows : 2 * parts * rows]
     grad_proj_w = shard_pack[2 * parts * rows :]
-    grad_qkv_w = jnp.concatenate([both(value) for value in shard_sides], 1)
+    grad_qkv_w = jnp.concatenate(shard_sides, 1)
     return (
         block_out,
         input_grad,
@@ -1120,6 +1121,8 @@
             and width % 128 == 0
             and (width // fsdp_size) % 16 == 0
             and inner % width == 0
+            and width // fsdp_size <= 128
+            and 128 + inner // fsdp_size <= 3 * width
             and fsdp_size % (inner // width) == 0
         )
         if fits:

time: 537 us -> 578 us (1.076)
  waiting for transfers between devices: 77 us -> 161 us
  Pallas kernels: 321 us -> 298 us
  local copies, waits for them, and re-layouts: 42.6 us -> 26.4 us
    unnamed x3 -> x5, waiting for transfers between devices: 0.05 us -> 81.3 us
    pallas_call x1, Pallas kernels: 83.8 us -> 57.5 us  [feed(): pl.pallas_call(feed_kernel, grid=(count,), in_specs=[rows(width), rows(wi...]
    ppermute x6 -> x1, waiting for transfers between devices: 15.5 us -> 0.01 us  [fast_body(): dkv_got = lax.ppermute(dkv_other, 'fsdp', swap_cores)]
    ppermute x3 -> x4, waiting for transfers between devices: 3.18 us -> 18.2 us  [both(): lax.ppermute(value, 'seq', swap_sides).astype(F32)]
    ppermute x2, waiting for transfers between devices: 6.82 us -> 14.5 us  [return_units(): got = lax.ppermute(values[1], 'seq', swap_sides)]
    ppermute x6 -> x1, starting transfers between devices: 7.19 us -> 0.26 us  [fast_body(): dkv_got = lax.ppermute(dkv_other, 'fsdp', swap_cores)]
    squeeze x3 -> x0, local copies, waits for them, and re-layouts: 6.36 us -> none  [the longest x1 3.19 us: fast_body(): to_other, cotangent = lax.optimization_barrier((qkv[1:, 2], cotangent))]
    ppermute x3 -> x4, starting transfers between devices: 14.3 us -> 19.3 us  [both(): lax.ppermute(value, 'seq', swap_sides).astype(F32)]
  transfers between devices with their start and end apart: 29 -> 26, of which waited for: 11 -> 9; matrix products, arithmetic and copies ran while one was open for 11% -> 8% of each run, Pallas kernels for 38% -> 36%
where the time goes in v1:
time: 578 us; the launch traced here: 570 us
  Pallas kernels  298 us (52%)
  waiting for transfers between devices  161 us (28%)
  starting transfers between devices  42.3 us (7%)
  other arithmetic  26.8 us (5%)
  local copies, waits for them, and re-layouts  26.4 us (5%)
  between operations  15 us (3%)
    pallas_call x2, Pallas kernels, mix_back(): pl.pallas_call(functools.partial(mix_back_kernel, unit_count), grid=(pair...  101 us
    unnamed x5, waiting for transfers between devices  81.3 us
    pallas_call x2, Pallas kernels, mix(): pl.pallas_call(mix_kernel, grid=(pairs, unit_count), in_specs=[pl.BlockSp...  57.9 us
    pallas_call x1, Pallas kernels, feed(): pl.pallas_call(feed_kernel, grid=(count,), in_specs=[rows(width), rows(wi...  57.5 us
    pallas_call x1, Pallas kernels, weight_grads(): pl.pallas_call(functools.partial(weight_kernel, parts, shards), grid=(2 *...  35.1 us
    ppermute x2, waiting for transfers between devices, gather_units(): lax.ppermute(lax.dynamic_index_in_dim(values, 2 * (1 - side), 0, False),...  32.3 us
    ppermute x4, starting transfers between devices, both(): lax.ppermute(value, 'seq', swap_sides).astype(F32)  19.3 us
    ppermute x4, waiting for transfers between devices, both(): lax.ppermute(value, 'seq', swap_sides).astype(F32)  18.2 us
  transfers between devices with their start and end apart: 26, of which 9 were waited for; matrix products, arithmetic and copies ran while one was open for 8% of the time, Pallas kernels for 36%

profile of v1, /device:TPU:0, one launch (start us, length us, event | category | flops | bytes accessed | tf_op | source)
XLA Modules:
  0.0 569.6 jit_solution(4842473074064807043)
XLA Ops:
  8.4 1.7 head_pack.1
  10.3 3.0 constant_dynamic-slice_fusion.3
  13.2 1.6 collective-permute-start.1
  14.8 3.3 collective-permute-start
  18.1 1.3 select_bitcast_fusion.5
  19.4 32.3 %collective-permute-done = bf16[648,768]{1,0:T(8,128)(2,1)S(1)} collective-permute-done((bf16[648,768]{1,0:T(8,128)(2,1)S(1)}, bf16[648,768]{1,0:T(8,128)(2,1)S(1)}, u32[]{:S(2)}, u32[]{:S(2)}) %collective-permute-start) | collective-permute-done | bytes 995360 | tf_op jit(solution)/shard_map/ppermute | solution.py:950
  51.8 1.9 pad_maximum_fusion.x_ref
  54.8 9.1 %all-gather.5.cloned.1.call-done = bf16[896,2304]{1,0:T(8,128)(2,1)} async-done(((bf16[56,2304]{1,0:T(8,128)(2,1)}), bf16[896,2304]{1,0:T(8,128)(2,1)}) %all-gather.5.cloned.1.call-update) | async-done | bytes 4128784 | tf_op jit(solution)/shard_map/all_gather | solution.py:983
  65.3 14.5 %project.1 = (bf16[3,3,648,768]{3,2,1,0:T(8,128)(2,1)}, bf16[3,648,768]{2,1,0:T(8,128)(2,1)}, bf16[2,648,768]{2,1,0:T(8,128)(2,1)}) custom-call(bf16[3,648,768]{2,1,0:T(8,128)(2,1)} %pad_maximum_fusion.x_ref, bf16[16,56,2304]{2,1,0:T(8,128)(2,1)} %bitcast.118, f32[8,768]{1,0:T(8,128)} %reshape.181.vectors_ref), custom_call_target="tpu_custom_call" | custom-call | flops 6879707136 | bytes 18468864 | tf_op jit(solution)/shard_map/project/pallas_call | solution.py:363
  79.8 1.5 constant_dynamic-slice_fusion.2
  81.3 1.6 collective-permute-start.4
  82.9 2.2 collective-permute-start.3
  85.1 38.0 %mix.2 = (bf16[3,648,768]{2,1,0:T(8,128)(2,1)}, f32[2,6,8,648]{3,2,1,0:T(8,128)}) custom-call(bf16[3,3,648,768]{3,2,1,0:T(8,128)(2,1)} %get-tuple-element.77.q_ref.ka_ref.va_ref.kb_ref.vb_ref, bf16[3,3,648,768]{3,2,1,0:T(8,128)(2,1)} %get-tuple-element.77.q_ref.ka_ref.va_ref.kb_ref.vb_ref, ...), custom_call_target="tpu_custom_call" | custom-call | flops 20639121408 | bytes 7962624 | tf_op jit(solution)/shard_map/mix/pallas_call | solution.py:463
  124.7 1.3 select_bitcast_fusion.4
  126.1 3.1 pad_maximum_fusion.1.cot_ref
  129.2 1.3 copy-done
  130.5 19.9 %mix.3 = (bf16[3,648,768]{2,1,0:T(8,128)(2,1)}, f32[1,6,8,648]{3,2,1,0:T(8,128)}) custom-call(bf16[3,3,648,768]{3,2,1,0:T(8,128)(2,1)} %get-tuple-element.77.q_ref.ka_ref.va_ref.kb_ref.vb_ref, bf16[3,3,648,768]{3,2,1,0:T(8,128)(2,1)} %get-tuple-element.77.q_ref.ka_ref.va_ref.kb_ref.vb_ref, ...), custom_call_target="tpu_custom_call", output_to_operand_aliasing={{0}: (5, {})} | custom-call | flops 10319560704 | bytes 3981312 | tf_op jit(solution)/shard_map/mix/pallas_call | solution.py:463
  150.4 3.0 all-gather.7.cloned.1.call-done
  153.3 57.5 %feed.1 = (bf16[3,648,768]{2,1,0:T(8,128)(2,1)}, bf16[3,648,768]{2,1,0:T(8,128)(2,1)}, bf16[3,648,768]{2,1,0:T(8,128)(2,1)}, bf16[3,648,3072]{2,1,0:T(8,128)(2,1...) custom-call(bf16[3,648,768]{2,1,0:T(8,128)(2,1)} %pad_maximum_fusion.x_r, ...), custom_call_target="tpu_custom_call" | custom-call | flops 41278242816 | bytes 53747712 | tf_op jit(solution)/shard_map/feed/pallas_call | solution.py:693
  210.9 35.1 %weight_grads.1 = bf16[16,432,768]{2,1,0:T(8,128)(2,1)} custom-call(bf16[1944,768]{1,0:T(8,128)(2,1)} %bitcast.149, bf16[1944,3072]{1,0:T(8,128)(2,1)} %bitcast.148, bf16[1944,3072]{1,0:T(8,128)(2,1)} %bitcast.147, bf16[1944,768]{1,0:T(8,128)(2,1)} %bitcast.127, bf16[1944,768]{1,0:T(8,128)(2,1)} %bitcast.112, bf16[1944,768]{1,0:T(8,128)(2,1)} %bitcast.125), custom_call_target="tpu_custom_call" | custom-call | flops 20639121408 | bytes 35831808 | tf_op jit(solution)/shard_map/weight_grads/pallas_call | solution.py:772
  246.0 33.6 %mix_back.2 = (bf16[3,648,768]{2,1,0:T(8,128)(2,1)}, bf16[2,1,648,768]{3,2,1,0:T(8,128)(2,1)}, bf16[2,1,648,768]{3,2,1,0:T(8,128)(2,1)}) custom-call(bf16[3,3,648,768]{3,2,1,0:T(8,128)(2,1)} %get-tuple-element.77.q_ref.ka_ref.va_ref.kb_ref.vb_ref, bf16[3,3,648,768]{3,2,1,0:T(8,128)(2,1)} %get-tuple-element.77.q_ref.ka_ref.va_ref.kb_ref.vb_ref, ...), custom_call_target="tpu_custom_call" | custom-call | flops 1000 | bytes 1000 | tf_op jit(solution)/shard_map/mix_back/pallas_call | solution.py:579
  279.9 67.1 %mix_back.3 = (bf16[3,648,768]{2,1,0:T(8,128)(2,1)}, bf16[2,3,648,768]{3,2,1,0:T(8,128)(2,1)}, f32[8,128]{1,0:T(8,128)}) custom-call(bf16[3,3,648,768]{3,2,1,0:T(8,128)(2,1)} %get-tuple-element.77.q_ref.ka_ref.va_ref.kb_ref.vb_ref, bf16[3,3,648,768]{3,2,1,0:T(8,128)(2,1)} %get-tuple-element.77.q_ref.ka_ref.va_ref.kb_ref.vb_ref, ...), custom_call_target="tpu_custom_call", output_to_operand_aliasing={{0}: (8, {})} | custom-call | flops 1000 | bytes 1000 | tf_op jit(solution)/shard_map/mix_back/pallas_call | solution.py:579
  347.1 1.9 fusion.dkv_ref
  349.0 13.8 %qkv_weight_grad.1 = (bf16[16,48,1152]{2,1,0:T(8,128)(2,1)}, bf16[16,48,1152]{2,1,0:T(8,128)(2,1)}) custom-call(bf16[1944,768]{1,0:T(8,128)(2,1)} %bitcast.126, bf16[1944,768]{1,0:T(8,128)(2,1)} %bitcast.110, bf16[2,1944,768]{2,1,0:T(8,128)(2,1)} %bitcast.111), custom_call_target="tpu_custom_call" | custom-call | flops 1000 | bytes 1000 | tf_op jit(solution)/shard_map/qkv_weight_grad/pallas_call | solution.py:840
  362.8 2.3 dynamic-slice_bitcast_fusion.2
  367.5 2.2 dynamic-slice_bitcast_fusion.3
  371.6 1.4 slice_bitcast_fusion
  373.0 1.5 collective-permute-start.5
  374.4 1.6 collective-permute-start.6
  376.1 2.3 fusion.1
  378.4 2.3 fusion.2
  380.7 1.8 dynamic-slice_bitcast_fusion.4
  383.0 14.5 %collective-permute-done.5 = bf16[648,768]{1,0:T(8,128)(2,1)} collective-permute-done((bf16[648,768]{1,0:T(8,128)(2,1)}, bf16[648,768]{1,0:T(8,128)(2,1)}, u32[]{:S(2)}, u32[]{:S(2)}) %collective-permute-start.5) | collective-permute-done | bytes 995360 | tf_op jit(solution)/shard_map/ppermute | solution.py:957
  397.5 1.4 fusion.3
  398.9 1.9 pad_maximum_fusion.2
  400.8 12.4 %collective-permute-start.21 = (bf16[432,768]{1,0:T(8,128)(2,1)}, bf16[432,768]{1,0:T(8,128)(2,1)}, u32[]{:S(2)}, u32[]{:S(2)}) collective-permute-start(bf16[432,768]{1,0:T(8,128)(2,1)} %bitcast.41), channel_id=1, source_target_pairs={{0,16},{16,0},{1,17},{17,1},{2,18},{18,2},{3,19},{19,3},{4,20},{20... | collective-permute-start | bytes 1990664 | tf_op jit(solution)/shard_map/ppermute | solution.py:968
  413.9 17.0 %input_grads.1 = (bf16[648,768]{1,0:T(8,128)(2,1)}, bf16[648,768]{1,0:T(8,128)(2,1)}, bf16[648,768]{1,0:T(8,128)(2,1)}, f32[8,768]{1,0:T(8,128)}) custom-call(bf16[3,648,768]{2,1,0:T(8,128)(2,1)} %pad_maximum_fusion.x_ref, bf16[3,648,768]{2,1,0:T(8,128)(2,1)} %get-tuple-element.92.dx_ref, bf16[3,648,768]{2,1,0:T(8,128)(2,1)} %get-tuple-element.106.dq_ref, ...), custom_call_target="tpu_custom_call" | custom-call | flops 1000 | bytes 1000 | tf_op jit(solution)/shard_map/input_grads/pallas_call | solution.py:887
  435.1 1.6 collective-permute-start.17
  436.7 81.3 %all-reduce.4.cloned.1.call-done = f32[128,128]{1,0:T(8,128)} async-done(((f32[128,128]{1,0:T(8,128)}), f32[128,128]{1,0:T(8,128)}) %all-reduce.4.cloned.1.call-update) | async-done | bytes 65552
  518.7 1.5 collective-permute-start.20
  520.1 4.1 collective-permute-start.14
  527.4 1.4 convert_add_fusion.2
  532.1 1.4 collective-permute-start.15
  534.5 2.7 collective-permute-start.19
  537.2 1.7 collective-permute-done.15
  538.9 2.7 collective-permute-start.16
  541.7 17.0 %collective-permute-done.19 = bf16[48,1152]{1,0:T(8,128)(2,1)S(1)} collective-permute-done((bf16[48,1152]{1,0:T(8,128)(2,1)S(1)}, bf16[48,1152]{1,0:T(8,128)(2,1)S(1)}, u32[]{:S(2)}, u32[]{:S(2)}) %collective-permute-start.19) | collective-permute-done | bytes 110624 | tf_op jit(solution)/shard_map/ppermute | solution.py:968
  561.0 1.9 pad_maximum_fusion.3
  (119 shorter events, 24.9 us)
Async XLA Ops:
  7.2 56.7 %all-gather.5.cloned.1.call-start = ((), (), s32[]{:S(2)}) async-start(), calls=%async_computation.2 | async-start | bytes 4386816 | tf_op jit(solution)/shard_map/all_gather | solution.py:983
  10.2 143.1 %all-gather.7.cloned.1.call-start = ((), (), s32[]{:S(2)}) async-start(), calls=%async_computation.3 | async-start | bytes 11280384 | tf_op jit(solution)/shard_map/all_gather | solution.py:993
  13.2 4.9 collective-permute-start.1
  14.8 36.9 %collective-permute-start = (bf16[648,768]{1,0:T(8,128)(2,1)S(1)}, bf16[648,768]{1,0:T(8,128)(2,1)S(1)}, u32[]{:S(2)}, u32[]{:S(2)}) collective-permute-start(bf16[648,768]{1,0:T(8,128)(2,1)S(1)} %get-tuple-element.143), channel_id=1, source_target_pairs={{0,16},{16,0},{1,17},{17,1},{2,18},{18,2},{3,19},{19,3},{4,20},{20... | collective-permute-start | bytes 2985992 | tf_op jit(solution)/shard_map/ppermute | solution.py:950
  51.8 1.9 copy-start.11
  51.8 2.0 copy-start.12
  51.8 2.0 copy-start.13
  53.9 0.9 copy-start.10
  54.8 326.0 %reduce-scatter.2.cloned.1.call-start = ((), (), s32[]{:S(2)}) async-start(), calls=%async_computation.1 | async-start | bytes 11280384 | tf_op jit(solution)/shard_map/reduce_scatter | solution.py:1031
  65.3 14.5 %copy-start.1 = (bf16[3,648,768]{2,1,0:T(8,128)(2,1)S(1)}, bf16[3,648,768]{2,1,0:T(8,128)(2,1)}, u32[]{:S(2)}) copy-start(bf16[3,648,768]{2,1,0:T(8,128)(2,1)} %param.18) | copy-start | bytes 8957956
  81.3 43.4 %collective-permute-start.4 = (bf16[648,768]{1,0:T(8,128)(2,1)}, bf16[648,768]{1,0:T(8,128)(2,1)}, u32[]{:S(2)}, u32[]{:S(2)}) collective-permute-start(bf16[648,768]{1,0:T(8,128)(2,1)} %get-tuple-element.139), channel_id=1, source_target_pairs={{16,1},{1,16},{18,3},{3,18},{20,5},{5,20},{22,7},{7,22},{24,9},{9,... | collective-permute-start | bytes 2985992 | tf_op jit(solution)/shard_map/ppermute | solution.py:947
  82.9 43.1 %collective-permute-start.3 = (bf16[648,768]{1,0:T(8,128)(2,1)}, bf16[648,768]{1,0:T(8,128)(2,1)}, u32[]{:S(2)}, u32[]{:S(2)}) collective-permute-start(bf16[648,768]{1,0:T(8,128)(2,1)} %get-tuple-element.140), channel_id=1, source_target_pairs={{0,16},{16,0},{1,17},{17,1},{2,18},{18,2},{3,19},{19,3},{4,20},{20... | collective-permute-start | bytes 2985992 | tf_op jit(solution)/shard_map/ppermute | solution.py:950
  85.1 44.1 %collective-permute-start.2 = (bf16[2,648,768]{2,1,0:T(8,128)(2,1)}, bf16[2,648,768]{2,1,0:T(8,128)(2,1)S(1)}, u32[]{:S(2)}, u32[]{:S(2)}) collective-permute-start(bf16[2,648,768]{2,1,0:T(8,128)(2,1)} %get-tuple-element.79), channel_id=1, source_target_pairs={{0,1},{1,0},{2,3},{3,2},{4,5},{5,4},{6,7},{7,6},{8,9},{9,8},{10,11... | collective-permute-start | bytes 5971976 | tf_op jit(solution)/shard_map/ppermute | solution.py:1000
  129.2 1.3 copy-start
  246.0 272.0 %all-reduce.4.cloned.1.call-start = ((), (), s32[]{:S(2)}) async-start(), calls=%async_computation.4 | async-start | bytes 131072
  279.7 67.4 %collective-permute-start.7 = (bf16[2,1,648,768]{3,2,1,0:T(8,128)(2,1)}, bf16[2,1,648,768]{3,2,1,0:T(8,128)(2,1)S(1)}, u32[]{:S(2)}, u32[]{:S(2)}) collective-permute-start(bf16[2,1,648,768]{3,2,1,0:T(8,128)(2,1)} %get-tuple-element.100), channel_id=1, source_target_pairs={{0,1},{1,0},{2,3},{3,2},{4,5},{5,4},{6,7},{7,6},{8,9},{9,8},{10,11... | collective-permute-start | bytes 5971976 | tf_op jit(solution)/shard_map/ppermute | solution.py:1033
  279.9 67.1 %copy-start.5 = (bf16[2,1,648,768]{3,2,1,0:T(8,128)(2,1)S(1)}, bf16[2,1,648,768]{3,2,1,0:T(8,128)(2,1)}, u32[]{:S(2)}) copy-start(bf16[2,1,648,768]{3,2,1,0:T(8,128)(2,1)} %get-tuple-element.99) | copy-start | bytes 5971972
  348.9 16.4 %copy-start.15 = (u32[32]{0:T(128)S(1)}, u32[32]{0:T(128)}, u32[]{:S(2)}) copy-start(u32[32]{0:T(128)} %constant.184) | copy-start | bytes 388
  362.8 7.2 %copy-start.14 = (f32[8,768]{1,0:T(8,128)S(1)}, f32[8,768]{1,0:T(8,128)}, u32[]{:S(2)}) copy-start(f32[8,768]{1,0:T(8,128)} %get-tuple-element.120) | copy-start | bytes 73732
  362.8 8.8 %copy-start.2 = (bf16[3,648,768]{2,1,0:T(8,128)(2,1)S(1)}, bf16[3,648,768]{2,1,0:T(8,128)(2,1)}, u32[]{:S(2)}) copy-start(bf16[3,648,768]{2,1,0:T(8,128)(2,1)} %get-tuple-element.86) | copy-start | bytes 8957956
  365.1 10.9 %collective-permute-start.9 = (bf16[8,48,1152]{2,1,0:T(8,128)(2,1)}, bf16[8,48,1152]{2,1,0:T(8,128)(2,1)}, u32[]{:S(2)}, u32[]{:S(2)}) collective-permute-start(bf16[8,48,1152]{2,1,0:T(8,128)(2,1)} %dynamic-slice_bitcast_fusion.2), channel_id=1, source_target_pairs={{0,1},{1,0},{2,3},{3,2},{4,5},{5,4},{6,7},{7,6},{8,9},{9,8},{10,11... | collective-permute-start | bytes 2654216 | tf_op jit(solution)/shard_map/ppermute | solution.py:911
  369.7 8.7 %collective-permute-start.8 = (bf16[8,48,1152]{2,1,0:T(8,128)(2,1)}, bf16[8,48,1152]{2,1,0:T(8,128)(2,1)}, u32[]{:S(2)}, u32[]{:S(2)}) collective-permute-start(bf16[8,48,1152]{2,1,0:T(8,128)(2,1)} %dynamic-slice_bitcast_fusion.3), channel_id=1, source_target_pairs={{0,1},{1,0},{2,3},{3,2},{4,5},{5,4},{6,7},{7,6},{8,9},{9,8},{10,11... | collective-permute-start | bytes 2654216 | tf_op jit(solution)/shard_map/ppermute | solution.py:911
  371.6 4.5 copy-start.7
  371.6 6.8 %copy-start.6 = (bf16[16,48,1152]{2,1,0:T(8,128)(2,1)S(1)}, bf16[16,48,1152]{2,1,0:T(8,128)(2,1)}, u32[]{:S(2)}) copy-start(bf16[16,48,1152]{2,1,0:T(8,128)(2,1)} %get-tuple-element.101) | copy-start | bytes 5308420
  373.0 24.5 %collective-permute-start.5 = (bf16[648,768]{1,0:T(8,128)(2,1)}, bf16[648,768]{1,0:T(8,128)(2,1)}, u32[]{:S(2)}, u32[]{:S(2)}) collective-permute-start(bf16[648,768]{1,0:T(8,128)(2,1)} %get-tuple-element.137), channel_id=1, source_target_pairs={{0,16},{16,0},{1,17},{17,1},{2,18},{18,2},{3,19},{19,3},{4,20},{20... | collective-permute-start | bytes 2985992 | tf_op jit(solution)/shard_map/ppermute | solution.py:957
  374.4 23.0 %collective-permute-start.6 = (bf16[648,768]{1,0:T(8,128)(2,1)}, bf16[648,768]{1,0:T(8,128)(2,1)}, u32[]{:S(2)}, u32[]{:S(2)}) collective-permute-start(bf16[648,768]{1,0:T(8,128)(2,1)} %get-tuple-element.136), channel_id=1, source_target_pairs={{16,1},{1,16},{18,3},{3,18},{20,5},{5,20},{22,7},{7,22},{24,9},{9,... | collective-permute-start | bytes 2985992 | tf_op jit(solution)/shard_map/ppermute | solution.py:958
  382.5 48.4 %collective-permute-start.11 = (bf16[4,48,1152]{2,1,0:T(8,128)(2,1)}, bf16[4,48,1152]{2,1,0:T(8,128)(2,1)S(1)}, u32[]{:S(2)}, u32[]{:S(2)}) collective-permute-start(bf16[4,48,1152]{2,1,0:T(8,128)(2,1)} %dynamic-slice_bitcast_fusion.4), channel_id=1, source_target_pairs={{0,4},{1,5},{2,6},{3,7},{4,0},{5,1},{6,2},{7,3},{8,12},{9,13},{10,... | collective-permute-start | bytes 1327112 | tf_op jit(solution)/shard_map/ppermute | solution.py:911
  398.9 14.4 %copy-start.4 = (bf16[8,48,1152]{2,1,0:T(8,128)(2,1)S(1)}, bf16[8,48,1152]{2,1,0:T(8,128)(2,1)}, u32[]{:S(2)}) copy-start(bf16[8,48,1152]{2,1,0:T(8,128)(2,1)} %fusion.2) | copy-start | bytes 2654212
  400.8 126.6 %collective-permute-start.21 = (bf16[432,768]{1,0:T(8,128)(2,1)}, bf16[432,768]{1,0:T(8,128)(2,1)}, u32[]{:S(2)}, u32[]{:S(2)}) collective-permute-start(bf16[432,768]{1,0:T(8,128)(2,1)} %bitcast.41), channel_id=1, source_target_pairs={{0,16},{16,0},{1,17},{17,1},{2,18},{18,2},{3,19},{19,3},{4,20},{20... | collective-permute-start | bytes 1990664 | tf_op jit(solution)/shard_map/ppermute | solution.py:968
  413.3 17.7 %copy-start.3 = (bf16[8,48,1152]{2,1,0:T(8,128)(2,1)S(1)}, bf16[8,48,1152]{2,1,0:T(8,128)(2,1)}, u32[]{:S(2)}) copy-start(bf16[8,48,1152]{2,1,0:T(8,128)(2,1)} %fusion.1) | copy-start | bytes 2654212
  413.3 17.8 %collective-permute-start.10 = (bf16[4,48,1152]{2,1,0:T(8,128)(2,1)S(1)}, bf16[4,48,1152]{2,1,0:T(8,128)(2,1)}, u32[]{:S(2)}, u32[]{:S(2)}) collective-permute-start(bf16[4,48,1152]{2,1,0:T(8,128)(2,1)S(1)} %dynamic-slice_bitcast_fusion.5), channel_id=1, source_target_pairs={{0,2},{1,3},{2,0},{3,1},{4,6},{5,7},{6,4},{7,5},{8,10},{9,11},{10,... | collective-permute-start | bytes 1327112 | tf_op jit(solution)/shard_map/ppermute | solution.py:911
  430.9 93.9 %copy-start.8 = (bf16[648,768]{1,0:T(8,128)(2,1)S(1)}, bf16[648,768]{1,0:T(8,128)(2,1)}, u32[]{:S(2)}) copy-start(bf16[648,768]{1,0:T(8,128)(2,1)} %get-tuple-element.114) | copy-start | bytes 2985988
  435.1 94.5 %collective-permute-start.17 = (bf16[2,48,1152]{2,1,0:T(8,128)(2,1)S(1)}, bf16[2,48,1152]{2,1,0:T(8,128)(2,1)S(1)}, u32[]{:S(2)}, u32[]{:S(2)}) collective-permute-start(bf16[2,48,1152]{2,1,0:T(8,128)(2,1)S(1)} %dynamic-slice_bitcast_fusion.6), channel_id=1, source_target_pairs={{0,8},{1,9},{2,10},{3,11},{4,12},{5,13},{6,14},{7,15},{8,0},{9,1},... | collective-permute-start | bytes 663560 | tf_op jit(solution)/shard_map/ppermute | solution.py:911
  518.7 6.1 %collective-permute-start.20 = (f32[8,128]{1,0:T(8,128)S(1)}, f32[8,128]{1,0:T(8,128)S(1)}, u32[]{:S(2)}, u32[]{:S(2)}) collective-permute-start(f32[8,128]{1,0:T(8,128)S(1)} %constant_dynamic-slice_fusion.4), channel_id=1, source_target_pairs={{0,16},{16,0},{1,17},{17,1},{2,18},{18,2},{3,19},{19,3},{4,20},{20... | collective-permute-start | bytes 12296 | tf_op jit(solution)/shard_map/ppermute | solution.py:968
  520.1 11.0 %collective-permute-start.14 = (bf16[2,48,1152]{2,1,0:T(8,128)(2,1)S(1)}, bf16[2,48,1152]{2,1,0:T(8,128)(2,1)S(1)}, u32[]{:S(2)}, u32[]{:S(2)}) collective-permute-start(bf16[2,48,1152]{2,1,0:T(8,128)(2,1)S(1)} %dynamic-slice_bitcast_fusion.7), channel_id=1, source_target_pairs={{0,4},{1,5},{2,6},{3,7},{4,0},{5,1},{6,2},{7,3},{8,12},{9,13},{10,... | collective-permute-start | bytes 663560 | tf_op jit(solution)/shard_map/ppermute | solution.py:911
  524.2 35.6 %collective-permute-start.12 = (bf16[648,768]{1,0:T(8,128)(2,1)}, bf16[648,768]{1,0:T(8,128)(2,1)S(1)}, u32[]{:S(2)}, u32[]{:S(2)}) collective-permute-start(bf16[648,768]{1,0:T(8,128)(2,1)} %get-tuple-element.113), channel_id=1, source_target_pairs={{0,16},{16,0},{1,17},{17,1},{2,18},{18,2},{3,19},{19,3},{4,20},{20... | collective-permute-start | bytes 2985992 | tf_op jit(solution)/shard_map/ppermute | solution.py:957
  524.8 35.1 %collective-permute-start.13 = (bf16[648,768]{1,0:T(8,128)(2,1)S(1)}, bf16[648,768]{1,0:T(8,128)(2,1)S(1)}, u32[]{:S(2)}, u32[]{:S(2)}) collective-permute-start(bf16[648,768]{1,0:T(8,128)(2,1)S(1)} %copy-done.8), channel_id=1, source_target_pairs={{16,1},{1,16},{18,3},{3,18},{20,5},{5,20},{22,7},{7,22},{24,9},{9,... | collective-permute-start | bytes 2985992 | tf_op jit(solution)/shard_map/ppermute | solution.py:958
  529.6 4.8 collective-permute-start.18
  532.1 28.8 %copy-start.9 = (bf16[648,768]{1,0:T(8,128)(2,1)S(1)}, bf16[648,768]{1,0:T(8,128)(2,1)}, u32[]{:S(2)}) copy-start(bf16[648,768]{1,0:T(8,128)(2,1)} %get-tuple-element.112) | copy-start | bytes 2985988
  532.1 6.8 %collective-permute-start.15 = (bf16[1,48,1152]{2,1,0:T(8,128)(2,1)S(1)}, bf16[1,48,1152]{2,1,0:T(8,128)(2,1)S(1)}, u32[]{:S(2)}, u32[]{:S(2)}) collective-permute-start(bf16[1,48,1152]{2,1,0:T(8,128)(2,1)S(1)} %constant_dynamic-slice_fusion.1), channel_id=1, source_target_pairs={{0,8},{1,9},{2,10},{3,11},{4,12},{5,13},{6,14},{7,15},{8,0},{9,1},... | collective-permute-start | bytes 331784 | tf_op jit(solution)/shard_map/ppermute | solution.py:911
  534.5 24.2 %collective-permute-start.19 = (bf16[48,1152]{1,0:T(8,128)(2,1)S(1)}, bf16[48,1152]{1,0:T(8,128)(2,1)S(1)}, u32[]{:S(2)}, u32[]{:S(2)}) collective-permute-start(bf16[48,1152]{1,0:T(8,128)(2,1)S(1)} %fusion.10), channel_id=1, source_target_pairs={{0,16},{16,0},{1,17},{17,1},{2,18},{18,2},{3,19},{19,3},{4,20},{20... | collective-permute-start | bytes 331784 | tf_op jit(solution)/shard_map/ppermute | solution.py:968
  538.9 20.9 %collective-permute-start.16 = (bf16[48,1152]{1,0:T(8,128)(2,1)S(1)}, bf16[48,1152]{1,0:T(8,128)(2,1)S(1)}, u32[]{:S(2)}, u32[]{:S(2)}) collective-permute-start(bf16[48,1152]{1,0:T(8,128)(2,1)S(1)} %fusion.9), channel_id=1, source_target_pairs={{0,16},{16,0},{1,17},{17,1},{2,18},{18,2},{3,19},{19,3},{4,20},{20... | collective-permute-start | bytes 331784 | tf_op jit(solution)/shard_map/ppermute | solution.py:968
Sparse Core Ops, SparseCore 0:
  10.9 52.9 all-gather.4
  66.1 87.1 all-gather.6
  246.1 118.3 reduce-scatter.1
  435.2 82.7 all-reduce.3

commit v2 on v1

--- a/solution.py
+++ b/solution.py
@@ -805,38 +805,39 @@
     return slot
 
 
-def qkv_weight_kernel(shards, normed_ref, dq_ref, dkv_ref, low_ref, high_ref, left):
+def qkv_weight_kernel(shards, normed_ref, dq_ref, dkv_ref, out_ref, left):
     step = pl.program_id(0)
     width = normed_ref.shape[-1]
     rows = width // shards
     half = width // 2
-    low_order, high_order = halving_orders(shards)
-
-    def keep(ref, order, start, grad):
+    orders = halving_orders(shards)
+
+    def keep(side, start, grad):
         for shard in range(shards):
-            ref[slot_of(shard, order), :, start : start + grad.shape[1]] = grad[
+            slot = slot_of(shard, orders[side][1:])
+            out_ref[shard % 2, side, slot, :, start : start + grad.shape[1]] = grad[
                 shard * rows : (shard + 1) * rows
             ]
 
     @pl.when(step == 0)
     def query_part():
         left[...] = normed_ref[...].T
-        keep(low_ref, low_order, 0, mul(left[...], dq_ref[...]).astype(BF16))
+        keep(0, 0, mul(left[...], dq_ref[...]).astype(BF16))
 
     @pl.when(step == 1)
     def key_part():
         grad = mul(left[...], dkv_ref[0]).astype(BF16)
-        keep(low_ref, low_order, width, grad[:, :half])
-        keep(high_ref, high_order, 0, grad[:, half:])
+        keep(0, width, grad[:, :half])
+        keep(1, 0, grad[:, half:])
 
     @pl.when(step == 2)
     def value_part():
-        keep(high_ref, high_order, half, mul(left[...], dkv_ref[0]).astype(BF16))
+        keep(1, half, mul(left[...], dkv_ref[0]).astype(BF16))
 
 
 def qkv_weight_grad(normed, dq, dkv, shards):
     count, width = normed.shape
-    half = (shards, width // shards, 3 * width // 2)
+    half = (2, 2, shards // 2, width // shards, 3 * width // 2)
     return pl.pallas_call(
         functools.partial(qkv_weight_kernel, shards),
         grid=(3,),
@@ -845,8 +846,8 @@
             whole(dq.shape),
             pl.BlockSpec((1, count, width), lambda s: (jnp.maximum(s - 1, 0), 0, 0)),
         ],
-        out_specs=[whole(half), whole(half)],
-        out_shape=[shaped(half, BF16), shaped(half, BF16)],
+        out_specs=whole(half),
+        out_shape=shaped(half, BF16),
         scratch_shapes=[pltpu.VMEM((width, count), BF16)],
         compiler_params=params(1),
         cost_estimate=LATE,
@@ -953,16 +954,17 @@
         kept = lax.dynamic_index_in_dim(values, 2 * side, 0, False)
         return jnp.stack([kept, got, middle_swap(values[1])])
 
-    def return_units(values, after=None):
-        got = lax.ppermute(values[1], "seq", swap_sides)
-        centre = lax.ppermute(values[2], ("seq", "fsdp"), swap_middle)
-        if after is not None:
-            got, centre, after = lax.optimization_barrier((got, centre, after))
+    def send_back(values):
+        return (
+            lax.ppermute(values[1], "seq", swap_sides),
+            lax.ppermute(values[2], ("seq", "fsdp"), swap_middle),
+        )
+
+    def in_place(values, got, centre):
         centre = jnp.where(stays, values[2], centre)
         first = jnp.where(side == 0, values[0], got)
         last = jnp.where(side == 0, got, values[0])
-        value = jnp.stack([first, centre, last])
-        return value if after is None else (value, after)
+        return jnp.stack([first, centre, last])
 
     def both(value):
         return value.astype(F32) + lax.ppermute(value, "seq", swap_sides).astype(F32)
@@ -1013,7 +1015,7 @@
         sums_two,
         sum_hidden,
     ) = feed(units, mixed, grads_up, full_pack, vectors, bias_hidden)
-    block_out = return_units(out)
+    out_got, out_centre = send_back(out)
 
     def flat(value):
         return value.reshape(row_count, value.shape[-1])
@@ -1033,12 +1035,11 @@
     dkv_got = lax.ppermute(dkv_other, "fsdp", swap_cores)
     dq, dkv, unused = mix_back(qkv, 0, 2, places_pair, mixed, grad_mixed, lse_pair, dq_one)
     dkv = dkv.at[:, 2].set((dkv_one.astype(F32) + dkv_got.astype(F32)).astype(BF16)[:, 0])
+    dq, dkv, out_got, out_centre = lax.optimization_barrier((dq, dkv, out_got, out_centre))
+    block_out = in_place(out, out_got, out_centre)
     sides = qkv_weight_grad(flat(normed), flat(dq), dkv.reshape(2, row_count, width), fsdp_size)
     orders = halving_orders(fsdp_size)
-    sides = [
-        halving_sum(value, "fsdp", fsdp_size, place, order[:1])
-        for value, order in zip(sides, orders)
-    ]
+    sides = halving_sum(sides, "fsdp", fsdp_size, place, [1])[0]
     sides, shard_pack, dq, dkv = lax.optimization_barrier((sides, shard_pack, dq, dkv))
     shard_pack = both(shard_pack)
     sides = [
@@ -1063,11 +1064,14 @@
         sum_hidden[0],
     ]
     packed = jnp.concatenate([value.reshape(fsdp_size, -1) for value in small_grads], 1)
-    packed = jnp.pad(packed, ((0, 0), (0, -packed.shape[1] % 1024)))
-    packed = packed.reshape(-1, 128)
-    mine = lax.psum_scatter(packed, "fsdp", scatter_dimension=0, tiled=True)
+    packed = jnp.pad(packed, ((0, 0), (0, -packed.shape[1] % 128)))
+    lines = packed.shape[1] // 128
+    everyone = lax.all_gather(packed.reshape(-1, 128), "fsdp", axis=0)
+    mine = lax.dynamic_slice_in_dim(everyone, place * lines, lines, 1).sum(0)
     shard_sides = [both(value) for value in shard_sides]
-    input_grad, shard_sides = return_units(grad_units, shard_sides)
+    got, centre = send_back(grad_units)
+    got, centre, shard_sides = lax.optimization_barrier((got, centre, shard_sides))
+    input_grad = in_place(grad_units, got, centre)
     mine = both(mine).reshape(-1)
     pieces = []
     for index in range(len(short)):

time: 578 us -> 502 us (0.87)
  waiting for transfers between devices: 161 us -> 68.3 us
  blocking collectives: 0 us -> 22.3 us
  starting transfers between devices: 42.3 us -> 30.6 us
  local copies, waits for them, and re-layouts: 26.4 us -> 32.6 us
    unnamed x5 -> x3, waiting for transfers between devices: 81.3 us -> 0.05 us
    all_gather x0 -> x1, blocking collectives: none -> 22.3 us  [fast_body(): everyone = lax.all_gather(packed.reshape(-1, 128), 'fsdp', axis=0)]
    ppermute x4, waiting for transfers between devices: 14.5 us -> 0.01 us  [the longest x2 0.01 us: send_back(): lax.ppermute(values[1], 'seq', swap_sides)]
    ppermute x4, starting transfers between devices: 19.3 us -> 9.08 us  [both(): lax.ppermute(value, 'seq', swap_sides).astype(F32)]
  transfers between devices with their start and end apart: 26 -> 24, of which waited for: 9 -> 8; matrix products, arithmetic and copies ran while one was open for 8% -> 9% of each run, Pallas kernels for 36% -> 41%
where the time goes in v2:
time: 502 us; the launch traced here: 493 us
  Pallas kernels  298 us (59%)
  waiting for transfers between devices  68.3 us (14%)
  local copies, waits for them, and re-layouts  32.6 us (6%)
  starting transfers between devices  30.6 us (6%)
  other arithmetic  26.4 us (5%)
  blocking collectives  22.3 us (4%)
  between operations  14.5 us (3%)
    pallas_call x2, Pallas kernels, mix_back(): pl.pallas_call(functools.partial(mix_back_kernel, unit_count), grid=(pair...  101 us
    pallas_call x2, Pallas kernels, mix(): pl.pallas_call(mix_kernel, grid=(pairs, unit_count), in_specs=[pl.BlockSp...  57.9 us
    pallas_call x1, Pallas kernels, feed(): pl.pallas_call(feed_kernel, grid=(count,), in_specs=[rows(width), rows(wi...  57.5 us
    pallas_call x1, Pallas kernels, weight_grads(): pl.pallas_call(functools.partial(weight_kernel, parts, shards), grid=(2 *...  35.3 us
    ppermute x2, waiting for transfers between devices, gather_units(): lax.ppermute(lax.dynamic_index_in_dim(values, 2 * (1 - side), 0, False),...  32.3 us
    ppermute x4, waiting for transfers between devices, both(): lax.ppermute(value, 'seq', swap_sides).astype(F32)  23 us
    all_gather x1, blocking collectives, fast_body(): everyone = lax.all_gather(packed.reshape(-1, 128), 'fsdp', axis=0)  22.3 us
    pallas_call x1, Pallas kernels, input_grads(): pl.pallas_call(input_kernel, grid=(count,), in_specs=[rows, rows, rows, p...  16.9 us
  transfers between devices with their start and end apart: 24, of which 8 were waited for; matrix products, arithmetic and copies ran while one was open for 9% of the time, Pallas kernels for 41%

profile of v2, /device:TPU:0, one launch (start us, length us, event | category | flops | bytes accessed | tf_op | source)
XLA Modules:
  0.0 493.0 jit_solution(5911099160475856438)
XLA Ops:
  8.4 1.7 head_pack.1
  10.3 3.0 constant_dynamic-slice_fusion.4
  13.2 1.6 collective-permute-start.1
  14.8 3.3 collective-permute-start
  18.1 1.3 select_bitcast_fusion.5
  19.4 32.3 %collective-permute-done = bf16[648,768]{1,0:T(8,128)(2,1)S(1)} collective-permute-done((bf16[648,768]{1,0:T(8,128)(2,1)S(1)}, bf16[648,768]{1,0:T(8,128)(2,1)S(1)}, u32[]{:S(2)}, u32[]{:S(2)}) %collective-permute-start) | collective-permute-done | bytes 995360 | tf_op jit(solution)/shard_map/ppermute | solution.py:951
  51.8 1.9 pad_maximum_fusion.x_ref
  54.8 9.1 %all-gather.5.cloned.1.call-done = bf16[896,2304]{1,0:T(8,128)(2,1)} async-done(((bf16[56,2304]{1,0:T(8,128)(2,1)}), bf16[896,2304]{1,0:T(8,128)(2,1)}) %all-gather.5.cloned.1.call-update) | async-done | bytes 4128784 | tf_op jit(solution)/shard_map/all_gather | solution.py:985
  65.3 14.5 %project.1 = (bf16[3,3,648,768]{3,2,1,0:T(8,128)(2,1)}, bf16[3,648,768]{2,1,0:T(8,128)(2,1)}, bf16[2,648,768]{2,1,0:T(8,128)(2,1)}) custom-call(bf16[3,648,768]{2,1,0:T(8,128)(2,1)} %pad_maximum_fusion.x_ref, bf16[16,56,2304]{2,1,0:T(8,128)(2,1)} %bitcast.108, f32[8,768]{1,0:T(8,128)} %reshape.164.vectors_ref), custom_call_target="tpu_custom_call" | custom-call | flops 6879707136 | bytes 18468864 | tf_op jit(solution)/shard_map/project/pallas_call | solution.py:363
  79.8 1.4 constant_dynamic-slice_fusion.3
  81.3 1.6 collective-permute-start.4
  82.9 2.2 collective-permute-start.3
  85.1 38.0 %mix.2 = (bf16[3,648,768]{2,1,0:T(8,128)(2,1)}, f32[2,6,8,648]{3,2,1,0:T(8,128)}) custom-call(bf16[3,3,648,768]{3,2,1,0:T(8,128)(2,1)} %get-tuple-element.78.q_ref.ka_ref.va_ref.kb_ref.vb_ref, bf16[3,3,648,768]{3,2,1,0:T(8,128)(2,1)} %get-tuple-element.78.q_ref.ka_ref.va_ref.kb_ref.vb_ref, ...), custom_call_target="tpu_custom_call" | custom-call | flops 20639121408 | bytes 7962624 | tf_op jit(solution)/shard_map/mix/pallas_call | solution.py:463
  124.7 1.3 select_bitcast_fusion.4
  126.0 3.1 pad_maximum_fusion.1.cot_ref
  129.2 1.3 copy-done.1
  130.5 19.9 %mix.3 = (bf16[3,648,768]{2,1,0:T(8,128)(2,1)}, f32[1,6,8,648]{3,2,1,0:T(8,128)}) custom-call(bf16[3,3,648,768]{3,2,1,0:T(8,128)(2,1)} %get-tuple-element.78.q_ref.ka_ref.va_ref.kb_ref.vb_ref, bf16[3,3,648,768]{3,2,1,0:T(8,128)(2,1)} %get-tuple-element.78.q_ref.ka_ref.va_ref.kb_ref.vb_ref, ...), custom_call_target="tpu_custom_call", output_to_operand_aliasing={{0}: (5, {})} | custom-call | flops 10319560704 | bytes 3981312 | tf_op jit(solution)/shard_map/mix/pallas_call | solution.py:463
  150.4 3.0 all-gather.7.cloned.1.call-done
  153.3 57.5 %feed.1 = (bf16[3,648,768]{2,1,0:T(8,128)(2,1)}, bf16[3,648,768]{2,1,0:T(8,128)(2,1)}, bf16[3,648,768]{2,1,0:T(8,128)(2,1)}, bf16[3,648,3072]{2,1,0:T(8,128)(2,1...) custom-call(bf16[3,648,768]{2,1,0:T(8,128)(2,1)} %pad_maximum_fusion.x_r, ...), custom_call_target="tpu_custom_call" | custom-call | flops 41278242816 | bytes 53747712 | tf_op jit(solution)/shard_map/feed/pallas_call | solution.py:693
  210.9 35.3 %weight_grads.1 = bf16[16,432,768]{2,1,0:T(8,128)(2,1)} custom-call(bf16[1944,768]{1,0:T(8,128)(2,1)} %bitcast.136, bf16[1944,3072]{1,0:T(8,128)(2,1)} %bitcast.135, bf16[1944,3072]{1,0:T(8,128)(2,1)} %bitcast.134, bf16[1944,768]{1,0:T(8,128)(2,1)} %bitcast.117, bf16[1944,768]{1,0:T(8,128)(2,1)} %bitcast.102, bf16[1944,768]{1,0:T(8,128)(2,1)} %bitcast.115), custom_call_target="tpu_custom_call" | custom-call | flops 20639121408 | bytes 35831808 | tf_op jit(solution)/shard_map/weight_grads/pallas_call | solution.py:772
  246.2 33.8 %mix_back.2 = (bf16[3,648,768]{2,1,0:T(8,128)(2,1)}, bf16[2,1,648,768]{3,2,1,0:T(8,128)(2,1)}, bf16[2,1,648,768]{3,2,1,0:T(8,128)(2,1)}) custom-call(bf16[3,3,648,768]{3,2,1,0:T(8,128)(2,1)} %get-tuple-element.78.q_ref.ka_ref.va_ref.kb_ref.vb_ref, bf16[3,3,648,768]{3,2,1,0:T(8,128)(2,1)} %get-tuple-element.78.q_ref.ka_ref.va_ref.kb_ref.vb_ref, ...), custom_call_target="tpu_custom_call" | custom-call | flops 1000 | bytes 1000 | tf_op jit(solution)/shard_map/mix_back/pallas_call | solution.py:579
  280.2 1.4 slice_bitcast_fusion
  281.6 1.5 collective-permute-start.6
  283.8 67.1 %mix_back.3 = (bf16[3,648,768]{2,1,0:T(8,128)(2,1)}, bf16[2,3,648,768]{3,2,1,0:T(8,128)(2,1)}, f32[8,128]{1,0:T(8,128)}) custom-call(bf16[3,3,648,768]{3,2,1,0:T(8,128)(2,1)} %get-tuple-element.78.q_ref.ka_ref.va_ref.kb_ref.vb_ref, bf16[3,3,648,768]{3,2,1,0:T(8,128)(2,1)} %get-tuple-element.78.q_ref.ka_ref.va_ref.kb_ref.vb_ref, ...), custom_call_target="tpu_custom_call", output_to_operand_aliasing={{0}: (8, {})} | custom-call | flops 1000 | bytes 1000 | tf_op jit(solution)/shard_map/mix_back/pallas_call | solution.py:579
  351.0 3.4 fusion.dkv_ref
  355.7 13.6 %qkv_weight_grad.1 = bf16[2,2,8,48,1152]{4,3,2,1,0:T(8,128)(2,1)} custom-call(bf16[1944,768]{1,0:T(8,128)(2,1)} %bitcast.116, bf16[1944,768]{1,0:T(8,128)(2,1)} %bitcast.100, bf16[2,1944,768]{2,1,0:T(8,128)(2,1)} %bitcast.101), custom_call_target="tpu_custom_call" | custom-call | flops 1000 | bytes 1000 | tf_op jit(solution)/shard_map/qkv_weight_grad/pallas_call | solution.py:841
  369.4 3.0 constant_dynamic-slice_fusion.2
  372.3 1.8 collective-permute-start.8
  374.1 1.5 slice_reduce_fusion
  376.4 1.5 slice_reduce_fusion.1
  378.0 1.4 reshape_squeeze.31
  379.3 1.4 reshape_squeeze.32
  380.7 1.3 reshape_squeeze.33
  382.0 1.4 reshape_squeeze.34
  383.4 3.1 fusion.1
  386.5 1.7 fusion.11
  390.4 1.7 fusion.2
  392.1 2.2 collective-permute-start.20
  395.7 16.9 %input_grads.1 = (bf16[648,768]{1,0:T(8,128)(2,1)}, bf16[648,768]{1,0:T(8,128)(2,1)}, bf16[648,768]{1,0:T(8,128)(2,1)}, f32[8,768]{1,0:T(8,128)}) custom-call(bf16[3,648,768]{2,1,0:T(8,128)(2,1)} %pad_maximum_fusion.x_ref, bf16[3,648,768]{2,1,0:T(8,128)(2,1)} %get-tuple-element.92.dx_ref, bf16[3,648,768]{2,1,0:T(8,128)(2,1)} %get-tuple-element.108.dq_ref, ...), custom_call_target="tpu_custom_call" | custom-call | flops 1000 | bytes 1000 | tf_op jit(solution)/shard_map/input_grads/pallas_call | solution.py:888
  415.0 1.6 collective-permute-start.16
  417.1 22.3 %all_gather.19 = f32[16,80,128]{2,1,0:T(8,128)S(1)} all-gather(f32[1,80,128]{2,1,0:T(8,128)S(1)} %all_gather_reshape.3), channel_id=1, replica_groups=mesh['seq'=2,'fsdp'=16] {'fsdp'}, dimensions={0}, use_global_device_ids=true | all-gather | bytes 696320 | tf_op jit(solution)/shard_map/all_gather | solution.py:1069
  439.9 1.8 collective-permute-start.13
  445.0 1.3 convert_add_fusion
  449.0 2.9 collective-permute-start.14
  452.1 3.1 collective-permute-start.18
  455.8 3.3 collective-permute-start.15
  459.1 20.8 %collective-permute-done.18 = bf16[48,1152]{1,0:T(8,128)(2,1)S(1)} collective-permute-done((bf16[48,1152]{1,0:T(8,128)(2,1)S(1)}, bf16[48,1152]{1,0:T(8,128)(2,1)S(1)}, u32[]{:S(2)}, u32[]{:S(2)}) %collective-permute-start.18) | collective-permute-done | bytes 110624 | tf_op jit(solution)/shard_map/ppermute | solution.py:970
  483.2 3.1 pad_maximum_fusion.2
  (133 shorter events, 25.3 us)
Async XLA Ops:
  7.2 56.7 %all-gather.5.cloned.1.call-start = ((), (), s32[]{:S(2)}) async-start(), calls=%async_computation.2 | async-start | bytes 4386816 | tf_op jit(solution)/shard_map/all_gather | solution.py:985
  10.2 143.1 %all-gather.7.cloned.1.call-start = ((), (), s32[]{:S(2)}) async-start(), calls=%async_computation.3 | async-start | bytes 11280384 | tf_op jit(solution)/shard_map/all_gather | solution.py:995
  13.2 4.9 collective-permute-start.1
  14.8 37.0 %collective-permute-start = (bf16[648,768]{1,0:T(8,128)(2,1)S(1)}, bf16[648,768]{1,0:T(8,128)(2,1)S(1)}, u32[]{:S(2)}, u32[]{:S(2)}) collective-permute-start(bf16[648,768]{1,0:T(8,128)(2,1)S(1)} %get-tuple-element.145), channel_id=1, source_target_pairs={{0,16},{16,0},{1,17},{17,1},{2,18},{18,2},{3,19},{19,3},{4,20},{20... | collective-permute-start | bytes 2985992 | tf_op jit(solution)/shard_map/ppermute | solution.py:951
  51.8 1.9 copy-start.19
  51.8 2.0 copy-start.20
  51.8 2.0 copy-start.21
  54.7 331.8 %reduce-scatter.2.cloned.1.call-start = ((), (), s32[]{:S(2)}) async-start(), calls=%async_computation.1 | async-start | bytes 11280384 | tf_op jit(solution)/shard_map/reduce_scatter | solution.py:1033
  65.3 14.5 %copy-start.2 = (bf16[3,648,768]{2,1,0:T(8,128)(2,1)S(1)}, bf16[3,648,768]{2,1,0:T(8,128)(2,1)}, u32[]{:S(2)}) copy-start(bf16[3,648,768]{2,1,0:T(8,128)(2,1)} %param.18) | copy-start | bytes 8957956
  81.3 43.4 %collective-permute-start.4 = (bf16[648,768]{1,0:T(8,128)(2,1)}, bf16[648,768]{1,0:T(8,128)(2,1)}, u32[]{:S(2)}, u32[]{:S(2)}) collective-permute-start(bf16[648,768]{1,0:T(8,128)(2,1)} %get-tuple-element.141), channel_id=1, source_target_pairs={{16,1},{1,16},{18,3},{3,18},{20,5},{5,20},{22,7},{7,22},{24,9},{9,... | collective-permute-start | bytes 2985992 | tf_op jit(solution)/shard_map/ppermute | solution.py:948
  82.9 43.1 %collective-permute-start.3 = (bf16[648,768]{1,0:T(8,128)(2,1)}, bf16[648,768]{1,0:T(8,128)(2,1)}, u32[]{:S(2)}, u32[]{:S(2)}) collective-permute-start(bf16[648,768]{1,0:T(8,128)(2,1)} %get-tuple-element.142), channel_id=1, source_target_pairs={{0,16},{16,0},{1,17},{17,1},{2,18},{18,2},{3,19},{19,3},{4,20},{20... | collective-permute-start | bytes 2985992 | tf_op jit(solution)/shard_map/ppermute | solution.py:951
  85.1 44.1 %collective-permute-start.2 = (bf16[2,648,768]{2,1,0:T(8,128)(2,1)}, bf16[2,648,768]{2,1,0:T(8,128)(2,1)S(1)}, u32[]{:S(2)}, u32[]{:S(2)}) collective-permute-start(bf16[2,648,768]{2,1,0:T(8,128)(2,1)} %get-tuple-element.80), channel_id=1, source_target_pairs={{0,1},{1,0},{2,3},{3,2},{4,5},{5,4},{6,7},{7,6},{8,9},{9,8},{10,11... | collective-permute-start | bytes 5971976 | tf_op jit(solution)/shard_map/ppermute | solution.py:1002
  129.2 1.3 copy-start.1
  246.2 34.1 %copy-start.3 = (bf16[3,648,768]{2,1,0:T(8,128)(2,1)S(1)}, bf16[3,648,768]{2,1,0:T(8,128)(2,1)}, u32[]{:S(2)}) copy-start(bf16[3,648,768]{2,1,0:T(8,128)(2,1)} %get-tuple-element.87) | copy-start | bytes 8957956
  280.0 71.0 %collective-permute-start.5 = (bf16[2,1,648,768]{3,2,1,0:T(8,128)(2,1)}, bf16[2,1,648,768]{3,2,1,0:T(8,128)(2,1)}, u32[]{:S(2)}, u32[]{:S(2)}) collective-permute-start(bf16[2,1,648,768]{3,2,1,0:T(8,128)(2,1)} %get-tuple-element.100), channel_id=1, source_target_pairs={{0,1},{1,0},{2,3},{3,2},{4,5},{5,4},{6,7},{7,6},{8,9},{9,8},{10,11... | collective-permute-start | bytes 5971976 | tf_op jit(solution)/shard_map/ppermute | solution.py:1035
  281.6 72.8 %collective-permute-start.6 = (bf16[648,768]{1,0:T(8,128)(2,1)}, bf16[648,768]{1,0:T(8,128)(2,1)S(1)}, u32[]{:S(2)}, u32[]{:S(2)}) collective-permute-start(bf16[648,768]{1,0:T(8,128)(2,1)} %get-tuple-element.139), channel_id=1, source_target_pairs={{0,16},{16,0},{1,17},{17,1},{2,18},{18,2},{3,19},{19,3},{4,20},{20... | collective-permute-start | bytes 2985992 | tf_op jit(solution)/shard_map/ppermute | solution.py:959
  283.1 71.3 %collective-permute-start.7 = (bf16[648,768]{1,0:T(8,128)(2,1)}, bf16[648,768]{1,0:T(8,128)(2,1)S(1)}, u32[]{:S(2)}, u32[]{:S(2)}) collective-permute-start(bf16[648,768]{1,0:T(8,128)(2,1)} %get-tuple-element.138), channel_id=1, source_target_pairs={{16,1},{1,16},{18,3},{3,18},{20,5},{5,20},{22,7},{7,22},{24,9},{9,... | collective-permute-start | bytes 2985992 | tf_op jit(solution)/shard_map/ppermute | solution.py:960
  283.8 67.2 %copy-start.12 = (bf16[2,1,648,768]{3,2,1,0:T(8,128)(2,1)S(1)}, bf16[2,1,648,768]{3,2,1,0:T(8,128)(2,1)}, u32[]{:S(2)}) copy-start(bf16[2,1,648,768]{3,2,1,0:T(8,128)(2,1)} %get-tuple-element.99) | copy-start | bytes 5971972
  354.4 1.3 copy-start.15
  369.3 14.0 %copy-start = (bf16[2,2,8,48,1152]{4,3,2,1,0:T(8,128)(2,1)S(1)}, bf16[2,2,8,48,1152]{4,3,2,1,0:T(8,128)(2,1)}, u32[]{:S(2)}) copy-start(bf16[2,2,8,48,1152]{4,3,2,1,0:T(8,128)(2,1)} %qkv_weight_grad.1) | copy-start | bytes 10616836
  372.3 11.1 %collective-permute-start.8 = (bf16[1,2,8,48,1152]{4,3,2,1,0:T(8,128)(2,1)}, bf16[1,2,8,48,1152]{4,3,2,1,0:T(8,128)(2,1)}, u32[]{:S(2)}, u32[]{:S(2)}) collective-permute-start(bf16[1,2,8,48,1152]{4,3,2,1,0:T(8,128)(2,1)} %constant_dynamic-slice_fusion.2), channel_id=1, source_target_pairs={{0,1},{1,0},{2,3},{3,2},{4,5},{5,4},{6,7},{7,6},{8,9},{9,8},{10,11... | collective-permute-start | bytes 5308424 | tf_op jit(solution)/shard_map/ppermute | solution.py:912
  386.5 3.9 copy-start.4
  386.5 3.9 copy-start.14
  388.2 6.1 %copy-start.8 = (bf16[1,8,48,1152]{3,2,1,0:T(8,128)(2,1)}, bf16[1,8,48,1152]{3,2,1,0:T(8,128)(2,1)S(1)}, u32[]{:S(2)}) copy-start(bf16[1,8,48,1152]{3,2,1,0:T(8,128)(2,1)S(1)} %get-tuple-element.149) | copy-start | bytes 2654212
  389.9 22.7 %collective-permute-start.10 = (bf16[4,48,1152]{2,1,0:T(8,128)(2,1)}, bf16[4,48,1152]{2,1,0:T(8,128)(2,1)}, u32[]{:S(2)}, u32[]{:S(2)}) collective-permute-start(bf16[4,48,1152]{2,1,0:T(8,128)(2,1)} %dynamic-slice_bitcast_fusion.2), channel_id=1, source_target_pairs={{0,4},{1,5},{2,6},{3,7},{4,0},{5,1},{6,2},{7,3},{8,12},{9,13},{10,... | collective-permute-start | bytes 1327112 | tf_op jit(solution)/shard_map/ppermute | solution.py:912
  392.1 52.9 %collective-permute-start.20 = (bf16[432,768]{1,0:T(8,128)(2,1)}, bf16[432,768]{1,0:T(8,128)(2,1)S(1)}, u32[]{:S(2)}, u32[]{:S(2)}) collective-permute-start(bf16[432,768]{1,0:T(8,128)(2,1)} %bitcast.36), channel_id=1, source_target_pairs={{0,16},{16,0},{1,17},{17,1},{2,18},{18,2},{3,19},{19,3},{4,20},{20... | collective-permute-start | bytes 1990664 | tf_op jit(solution)/shard_map/ppermute | solution.py:970
  395.1 17.5 %copy-start.11 = (bf16[1,8,48,1152]{3,2,1,0:T(8,128)(2,1)S(1)}, bf16[1,8,48,1152]{3,2,1,0:T(8,128)(2,1)}, u32[]{:S(2)}) copy-start(bf16[1,8,48,1152]{3,2,1,0:T(8,128)(2,1)} %copy-done.10) | copy-start | bytes 2654212
  395.1 18.7 %copy-start.9 = (bf16[1,8,48,1152]{3,2,1,0:T(8,128)(2,1)S(1)}, bf16[1,8,48,1152]{3,2,1,0:T(8,128)(2,1)}, u32[]{:S(2)}) copy-start(bf16[1,8,48,1152]{3,2,1,0:T(8,128)(2,1)} %copy-done.8) | copy-start | bytes 2654212
  395.1 18.7 %collective-permute-start.9 = (bf16[4,48,1152]{2,1,0:T(8,128)(2,1)}, bf16[4,48,1152]{2,1,0:T(8,128)(2,1)}, u32[]{:S(2)}, u32[]{:S(2)}) collective-permute-start(bf16[4,48,1152]{2,1,0:T(8,128)(2,1)} %dynamic-slice_bitcast_fusion.3), channel_id=1, source_target_pairs={{0,2},{1,3},{2,0},{3,1},{4,6},{5,7},{6,4},{7,5},{8,10},{9,11},{10,... | collective-permute-start | bytes 1327112 | tf_op jit(solution)/shard_map/ppermute | solution.py:912
  412.5 4.0 copy-start.26
  412.5 4.4 copy-start.22
  412.6 4.4 copy-start.23
  412.6 4.4 copy-start.24
  412.6 4.4 copy-start.25
  412.6 30.5 %copy-start.16 = (bf16[648,768]{1,0:T(8,128)(2,1)S(1)}, bf16[648,768]{1,0:T(8,128)(2,1)}, u32[]{:S(2)}) copy-start(bf16[648,768]{1,0:T(8,128)(2,1)} %get-tuple-element.116) | copy-start | bytes 2985988
  415.0 32.0 %collective-permute-start.16 = (bf16[2,48,1152]{2,1,0:T(8,128)(2,1)S(1)}, bf16[2,48,1152]{2,1,0:T(8,128)(2,1)S(1)}, u32[]{:S(2)}, u32[]{:S(2)}) collective-permute-start(bf16[2,48,1152]{2,1,0:T(8,128)(2,1)S(1)} %dynamic-slice_bitcast_fusion.4), channel_id=1, source_target_pairs={{0,8},{1,9},{2,10},{3,11},{4,12},{5,13},{6,14},{7,15},{8,0},{9,1},... | collective-permute-start | bytes 663560 | tf_op jit(solution)/shard_map/ppermute | solution.py:912
  439.4 3.7 collective-permute-start.19
  439.9 8.1 %collective-permute-start.13 = (bf16[2,48,1152]{2,1,0:T(8,128)(2,1)S(1)}, bf16[2,48,1152]{2,1,0:T(8,128)(2,1)S(1)}, u32[]{:S(2)}, u32[]{:S(2)}) collective-permute-start(bf16[2,48,1152]{2,1,0:T(8,128)(2,1)S(1)} %dynamic-slice_bitcast_fusion.5), channel_id=1, source_target_pairs={{0,4},{1,5},{2,6},{3,7},{4,0},{5,1},{6,2},{7,3},{8,12},{9,13},{10,... | collective-permute-start | bytes 663560 | tf_op jit(solution)/shard_map/ppermute | solution.py:912
  441.7 39.4 %collective-permute-start.11 = (bf16[648,768]{1,0:T(8,128)(2,1)}, bf16[648,768]{1,0:T(8,128)(2,1)S(1)}, u32[]{:S(2)}, u32[]{:S(2)}) collective-permute-start(bf16[648,768]{1,0:T(8,128)(2,1)} %get-tuple-element.115), channel_id=1, source_target_pairs={{0,16},{16,0},{1,17},{17,1},{2,18},{18,2},{3,19},{19,3},{4,20},{20... | collective-permute-start | bytes 2985992 | tf_op jit(solution)/shard_map/ppermute | solution.py:959
  443.1 38.0 %collective-permute-start.12 = (bf16[648,768]{1,0:T(8,128)(2,1)S(1)}, bf16[648,768]{1,0:T(8,128)(2,1)S(1)}, u32[]{:S(2)}, u32[]{:S(2)}) collective-permute-start(bf16[648,768]{1,0:T(8,128)(2,1)S(1)} %copy-done.16), channel_id=1, source_target_pairs={{16,1},{1,16},{18,3},{3,18},{20,5},{5,20},{22,7},{7,22},{24,9},{9,... | collective-permute-start | bytes 2985992 | tf_op jit(solution)/shard_map/ppermute | solution.py:960
  447.1 5.0 %collective-permute-start.17 = (bf16[1,48,1152]{2,1,0:T(8,128)(2,1)S(1)}, bf16[1,48,1152]{2,1,0:T(8,128)(2,1)S(1)}, u32[]{:S(2)}, u32[]{:S(2)}) collective-permute-start(bf16[1,48,1152]{2,1,0:T(8,128)(2,1)S(1)} %constant_dynamic-slice_fusion), channel_id=1, source_target_pairs={{0,2},{1,3},{2,0},{3,1},{4,6},{5,7},{6,4},{7,5},{8,10},{9,11},{10,... | collective-permute-start | bytes 331784 | tf_op jit(solution)/shard_map/ppermute | solution.py:912
  449.0 33.1 %copy-start.17 = (bf16[648,768]{1,0:T(8,128)(2,1)S(1)}, bf16[648,768]{1,0:T(8,128)(2,1)}, u32[]{:S(2)}) copy-start(bf16[648,768]{1,0:T(8,128)(2,1)} %get-tuple-element.114) | copy-start | bytes 2985988
  449.0 6.8 %collective-permute-start.14 = (bf16[1,48,1152]{2,1,0:T(8,128)(2,1)S(1)}, bf16[1,48,1152]{2,1,0:T(8,128)(2,1)S(1)}, u32[]{:S(2)}, u32[]{:S(2)}) collective-permute-start(bf16[1,48,1152]{2,1,0:T(8,128)(2,1)S(1)} %constant_dynamic-slice_fusion.1), channel_id=1, source_target_pairs={{0,8},{1,9},{2,10},{3,11},{4,12},{5,13},{6,14},{7,15},{8,0},{9,1},... | collective-permute-start | bytes 331784 | tf_op jit(solution)/shard_map/ppermute | solution.py:912
  452.1 27.8 %collective-permute-start.18 = (bf16[48,1152]{1,0:T(8,128)(2,1)S(1)}, bf16[48,1152]{1,0:T(8,128)(2,1)S(1)}, u32[]{:S(2)}, u32[]{:S(2)}) collective-permute-start(bf16[48,1152]{1,0:T(8,128)(2,1)S(1)} %fusion.9), channel_id=1, source_target_pairs={{0,16},{16,0},{1,17},{17,1},{2,18},{18,2},{3,19},{19,3},{4,20},{20... | collective-permute-start | bytes 331784 | tf_op jit(solution)/shard_map/ppermute | solution.py:970
  455.8 25.2 %collective-permute-start.15 = (bf16[48,1152]{1,0:T(8,128)(2,1)S(1)}, bf16[48,1152]{1,0:T(8,128)(2,1)S(1)}, u32[]{:S(2)}, u32[]{:S(2)}) collective-permute-start(bf16[48,1152]{1,0:T(8,128)(2,1)S(1)} %fusion.8), channel_id=1, source_target_pairs={{0,16},{16,0},{1,17},{17,1},{2,18},{18,2},{3,19},{19,3},{4,20},{20... | collective-permute-start | bytes 331784 | tf_op jit(solution)/shard_map/ppermute | solution.py:970
  481.2 1.4 copy-start.5
  481.2 1.7 copy-start.6
  481.2 1.9 copy-start.7
  (3 other events, 2.8 us)
Sparse Core Ops, SparseCore 0:
  10.9 52.9 all-gather.4
  66.1 87.1 all-gather.6
  246.3 118.3 reduce-scatter.1

commit v3 on v2

--- a/solution.py
+++ b/solution.py
@@ -1037,19 +1037,16 @@
     dkv = dkv.at[:, 2].set((dkv_one.astype(F32) + dkv_got.astype(F32)).astype(BF16)[:, 0])
     dq, dkv, out_got, out_centre = lax.optimization_barrier((dq, dkv, out_got, out_centre))
     block_out = in_place(out, out_got, out_centre)
+    *grad_units, sums_one = input_grads(units, grad_attended, dq, dkv, full_head, vectors)
+    got, centre = send_back(grad_units)
+    dq, dkv, sums_one = lax.optimization_barrier((dq, dkv, sums_one))
     sides = qkv_weight_grad(flat(normed), flat(dq), dkv.reshape(2, row_count, width), fsdp_size)
     orders = halving_orders(fsdp_size)
     sides = halving_sum(sides, "fsdp", fsdp_size, place, [1])[0]
-    sides, shard_pack, dq, dkv = lax.optimization_barrier((sides, shard_pack, dq, dkv))
+    sides, shard_pack = lax.optimization_barrier((sides, shard_pack))
     shard_pack = both(shard_pack)
-    sides = [
-        halving_sum(value, "fsdp", fsdp_size, place, order[1:2])
-        for value, order in zip(sides, orders)
-    ]
-    *grad_units, sums_one = input_grads(units, grad_attended, dq, dkv, full_head, vectors)
-    sides, grad_units, sums_one = lax.optimization_barrier((sides, grad_units, sums_one))
     shard_sides = [
-        halving_sum(value, "fsdp", fsdp_size, place, order[2:])[0]
+        halving_sum(value, "fsdp", fsdp_size, place, order[1:])[0]
         for value, order in zip(sides, orders)
     ]
     small_grads = [
@@ -1064,13 +1061,14 @@
         sum_hidden[0],
     ]
     packed = jnp.concatenate([value.reshape(fsdp_size, -1) for value in small_grads], 1)
-    packed = jnp.pad(packed, ((0, 0), (0, -packed.shape[1] % 128)))
+    packed = jnp.pad(packed, ((0, 0), (0, -packed.shape[1] % 1280)))
     lines = packed.shape[1] // 128
     everyone = lax.all_gather(packed.reshape(-1, 128), "fsdp", axis=0)
+    shard_sides = [both(value) for value in shard_sides]
+    got, centre, shard_sides, everyone = lax.optimization_barrier(
+        (got, centre, shard_sides, everyone)
+    )
     mine = lax.dynamic_slice_in_dim(everyone, place * lines, lines, 1).sum(0)
-    shard_sides = [both(value) for value in shard_sides]
-    got, centre = send_back(grad_units)
-    got, centre, shard_sides = lax.optimization_barrier((got, centre, shard_sides))
     input_grad = in_place(grad_units, got, centre)
     mine = both(mine).reshape(-1)
     pieces = []

time: 502 us -> 511 us (1.018)
  blocking collectives: 22.3 us -> 0 us
  waiting for transfers between devices: 68.3 us -> 85.1 us
  Pallas kernels: 298 us -> 310 us
  local copies, waits for them, and re-layouts: 32.6 us -> 39.3 us
    ppermute x7, waiting for transfers between devices: 0.79 us -> 29.6 us  [halving_sum(): lax.ppermute(lax.dynamic_index_in_dim(halves, 1 - bit, 0, False), axis, p...]
    all_gather x1 -> x0, blocking collectives: 22.3 us -> none  [fast_body(): everyone = lax.all_gather(packed.reshape(-1, 128), 'fsdp', axis=0)]
    ppermute x4, waiting for transfers between devices: 23 us -> 10.9 us  [both(): lax.ppermute(value, 'seq', swap_sides).astype(F32)]
    pallas_call x1, Pallas kernels: 35.3 us -> 46.9 us  [weight_grads(): pl.pallas_call(functools.partial(weight_kernel, parts, shards), grid=(2 *...]
    another operation x9, local copies, waits for them, and re-layouts: 6.48 us -> 11.6 us  [fast_body(): value.reshape(fsdp_size, -1)]
  transfers between devices with their start and end apart: 24 -> 25, of which waited for: 8 -> 9; matrix products, arithmetic and copies ran while one was open for 9% -> 12% of each run, Pallas kernels for 41% -> 41%
where the time goes in v3:
time: 511 us; the launch traced here: 503 us
  Pallas kernels  310 us (61%)
  waiting for transfers between devices  85.1 us (17%)
  local copies, waits for them, and re-layouts  39.3 us (8%)
  starting transfers between devices  27.9 us (5%)
  other arithmetic  25.6 us (5%)
  between operations  14.4 us (3%)
    pallas_call x2, Pallas kernels, mix_back(): pl.pallas_call(functools.partial(mix_back_kernel, unit_count), grid=(pair...  101 us
    pallas_call x2, Pallas kernels, mix(): pl.pallas_call(mix_kernel, grid=(pairs, unit_count), in_specs=[pl.BlockSp...  57.9 us
    pallas_call x1, Pallas kernels, feed(): pl.pallas_call(feed_kernel, grid=(count,), in_specs=[rows(width), rows(wi...  57.3 us
    pallas_call x1, Pallas kernels, weight_grads(): pl.pallas_call(functools.partial(weight_kernel, parts, shards), grid=(2 *...  46.9 us
    ppermute x2, waiting for transfers between devices, gather_units(): lax.ppermute(lax.dynamic_index_in_dim(values, 2 * (1 - side), 0, False),...  32.3 us
    ppermute x7, waiting for transfers between devices, halving_sum(): lax.ppermute(lax.dynamic_index_in_dim(halves, 1 - bit, 0, False), axis, p...  29.6 us
    pallas_call x1, Pallas kernels, input_grads(): pl.pallas_call(input_kernel, grid=(count,), in_specs=[rows, rows, rows, p...  17.6 us
    pallas_call x1, Pallas kernels, project(): pl.pallas_call(project_kernel, grid=(count,), in_specs=[pl.BlockSpec((1,...  14.5 us
  transfers between devices with their start and end apart: 25, of which 9 were waited for; matrix products, arithmetic and copies ran while one was open for 12% of the time, Pallas kernels for 41%

profile of v3, /device:TPU:0, one launch (start us, length us, event | category | flops | bytes accessed | tf_op | source)
XLA Modules:
  0.0 502.6 jit_solution(701373611889043588)
XLA Ops:
  8.4 1.7 head_pack.1
  10.3 3.0 constant_dynamic-slice_fusion.4
  13.2 1.6 collective-permute-start.1
  14.8 3.3 collective-permute-start
  19.4 32.3 %collective-permute-done = bf16[648,768]{1,0:T(8,128)(2,1)S(1)} collective-permute-done((bf16[648,768]{1,0:T(8,128)(2,1)S(1)}, bf16[648,768]{1,0:T(8,128)(2,1)S(1)}, u32[]{:S(2)}, u32[]{:S(2)}) %collective-permute-start) | collective-permute-done | bytes 995360 | tf_op jit(solution)/shard_map/ppermute | solution.py:951
  51.8 1.9 pad_maximum_fusion.x_ref
  54.8 9.1 %all-gather.8.cloned.1.call-done = bf16[896,2304]{1,0:T(8,128)(2,1)} async-done(((bf16[56,2304]{1,0:T(8,128)(2,1)}), bf16[896,2304]{1,0:T(8,128)(2,1)}) %all-gather.8.cloned.1.call-update) | async-done | bytes 4128784 | tf_op jit(solution)/shard_map/all_gather | solution.py:985
  65.3 14.5 %project.1 = (bf16[3,3,648,768]{3,2,1,0:T(8,128)(2,1)}, bf16[3,648,768]{2,1,0:T(8,128)(2,1)}, bf16[2,648,768]{2,1,0:T(8,128)(2,1)}) custom-call(bf16[3,648,768]{2,1,0:T(8,128)(2,1)} %pad_maximum_fusion.x_ref, bf16[16,56,2304]{2,1,0:T(8,128)(2,1)} %bitcast.107, f32[8,768]{1,0:T(8,128)} %reshape.164.vectors_ref), custom_call_target="tpu_custom_call" | custom-call | flops 6879707136 | bytes 18468864 | tf_op jit(solution)/shard_map/project/pallas_call | solution.py:363
  79.8 1.4 constant_dynamic-slice_fusion.3
  81.3 1.6 collective-permute-start.4
  82.9 2.2 collective-permute-start.3
  85.1 38.0 %mix.2 = (bf16[3,648,768]{2,1,0:T(8,128)(2,1)}, f32[2,6,8,648]{3,2,1,0:T(8,128)}) custom-call(bf16[3,3,648,768]{3,2,1,0:T(8,128)(2,1)} %get-tuple-element.74.q_ref.ka_ref.va_ref.kb_ref.vb_ref, bf16[3,3,648,768]{3,2,1,0:T(8,128)(2,1)} %get-tuple-element.74.q_ref.ka_ref.va_ref.kb_ref.vb_ref, ...), custom_call_target="tpu_custom_call" | custom-call | flops 20639121408 | bytes 7962624 | tf_op jit(solution)/shard_map/mix/pallas_call | solution.py:463
  126.1 3.1 pad_maximum_fusion.1.cot_ref
  130.5 19.9 %mix.3 = (bf16[3,648,768]{2,1,0:T(8,128)(2,1)}, f32[1,6,8,648]{3,2,1,0:T(8,128)}) custom-call(bf16[3,3,648,768]{3,2,1,0:T(8,128)(2,1)} %get-tuple-element.74.q_ref.ka_ref.va_ref.kb_ref.vb_ref, bf16[3,3,648,768]{3,2,1,0:T(8,128)(2,1)} %get-tuple-element.74.q_ref.ka_ref.va_ref.kb_ref.vb_ref, ...), custom_call_target="tpu_custom_call", output_to_operand_aliasing={{0}: (5, {})} | custom-call | flops 10319560704 | bytes 3981312 | tf_op jit(solution)/shard_map/mix/pallas_call | solution.py:463
  150.3 3.0 all-gather.10.cloned.1.call-done
  153.3 57.3 %feed.1 = (bf16[3,648,768]{2,1,0:T(8,128)(2,1)}, bf16[3,648,768]{2,1,0:T(8,128)(2,1)}, bf16[3,648,768]{2,1,0:T(8,128)(2,1)}, bf16[3,648,3072]{2,1,0:T(8,128)(2,1...) custom-call(bf16[3,648,768]{2,1,0:T(8,128)(2,1)} %pad_maximum_fusion.x_r, ...), custom_call_target="tpu_custom_call" | custom-call | flops 41278242816 | bytes 53747712 | tf_op jit(solution)/shard_map/feed/pallas_call | solution.py:693
  210.7 46.9 %weight_grads.1 = bf16[16,432,768]{2,1,0:T(8,128)(2,1)} custom-call(bf16[1944,768]{1,0:T(8,128)(2,1)} %bitcast.136, bf16[1944,3072]{1,0:T(8,128)(2,1)} %bitcast.135, bf16[1944,3072]{1,0:T(8,128)(2,1)} %bitcast.134, bf16[1944,768]{1,0:T(8,128)(2,1)} %bitcast.116, bf16[1944,768]{1,0:T(8,128)(2,1)} %bitcast.101, bf16[1944,768]{1,0:T(8,128)(2,1)} %bitcast.115), custom_call_target="tpu_custom_call" | custom-call | flops 20639121408 | bytes 35831808 | tf_op jit(solution)/shard_map/weight_grads/pallas_call | solution.py:772
  257.6 33.8 %mix_back.2 = (bf16[3,648,768]{2,1,0:T(8,128)(2,1)}, bf16[2,1,648,768]{3,2,1,0:T(8,128)(2,1)}, bf16[2,1,648,768]{3,2,1,0:T(8,128)(2,1)}) custom-call(bf16[3,3,648,768]{3,2,1,0:T(8,128)(2,1)} %get-tuple-element.74.q_ref.ka_ref.va_ref.kb_ref.vb_ref, bf16[3,3,648,768]{3,2,1,0:T(8,128)(2,1)} %get-tuple-element.74.q_ref.ka_ref.va_ref.kb_ref.vb_ref, ...), custom_call_target="tpu_custom_call" | custom-call | flops 1000 | bytes 1000 | tf_op jit(solution)/shard_map/mix_back/pallas_call | solution.py:579
  291.6 1.5 slice_bitcast_fusion
  293.1 1.5 collective-permute-start.6
  295.3 67.1 %mix_back.3 = (bf16[3,648,768]{2,1,0:T(8,128)(2,1)}, bf16[2,3,648,768]{3,2,1,0:T(8,128)(2,1)}, f32[8,128]{1,0:T(8,128)}) custom-call(bf16[3,3,648,768]{3,2,1,0:T(8,128)(2,1)} %get-tuple-element.74.q_ref.ka_ref.va_ref.kb_ref.vb_ref, bf16[3,3,648,768]{3,2,1,0:T(8,128)(2,1)} %get-tuple-element.74.q_ref.ka_ref.va_ref.kb_ref.vb_ref, ...), custom_call_target="tpu_custom_call", output_to_operand_aliasing={{0}: (8, {})} | custom-call | flops 1000 | bytes 1000 | tf_op jit(solution)/shard_map/mix_back/pallas_call | solution.py:579
  362.4 3.4 fusion.dkv_ref
  365.9 17.6 %input_grads.1 = (bf16[648,768]{1,0:T(8,128)(2,1)}, bf16[648,768]{1,0:T(8,128)(2,1)}, bf16[648,768]{1,0:T(8,128)(2,1)}, f32[8,768]{1,0:T(8,128)}) custom-call(bf16[3,648,768]{2,1,0:T(8,128)(2,1)} %pad_maximum_fusion.x_ref, bf16[3,648,768]{2,1,0:T(8,128)(2,1)} %get-tuple-element.88.dx_ref, bf16[3,648,768]{2,1,0:T(8,128)(2,1)} %get-tuple-element.106.dq_ref, ...), custom_call_target="tpu_custom_call" | custom-call | flops 1000 | bytes 1000 | tf_op jit(solution)/shard_map/input_grads/pallas_call | solution.py:888
  383.6 13.6 %qkv_weight_grad.1 = bf16[2,2,8,48,1152]{4,3,2,1,0:T(8,128)(2,1)} custom-call(bf16[1944,768]{1,0:T(8,128)(2,1)} %bitcast.114, bf16[1944,768]{1,0:T(8,128)(2,1)} %bitcast.99, bf16[2,1944,768]{2,1,0:T(8,128)(2,1)} %bitcast.100), custom_call_target="tpu_custom_call" | custom-call | flops 1000 | bytes 1000 | tf_op jit(solution)/shard_map/qkv_weight_grad/pallas_call | solution.py:841
  397.1 3.0 constant_dynamic-slice_fusion.2
  400.1 1.8 collective-permute-start.10
  401.9 1.5 slice_reduce_fusion
  404.2 1.5 slice_reduce_fusion.1
  411.2 1.5 slice_reduce_fusion.5
  412.7 1.4 reshape_squeeze.27
  418.1 1.5 concatenate.15
  419.7 1.4 pad.6
  421.1 1.5 all_gather_reshape.3
  423.6 1.7 collective-permute-start.9
  425.3 3.1 fusion.1
  428.4 1.7 fusion.11
  431.0 1.8 fusion.2
  432.8 3.3 collective-permute-start.20
  436.8 8.8 %collective-permute-done.15 = bf16[4,48,1152]{2,1,0:T(8,128)(2,1)S(1)} collective-permute-done((bf16[4,48,1152]{2,1,0:T(8,128)(2,1)S(1)}, bf16[4,48,1152]{2,1,0:T(8,128)(2,1)S(1)}, u32[]{:S(2)}, u32[]{:S(2)}) %collective-permute-start.15) | collective-permute-done | bytes 442400 | tf_op jit(solution)/shard_map/ppermute | solution.py:912
  445.7 1.6 collective-permute-start.16
  448.8 14.9 %collective-permute-done.16 = bf16[2,48,1152]{2,1,0:T(8,128)(2,1)S(1)} collective-permute-done((bf16[2,48,1152]{2,1,0:T(8,128)(2,1)S(1)}, bf16[2,48,1152]{2,1,0:T(8,128)(2,1)S(1)}, u32[]{:S(2)}, u32[]{:S(2)}) %collective-permute-start.16) | collective-permute-done | bytes 221216 | tf_op jit(solution)/shard_map/ppermute | solution.py:912
  464.1 7.5 %collective-permute-done.20 = bf16[432,768]{1,0:T(8,128)(2,1)S(1)} collective-permute-done((bf16[432,768]{1,0:T(8,128)(2,1)S(1)}, bf16[432,768]{1,0:T(8,128)(2,1)S(1)}, u32[]{:S(2)}, u32[]{:S(2)}) %collective-permute-start.20) | collective-permute-done | bytes 663584 | tf_op jit(solution)/shard_map/ppermute | solution.py:970
  474.3 1.5 collective-permute-start.13
  475.9 5.7 %collective-permute-done.13 = bf16[1,48,1152]{2,1,0:T(8,128)(2,1)S(1)} collective-permute-done((bf16[1,48,1152]{2,1,0:T(8,128)(2,1)S(1)}, bf16[1,48,1152]{2,1,0:T(8,128)(2,1)S(1)}, u32[]{:S(2)}, u32[]{:S(2)}) %collective-permute-start.13) | collective-permute-done | bytes 110624 | tf_op jit(solution)/shard_map/ppermute | solution.py:912
  483.0 3.4 collective-permute-done.14
  487.5 1.7 collective-permute-start.19
  489.3 1.5 select_bitcast_fusion.2
  490.8 3.1 pad_maximum_fusion.2
  (120 shorter events, 32.5 us)
Async XLA Ops:
  7.2 56.7 %all-gather.8.cloned.1.call-start = ((), (), s32[]{:S(2)}) async-start(), calls=%async_computation.3 | async-start | bytes 4386816 | tf_op jit(solution)/shard_map/all_gather | solution.py:985
  10.2 143.1 %all-gather.10.cloned.1.call-start = ((), (), s32[]{:S(2)}) async-start(), calls=%async_computation.4 | async-start | bytes 11280384 | tf_op jit(solution)/shard_map/all_gather | solution.py:995
  13.2 4.9 collective-permute-start.1
  14.8 36.9 %collective-permute-start = (bf16[648,768]{1,0:T(8,128)(2,1)S(1)}, bf16[648,768]{1,0:T(8,128)(2,1)S(1)}, u32[]{:S(2)}, u32[]{:S(2)}) collective-permute-start(bf16[648,768]{1,0:T(8,128)(2,1)S(1)} %get-tuple-element.137), channel_id=1, source_target_pairs={{0,16},{16,0},{1,17},{17,1},{2,18},{18,2},{3,19},{19,3},{4,20},{20... | collective-permute-start | bytes 2985992 | tf_op jit(solution)/shard_map/ppermute | solution.py:951
  51.8 1.9 copy-start.16
  51.8 2.0 copy-start.17
  51.8 2.0 copy-start.18
  53.9 0.9 copy-start.14
  54.8 373.6 %reduce-scatter.2.cloned.1.call-start = ((), (), s32[]{:S(2)}) async-start(), calls=%async_computation.1 | async-start | bytes 11280384 | tf_op jit(solution)/shard_map/reduce_scatter | solution.py:1033
  65.3 14.5 %copy-start.2 = (bf16[3,648,768]{2,1,0:T(8,128)(2,1)S(1)}, bf16[3,648,768]{2,1,0:T(8,128)(2,1)}, u32[]{:S(2)}) copy-start(bf16[3,648,768]{2,1,0:T(8,128)(2,1)} %param.18) | copy-start | bytes 8957956
  81.3 43.5 %collective-permute-start.4 = (bf16[648,768]{1,0:T(8,128)(2,1)}, bf16[648,768]{1,0:T(8,128)(2,1)}, u32[]{:S(2)}, u32[]{:S(2)}) collective-permute-start(bf16[648,768]{1,0:T(8,128)(2,1)} %get-tuple-element.133), channel_id=1, source_target_pairs={{16,1},{1,16},{18,3},{3,18},{20,5},{5,20},{22,7},{7,22},{24,9},{9,... | collective-permute-start | bytes 2985992 | tf_op jit(solution)/shard_map/ppermute | solution.py:948
  82.9 43.2 %collective-permute-start.3 = (bf16[648,768]{1,0:T(8,128)(2,1)}, bf16[648,768]{1,0:T(8,128)(2,1)}, u32[]{:S(2)}, u32[]{:S(2)}) collective-permute-start(bf16[648,768]{1,0:T(8,128)(2,1)} %get-tuple-element.134), channel_id=1, source_target_pairs={{0,16},{16,0},{1,17},{17,1},{2,18},{18,2},{3,19},{19,3},{4,20},{20... | collective-permute-start | bytes 2985992 | tf_op jit(solution)/shard_map/ppermute | solution.py:951
  85.1 44.1 %collective-permute-start.2 = (bf16[2,648,768]{2,1,0:T(8,128)(2,1)}, bf16[2,648,768]{2,1,0:T(8,128)(2,1)S(1)}, u32[]{:S(2)}, u32[]{:S(2)}) collective-permute-start(bf16[2,648,768]{2,1,0:T(8,128)(2,1)} %get-tuple-element.76), channel_id=1, source_target_pairs={{0,1},{1,0},{2,3},{3,2},{4,5},{5,4},{6,7},{7,6},{8,9},{9,8},{10,11... | collective-permute-start | bytes 5971976 | tf_op jit(solution)/shard_map/ppermute | solution.py:1002
  129.2 1.3 copy-start.1
  257.5 229.0 %all-gather.6.cloned.1.call-start = ((), (), s32[]{:S(2)}) async-start(), calls=%async_computation.2 | async-start | bytes 1392640 | tf_op jit(solution)/shard_map/all_gather | solution.py:1066
  257.6 34.0 %copy-start.3 = (bf16[3,648,768]{2,1,0:T(8,128)(2,1)S(1)}, bf16[3,648,768]{2,1,0:T(8,128)(2,1)}, u32[]{:S(2)}) copy-start(bf16[3,648,768]{2,1,0:T(8,128)(2,1)} %get-tuple-element.83) | copy-start | bytes 8957956
  291.4 71.1 %collective-permute-start.5 = (bf16[2,1,648,768]{3,2,1,0:T(8,128)(2,1)}, bf16[2,1,648,768]{3,2,1,0:T(8,128)(2,1)}, u32[]{:S(2)}, u32[]{:S(2)}) collective-permute-start(bf16[2,1,648,768]{3,2,1,0:T(8,128)(2,1)} %get-tuple-element.96), channel_id=1, source_target_pairs={{0,1},{1,0},{2,3},{3,2},{4,5},{5,4},{6,7},{7,6},{8,9},{9,8},{10,11... | collective-permute-start | bytes 5971976 | tf_op jit(solution)/shard_map/ppermute | solution.py:1035
  293.1 72.8 %collective-permute-start.6 = (bf16[648,768]{1,0:T(8,128)(2,1)}, bf16[648,768]{1,0:T(8,128)(2,1)S(1)}, u32[]{:S(2)}, u32[]{:S(2)}) collective-permute-start(bf16[648,768]{1,0:T(8,128)(2,1)} %get-tuple-element.131), channel_id=1, source_target_pairs={{0,16},{16,0},{1,17},{17,1},{2,18},{18,2},{3,19},{19,3},{4,20},{20... | collective-permute-start | bytes 2985992 | tf_op jit(solution)/shard_map/ppermute | solution.py:959
  294.5 71.4 %collective-permute-start.7 = (bf16[648,768]{1,0:T(8,128)(2,1)}, bf16[648,768]{1,0:T(8,128)(2,1)S(1)}, u32[]{:S(2)}, u32[]{:S(2)}) collective-permute-start(bf16[648,768]{1,0:T(8,128)(2,1)} %get-tuple-element.130), channel_id=1, source_target_pairs={{16,1},{1,16},{18,3},{3,18},{20,5},{5,20},{22,7},{7,22},{24,9},{9,... | collective-permute-start | bytes 2985992 | tf_op jit(solution)/shard_map/ppermute | solution.py:960
  295.3 67.2 %copy-start.8 = (bf16[2,1,648,768]{3,2,1,0:T(8,128)(2,1)S(1)}, bf16[2,1,648,768]{3,2,1,0:T(8,128)(2,1)}, u32[]{:S(2)}) copy-start(bf16[2,1,648,768]{3,2,1,0:T(8,128)(2,1)} %get-tuple-element.95) | copy-start | bytes 5971972
  365.9 17.7 %copy-start.10 = (bf16[648,768]{1,0:T(8,128)(2,1)}, bf16[648,768]{1,0:T(8,128)(2,1)S(1)}, u32[]{:S(2)}) copy-start(bf16[648,768]{1,0:T(8,128)(2,1)S(1)} %collective-permute-done.6) | copy-start | bytes 2985988
  365.9 17.7 %copy-start.12 = (bf16[648,768]{1,0:T(8,128)(2,1)}, bf16[648,768]{1,0:T(8,128)(2,1)S(1)}, u32[]{:S(2)}) copy-start(bf16[648,768]{1,0:T(8,128)(2,1)S(1)} %collective-permute-done.7) | copy-start | bytes 2985988
  397.1 28.1 %copy-start = (bf16[2,2,8,48,1152]{4,3,2,1,0:T(8,128)(2,1)S(1)}, bf16[2,2,8,48,1152]{4,3,2,1,0:T(8,128)(2,1)}, u32[]{:S(2)}) copy-start(bf16[2,2,8,48,1152]{4,3,2,1,0:T(8,128)(2,1)} %qkv_weight_grad.1) | copy-start | bytes 10616836
  400.1 25.1 %collective-permute-start.10 = (bf16[1,2,8,48,1152]{4,3,2,1,0:T(8,128)(2,1)}, bf16[1,2,8,48,1152]{4,3,2,1,0:T(8,128)(2,1)}, u32[]{:S(2)}, u32[]{:S(2)}) collective-permute-start(bf16[1,2,8,48,1152]{4,3,2,1,0:T(8,128)(2,1)} %constant_dynamic-slice_fusion.2), channel_id=1, source_target_pairs={{0,1},{1,0},{2,3},{3,2},{4,5},{5,4},{6,7},{7,6},{8,9},{9,8},{10,11... | collective-permute-start | bytes 5308424 | tf_op jit(solution)/shard_map/ppermute | solution.py:912
  422.6 63.9 %collective-permute-start.8 = (bf16[648,768]{1,0:T(8,128)(2,1)}, bf16[648,768]{1,0:T(8,128)(2,1)}, u32[]{:S(2)}, u32[]{:S(2)}) collective-permute-start(bf16[648,768]{1,0:T(8,128)(2,1)} %get-tuple-element.102), channel_id=1, source_target_pairs={{0,16},{16,0},{1,17},{17,1},{2,18},{18,2},{3,19},{19,3},{4,20},{20... | collective-permute-start | bytes 2985992 | tf_op jit(solution)/shard_map/ppermute | solution.py:959
  423.6 62.9 %collective-permute-start.9 = (bf16[648,768]{1,0:T(8,128)(2,1)}, bf16[648,768]{1,0:T(8,128)(2,1)}, u32[]{:S(2)}, u32[]{:S(2)}) collective-permute-start(bf16[648,768]{1,0:T(8,128)(2,1)} %get-tuple-element.103), channel_id=1, source_target_pairs={{16,1},{1,16},{18,3},{3,18},{20,5},{5,20},{22,7},{7,22},{24,9},{9,... | collective-permute-start | bytes 2985992 | tf_op jit(solution)/shard_map/ppermute | solution.py:960
  428.4 2.4 copy-start.4
  428.4 2.6 copy-start.11
  430.2 2.6 copy-start.15
  430.2 15.4 %collective-permute-start.15 = (bf16[4,48,1152]{2,1,0:T(8,128)(2,1)S(1)}, bf16[4,48,1152]{2,1,0:T(8,128)(2,1)S(1)}, u32[]{:S(2)}, u32[]{:S(2)}) collective-permute-start(bf16[4,48,1152]{2,1,0:T(8,128)(2,1)S(1)} %dynamic-slice_bitcast_fusion.2), channel_id=1, source_target_pairs={{0,4},{1,5},{2,6},{3,7},{4,0},{5,1},{6,2},{7,3},{8,12},{9,13},{10,... | collective-permute-start | bytes 1327112 | tf_op jit(solution)/shard_map/ppermute | solution.py:912
  432.8 38.8 %collective-permute-start.20 = (bf16[432,768]{1,0:T(8,128)(2,1)S(1)}, bf16[432,768]{1,0:T(8,128)(2,1)S(1)}, u32[]{:S(2)}, u32[]{:S(2)}) collective-permute-start(bf16[432,768]{1,0:T(8,128)(2,1)S(1)} %bitcast.122), channel_id=1, source_target_pairs={{0,16},{16,0},{1,17},{17,1},{2,18},{18,2},{3,19},{19,3},{4,20},{20... | collective-permute-start | bytes 1990664 | tf_op jit(solution)/shard_map/ppermute | solution.py:970
  436.2 11.5 %collective-permute-start.11 = (bf16[4,48,1152]{2,1,0:T(8,128)(2,1)S(1)}, bf16[4,48,1152]{2,1,0:T(8,128)(2,1)S(1)}, u32[]{:S(2)}, u32[]{:S(2)}) collective-permute-start(bf16[4,48,1152]{2,1,0:T(8,128)(2,1)S(1)} %dynamic-slice_bitcast_fusion.3), channel_id=1, source_target_pairs={{0,2},{1,3},{2,0},{3,1},{4,6},{5,7},{6,4},{7,5},{8,10},{9,11},{10,... | collective-permute-start | bytes 1327112 | tf_op jit(solution)/shard_map/ppermute | solution.py:912
  445.7 18.0 %collective-permute-start.16 = (bf16[2,48,1152]{2,1,0:T(8,128)(2,1)S(1)}, bf16[2,48,1152]{2,1,0:T(8,128)(2,1)S(1)}, u32[]{:S(2)}, u32[]{:S(2)}) collective-permute-start(bf16[2,48,1152]{2,1,0:T(8,128)(2,1)S(1)} %dynamic-slice_bitcast_fusion.4), channel_id=1, source_target_pairs={{0,8},{1,9},{2,10},{3,11},{4,12},{5,13},{6,14},{7,15},{8,0},{9,1},... | collective-permute-start | bytes 663560 | tf_op jit(solution)/shard_map/ppermute | solution.py:912
  447.8 24.0 %collective-permute-start.12 = (bf16[2,48,1152]{2,1,0:T(8,128)(2,1)S(1)}, bf16[2,48,1152]{2,1,0:T(8,128)(2,1)S(1)}, u32[]{:S(2)}, u32[]{:S(2)}) collective-permute-start(bf16[2,48,1152]{2,1,0:T(8,128)(2,1)S(1)} %dynamic-slice_bitcast_fusion.5), channel_id=1, source_target_pairs={{0,4},{1,5},{2,6},{3,7},{4,0},{5,1},{6,2},{7,3},{8,12},{9,13},{10,... | collective-permute-start | bytes 663560 | tf_op jit(solution)/shard_map/ppermute | solution.py:912
  463.7 12.1 %collective-permute-start.17 = (bf16[1,48,1152]{2,1,0:T(8,128)(2,1)S(1)}, bf16[1,48,1152]{2,1,0:T(8,128)(2,1)S(1)}, u32[]{:S(2)}, u32[]{:S(2)}) collective-permute-start(bf16[1,48,1152]{2,1,0:T(8,128)(2,1)S(1)} %constant_dynamic-slice_fusion), channel_id=1, source_target_pairs={{0,2},{1,3},{2,0},{3,1},{4,6},{5,7},{6,4},{7,5},{8,10},{9,11},{10,... | collective-permute-start | bytes 331784 | tf_op jit(solution)/shard_map/ppermute | solution.py:912
  471.9 17.3 %copy-start.9 = (bf16[648,768]{1,0:T(8,128)(2,1)S(1)}, bf16[648,768]{1,0:T(8,128)(2,1)}, u32[]{:S(2)}) copy-start(bf16[648,768]{1,0:T(8,128)(2,1)} %get-tuple-element.103) | copy-start | bytes 2985988
  473.5 15.9 %copy-start.13 = (bf16[648,768]{1,0:T(8,128)(2,1)S(1)}, bf16[648,768]{1,0:T(8,128)(2,1)}, u32[]{:S(2)}) copy-start(bf16[648,768]{1,0:T(8,128)(2,1)} %get-tuple-element.101) | copy-start | bytes 2985988
  474.3 7.3 %collective-permute-start.13 = (bf16[1,48,1152]{2,1,0:T(8,128)(2,1)S(1)}, bf16[1,48,1152]{2,1,0:T(8,128)(2,1)S(1)}, u32[]{:S(2)}, u32[]{:S(2)}) collective-permute-start(bf16[1,48,1152]{2,1,0:T(8,128)(2,1)S(1)} %constant_dynamic-slice_fusion.1), channel_id=1, source_target_pairs={{0,8},{1,9},{2,10},{3,11},{4,12},{5,13},{6,14},{7,15},{8,0},{9,1},... | collective-permute-start | bytes 331784 | tf_op jit(solution)/shard_map/ppermute | solution.py:912
  475.8 7.2 %collective-permute-start.18 = (bf16[48,1152]{1,0:T(8,128)(2,1)S(1)}, bf16[48,1152]{1,0:T(8,128)(2,1)S(1)}, u32[]{:S(2)}, u32[]{:S(2)}) collective-permute-start(bf16[48,1152]{1,0:T(8,128)(2,1)S(1)} %fusion.9), channel_id=1, source_target_pairs={{0,16},{16,0},{1,17},{17,1},{2,18},{18,2},{3,19},{19,3},{4,20},{20... | collective-permute-start | bytes 331784 | tf_op jit(solution)/shard_map/ppermute | solution.py:970
  481.6 4.8 collective-permute-start.14
  487.5 3.3 copy-start.5
  487.5 3.3 copy-start.6
  487.5 3.3 copy-start.7
  487.5 7.2 %collective-permute-start.19 = (f32[10,128]{1,0:T(8,128)S(1)}, f32[10,128]{1,0:T(8,128)S(1)}, u32[]{:S(2)}, u32[]{:S(2)}) collective-permute-start(f32[10,128]{1,0:T(8,128)S(1)} %dynamic-slice_reduce_fusion), channel_id=1, source_target_pairs={{0,16},{16,0},{1,17},{17,1},{2,18},{18,2},{3,19},{19,3},{4,20},{20... | collective-permute-start | bytes 15368 | tf_op jit(solution)/shard_map/ppermute | solution.py:970
Sparse Core Ops, SparseCore 0:
  10.9 52.9 all-gather.7
  66.1 87.1 all-gather.9
  257.7 118.3 reduce-scatter.1
  425.4 41.3 all-gather.5

commit v4 on v3

--- a/solution.py
+++ b/solution.py
@@ -856,13 +856,28 @@
 
 
 def input_kernel(
-    x_ref, dx_ref, dq_ref, dkv_ref, weight_ref, vectors_ref, first_ref, second_ref, third_ref, sums_ref
+    x_ref,
+    dx_ref,
+    dq_ref,
+    dkv_ref,
+    weight_ref,
+    vectors_ref,
+    sums_two_ref,
+    hidden_sum_ref,
+    first_ref,
+    second_ref,
+    third_ref,
+    sums_ref,
 ):
     step = pl.program_id(0)
+    width = x_ref.shape[-1]
 
     @pl.when(step == 0)
     def clear():
         sums_ref[...] = jnp.zeros_like(sums_ref)
+        sums_ref[4:8] = sums_two_ref[0:4]
+        for part in range(hidden_sum_ref.shape[1] // width):
+            sums_ref[8 + part : 9 + part] = hidden_sum_ref[0:1, part * width : (part + 1) * width]
 
     gain = vectors_ref[0:1]
     unused, unit, scale = normalize(x_ref[0].astype(F32), gain, vectors_ref[1:2])
@@ -882,7 +897,7 @@
     sums_ref[3:4] += column(dkv_ref[1, 0].astype(F32))
 
 
-def input_grads(units, grad_middle, dq, dkv, weight, vectors):
+def input_grads(units, grad_middle, dq, dkv, weight, vectors, sums_two, sum_hidden):
     count, size, width = units.shape
     rows = pl.BlockSpec((1, size, width), lambda u: (u, 0, 0))
     return pl.pallas_call(
@@ -895,13 +910,15 @@
             pl.BlockSpec((2, 1, size, width), lambda u: (0, u, 0, 0)),
             whole(weight.shape),
             whole(vectors.shape),
-        ],
-        out_specs=[whole((size, width))] * 3 + [pl.BlockSpec((8, width), lambda u: (0, 0))],
-        out_shape=[shaped((size, width), BF16)] * 3 + [shaped((8, width), F32)],
+            whole(sums_two.shape),
+            whole(sum_hidden.shape),
+        ],
+        out_specs=[whole((size, width))] * 3 + [whole((32, width))],
+        out_shape=[shaped((size, width), BF16)] * 3 + [shaped((32, width), F32)],
         compiler_params=params(1),
         cost_estimate=LATE,
         name="input_grads",
-    )(units, grad_middle, dq, dkv, weight, vectors)
+    )(units, grad_middle, dq, dkv, weight, vectors, sums_two, sum_hidden)
 
 
 def halving_sum(value, axis, size, place, order):
@@ -1037,9 +1054,12 @@
     dkv = dkv.at[:, 2].set((dkv_one.astype(F32) + dkv_got.astype(F32)).astype(BF16)[:, 0])
     dq, dkv, out_got, out_centre = lax.optimization_barrier((dq, dkv, out_got, out_centre))
     block_out = in_place(out, out_got, out_centre)
-    *grad_units, sums_one = input_grads(units, grad_attended, dq, dkv, full_head, vectors)
+    *grad_units, sums = input_grads(
+        units, grad_attended, dq, dkv, full_head, vectors, sums_two, sum_hidden
+    )
     got, centre = send_back(grad_units)
-    dq, dkv, sums_one = lax.optimization_barrier((dq, dkv, sums_one))
+    everyone = lax.all_gather(sums, "fsdp", axis=0)
+    dq, dkv, sums = lax.optimization_barrier((dq, dkv, sums))
     sides = qkv_weight_grad(flat(normed), flat(dq), dkv.reshape(2, row_count, width), fsdp_size)
     orders = halving_orders(fsdp_size)
     sides = halving_sum(sides, "fsdp", fsdp_size, place, [1])[0]
@@ -1049,42 +1069,27 @@
         halving_sum(value, "fsdp", fsdp_size, place, order[1:])[0]
         for value, order in zip(sides, orders)
     ]
-    small_grads = [
-        sums_one[0],
-        sums_one[1],
-        sums_one[2],
-        sums_one[3],
-        sums_two[3],
-        sums_two[1],
-        sums_two[2],
-        sums_two[0],
-        sum_hidden[0],
-    ]
-    packed = jnp.concatenate([value.reshape(fsdp_size, -1) for value in small_grads], 1)
-    packed = jnp.pad(packed, ((0, 0), (0, -packed.shape[1] % 1280)))
-    lines = packed.shape[1] // 128
-    everyone = lax.all_gather(packed.reshape(-1, 128), "fsdp", axis=0)
     shard_sides = [both(value) for value in shard_sides]
     got, centre, shard_sides, everyone = lax.optimization_barrier(
         (got, centre, shard_sides, everyone)
     )
-    mine = lax.dynamic_slice_in_dim(everyone, place * lines, lines, 1).sum(0)
     input_grad = in_place(grad_units, got, centre)
-    mine = both(mine).reshape(-1)
-    pieces = []
-    for index in range(len(short)):
-        pieces.append(mine[index * count : (index + 1) * count])
+    totals = both(everyone[:, : 8 + parts].sum(0))
+    mine = lax.dynamic_slice_in_dim(totals[:8], place * count, count, 1)
     (
         grad_gain_one,
         grad_shift_one,
         grad_query_b,
         grad_value_b,
-        grad_proj_b,
+        grad_output_b,
         grad_gain_two,
         grad_shift_two,
-        grad_output_b,
-    ) = pieces
-    grad_hidden_b = mine[len(short) * count :][: hidden_bias.shape[0]]
+        grad_proj_b,
+    ) = [mine[index] for index in range(8)]
+    inner_count = hidden_bias.shape[0]
+    grad_hidden_b = lax.dynamic_slice_in_dim(
+        totals[8:].reshape(-1), place * inner_count, inner_count, 0
+    )
     grad_hidden_w = jnp.concatenate(
         [shard_pack[part * rows : (part + 1) * rows] for part in range(parts)], 1
     )
@@ -1123,6 +1128,7 @@
             and width % 128 == 0
             and (width // fsdp_size) % 16 == 0
             and inner % width == 0
+            and inner // width <= 24
             and width // fsdp_size <= 128
             and 128 + inner // fsdp_size <= 3 * width
             and fsdp_size % (inner // width) == 0

time: 511 us -> 480 us (0.939)
  local copies, waits for them, and re-layouts: 39.3 us -> 18.9 us
  Pallas kernels: 310 us -> 299 us
    ppermute x4, waiting for transfers between devices: 10.9 us -> 25.6 us  [both(): lax.ppermute(value, 'seq', swap_sides).astype(F32)]
    ppermute x7, waiting for transfers between devices: 29.6 us -> 16.3 us  [halving_sum(): lax.ppermute(lax.dynamic_index_in_dim(halves, 1 - bit, 0, False), axis, p...]
    another operation x10 -> x0, local copies, waits for them, and re-layouts: 13.2 us -> none  [the longest x9 11.6 us: fast_body(): value.reshape(fsdp_size, -1)]
    pallas_call x1, Pallas kernels: 46.9 us -> 35.2 us  [weight_grads(): pl.pallas_call(functools.partial(weight_kernel, parts, shards), grid=(2 *...]
    slice x6 -> x2, local copies, waits for them, and re-layouts: 5.74 us -> 0.01 us  [the longest x1 0.01 us: fast_body(): mine = lax.dynamic_slice_in_dim(totals[:8], place * count, count, 1)]
  transfers between devices with their start and end apart: 25 -> 25, of which waited for: 9 -> 9; matrix products, arithmetic and copies ran while one was open for 12% -> 8% of each run, Pallas kernels for 41% -> 43%
where the time goes in v4:
time: 480 us; the launch traced here: 472 us
  Pallas kernels  299 us (62%)
  waiting for transfers between devices  86.4 us (18%)
  starting transfers between devices  27.3 us (6%)
  other arithmetic  25.7 us (5%)
  local copies, waits for them, and re-layouts  18.9 us (4%)
  between operations  14.4 us (3%)
    pallas_call x2, Pallas kernels, mix_back(): pl.pallas_call(functools.partial(mix_back_kernel, unit_count), grid=(pair...  101 us
    pallas_call x2, Pallas kernels, mix(): pl.pallas_call(mix_kernel, grid=(pairs, unit_count), in_specs=[pl.BlockSp...  57.9 us
    pallas_call x1, Pallas kernels, feed(): pl.pallas_call(feed_kernel, grid=(count,), in_specs=[rows(width), rows(wi...  57.6 us
    pallas_call x1, Pallas kernels, weight_grads(): pl.pallas_call(functools.partial(weight_kernel, parts, shards), grid=(2 *...  35.2 us
    ppermute x2, waiting for transfers between devices, gather_units(): lax.ppermute(lax.dynamic_index_in_dim(values, 2 * (1 - side), 0, False),...  32.3 us
    ppermute x4, waiting for transfers between devices, both(): lax.ppermute(value, 'seq', swap_sides).astype(F32)  25.6 us
    pallas_call x1, Pallas kernels, input_grads(): pl.pallas_call(input_kernel, grid=(count,), in_specs=[rows, rows, rows, p...  17.7 us
    ppermute x7, waiting for transfers between devices, halving_sum(): lax.ppermute(lax.dynamic_index_in_dim(halves, 1 - bit, 0, False), axis, p...  16.3 us
  transfers between devices with their start and end apart: 25, of which 9 were waited for; matrix products, arithmetic and copies ran while one was open for 8% of the time, Pallas kernels for 43%

profile of v4, /device:TPU:0, one launch (start us, length us, event | category | flops | bytes accessed | tf_op | source)
XLA Modules:
  0.0 471.9 jit_solution(4736668941955070832)
XLA Ops:
  7.2 1.2 broadcast_in_dim.30.hidden_ref
  8.4 1.7 head_pack.1
  10.3 3.0 constant_dynamic-slice_fusion.5
  13.2 1.6 collective-permute-start.1
  14.9 3.3 collective-permute-start
  18.1 1.3 select_bitcast_fusion.5
  19.4 32.3 %collective-permute-done = bf16[648,768]{1,0:T(8,128)(2,1)S(1)} collective-permute-done((bf16[648,768]{1,0:T(8,128)(2,1)S(1)}, bf16[648,768]{1,0:T(8,128)(2,1)S(1)}, u32[]{:S(2)}, u32[]{:S(2)}) %collective-permute-start) | collective-permute-done | bytes 995360 | tf_op jit(solution)/shard_map/ppermute | solution.py:968
  51.8 1.9 pad_maximum_fusion.x_ref
  54.8 9.1 %all-gather.7.cloned.1.call-done = bf16[896,2304]{1,0:T(8,128)(2,1)} async-done(((bf16[56,2304]{1,0:T(8,128)(2,1)}), bf16[896,2304]{1,0:T(8,128)(2,1)}) %all-gather.7.cloned.1.call-update) | async-done | bytes 4128784 | tf_op jit(solution)/shard_map/all_gather | solution.py:1002
  65.3 14.4 %project.1 = (bf16[3,3,648,768]{3,2,1,0:T(8,128)(2,1)}, bf16[3,648,768]{2,1,0:T(8,128)(2,1)}, bf16[2,648,768]{2,1,0:T(8,128)(2,1)}) custom-call(bf16[3,648,768]{2,1,0:T(8,128)(2,1)} %pad_maximum_fusion.x_ref, bf16[16,56,2304]{2,1,0:T(8,128)(2,1)} %bitcast.121, f32[8,768]{1,0:T(8,128)} %reshape.163.vectors_ref), custom_call_target="tpu_custom_call" | custom-call | flops 6879707136 | bytes 18468864 | tf_op jit(solution)/shard_map/project/pallas_call | solution.py:363
  79.8 1.5 constant_dynamic-slice_fusion.4
  81.3 1.6 collective-permute-start.4
  82.9 2.2 collective-permute-start.3
  85.1 38.0 %mix.2 = (bf16[3,648,768]{2,1,0:T(8,128)(2,1)}, f32[2,6,8,648]{3,2,1,0:T(8,128)}) custom-call(bf16[3,3,648,768]{3,2,1,0:T(8,128)(2,1)} %get-tuple-element.73.q_ref.ka_ref.va_ref.kb_ref.vb_ref, bf16[3,3,648,768]{3,2,1,0:T(8,128)(2,1)} %get-tuple-element.73.q_ref.ka_ref.va_ref.kb_ref.vb_ref, ...), custom_call_target="tpu_custom_call" | custom-call | flops 20639121408 | bytes 7962624 | tf_op jit(solution)/shard_map/mix/pallas_call | solution.py:463
  124.7 1.3 select_bitcast_fusion.4
  126.0 3.1 pad_maximum_fusion.1.cot_ref
  129.2 1.3 copy-done.1
  130.5 19.9 %mix.3 = (bf16[3,648,768]{2,1,0:T(8,128)(2,1)}, f32[1,6,8,648]{3,2,1,0:T(8,128)}) custom-call(bf16[3,3,648,768]{3,2,1,0:T(8,128)(2,1)} %get-tuple-element.73.q_ref.ka_ref.va_ref.kb_ref.vb_ref, bf16[3,3,648,768]{3,2,1,0:T(8,128)(2,1)} %get-tuple-element.73.q_ref.ka_ref.va_ref.kb_ref.vb_ref, ...), custom_call_target="tpu_custom_call", output_to_operand_aliasing={{0}: (5, {})} | custom-call | flops 10319560704 | bytes 3981312 | tf_op jit(solution)/shard_map/mix/pallas_call | solution.py:463
  150.4 3.0 all-gather.9.cloned.1.call-done
  153.3 57.6 %feed.1 = (bf16[3,648,768]{2,1,0:T(8,128)(2,1)}, bf16[3,648,768]{2,1,0:T(8,128)(2,1)}, bf16[3,648,768]{2,1,0:T(8,128)(2,1)}, bf16[3,648,3072]{2,1,0:T(8,128)(2,1...) custom-call(bf16[3,648,768]{2,1,0:T(8,128)(2,1)} %pad_maximum_fusion.x_r, ...), custom_call_target="tpu_custom_call" | custom-call | flops 41278242816 | bytes 53747712 | tf_op jit(solution)/shard_map/feed/pallas_call | solution.py:693
  211.0 35.2 %weight_grads.1 = bf16[16,432,768]{2,1,0:T(8,128)(2,1)} custom-call(bf16[1944,768]{1,0:T(8,128)(2,1)} %bitcast.150, bf16[1944,3072]{1,0:T(8,128)(2,1)} %bitcast.149, bf16[1944,3072]{1,0:T(8,128)(2,1)} %bitcast.148, bf16[1944,768]{1,0:T(8,128)(2,1)} %bitcast.130, bf16[1944,768]{1,0:T(8,128)(2,1)} %bitcast.115, bf16[1944,768]{1,0:T(8,128)(2,1)} %bitcast.129), custom_call_target="tpu_custom_call" | custom-call | flops 20639121408 | bytes 35831808 | tf_op jit(solution)/shard_map/weight_grads/pallas_call | solution.py:772
  246.3 33.8 %mix_back.2 = (bf16[3,648,768]{2,1,0:T(8,128)(2,1)}, bf16[2,1,648,768]{3,2,1,0:T(8,128)(2,1)}, bf16[2,1,648,768]{3,2,1,0:T(8,128)(2,1)}) custom-call(bf16[3,3,648,768]{3,2,1,0:T(8,128)(2,1)} %get-tuple-element.73.q_ref.ka_ref.va_ref.kb_ref.vb_ref, bf16[3,3,648,768]{3,2,1,0:T(8,128)(2,1)} %get-tuple-element.73.q_ref.ka_ref.va_ref.kb_ref.vb_ref, ...), custom_call_target="tpu_custom_call" | custom-call | flops 1000 | bytes 1000 | tf_op jit(solution)/shard_map/mix_back/pallas_call | solution.py:579
  280.3 1.5 slice_bitcast_fusion
  281.8 1.5 collective-permute-start.6
  284.0 67.1 %mix_back.3 = (bf16[3,648,768]{2,1,0:T(8,128)(2,1)}, bf16[2,3,648,768]{3,2,1,0:T(8,128)(2,1)}, f32[8,128]{1,0:T(8,128)}) custom-call(bf16[3,3,648,768]{3,2,1,0:T(8,128)(2,1)} %get-tuple-element.73.q_ref.ka_ref.va_ref.kb_ref.vb_ref, bf16[3,3,648,768]{3,2,1,0:T(8,128)(2,1)} %get-tuple-element.73.q_ref.ka_ref.va_ref.kb_ref.vb_ref, ...), custom_call_target="tpu_custom_call", output_to_operand_aliasing={{0}: (8, {})} | custom-call | flops 1000 | bytes 1000 | tf_op jit(solution)/shard_map/mix_back/pallas_call | solution.py:579
  351.1 3.4 fusion.dkv_ref
  354.5 17.7 %input_grads.1 = (bf16[648,768]{1,0:T(8,128)(2,1)}, bf16[648,768]{1,0:T(8,128)(2,1)}, bf16[648,768]{1,0:T(8,128)(2,1)}, f32[32,768]{1,0:T(8,128)}) custom-call(bf16[3,648,768]{2,1,0:T(8,128)(2,1)} %pad_maximum_fusion.x_ref, bf16[3,648,768]{2,1,0:T(8,128)(2,1)} %get-tuple-element.87.dx_ref, bf16[3,648,768]{2,1,0:T(8,128)(2,1)} %get-tuple-element.107.dq_ref, ...), custom_call_target="tpu_custom_call" | custom-call | flops 1000 | bytes 1000 | tf_op jit(solution)/shard_map/input_grads/pallas_call | solution.py:903
  372.3 13.6 %qkv_weight_grad.1 = bf16[2,2,8,48,1152]{4,3,2,1,0:T(8,128)(2,1)} custom-call(bf16[1944,768]{1,0:T(8,128)(2,1)} %bitcast.128, bf16[1944,768]{1,0:T(8,128)(2,1)} %bitcast.113, bf16[2,1944,768]{2,1,0:T(8,128)(2,1)} %bitcast.114), custom_call_target="tpu_custom_call" | custom-call | flops 1000 | bytes 1000 | tf_op jit(solution)/shard_map/qkv_weight_grad/pallas_call | solution.py:841
  385.9 3.0 constant_dynamic-slice_fusion.3
  388.9 1.8 collective-permute-start.10
  390.7 1.0 collective-permute-start.8
  391.6 1.6 collective-permute-start.9
  393.3 1.0 collective-permute-done.10
  394.3 3.1 fusion.1
  397.5 1.7 fusion.11
  400.1 1.7 fusion.2
  401.9 2.5 collective-permute-start.20
  405.0 10.0 %collective-permute-done.15 = bf16[4,48,1152]{2,1,0:T(8,128)(2,1)S(1)} collective-permute-done((bf16[4,48,1152]{2,1,0:T(8,128)(2,1)S(1)}, bf16[4,48,1152]{2,1,0:T(8,128)(2,1)S(1)}, u32[]{:S(2)}, u32[]{:S(2)}) %collective-permute-start.15) | collective-permute-done | bytes 442400 | tf_op jit(solution)/shard_map/ppermute | solution.py:929
  415.1 1.5 collective-permute-start.16
  417.4 22.3 %collective-permute-done.20 = bf16[432,768]{1,0:T(8,128)(2,1)S(1)} collective-permute-done((bf16[432,768]{1,0:T(8,128)(2,1)S(1)}, bf16[432,768]{1,0:T(8,128)(2,1)S(1)}, u32[]{:S(2)}, u32[]{:S(2)}) %collective-permute-start.20) | collective-permute-done | bytes 663584 | tf_op jit(solution)/shard_map/ppermute | solution.py:987
  443.1 1.5 collective-permute-start.13
  445.6 4.5 collective-permute-done.13
  450.1 1.7 collective-permute-start.14
  451.9 3.3 collective-permute-done.14
  455.3 1.2 slice_reduce_fusion
  456.5 1.8 collective-permute-start.19
  458.4 1.5 select_bitcast_fusion.2
  459.9 3.1 pad_maximum_fusion.2
  (108 shorter events, 14.3 us)
Async XLA Ops:
  7.2 56.7 %all-gather.7.cloned.1.call-start = ((), (), s32[]{:S(2)}) async-start(), calls=%async_computation.2 | async-start | bytes 4386816 | tf_op jit(solution)/shard_map/all_gather | solution.py:1002
  10.2 143.1 %all-gather.9.cloned.1.call-start = ((), (), s32[]{:S(2)}) async-start(), calls=%async_computation.3 | async-start | bytes 11280384 | tf_op jit(solution)/shard_map/all_gather | solution.py:1012
  13.2 4.9 %collective-permute-start.1 = (bf16[648,768]{1,0:T(8,128)(2,1)}, bf16[648,768]{1,0:T(8,128)(2,1)}, u32[]{:S(2)}, u32[]{:S(2)}) collective-permute-start(bf16[648,768]{1,0:T(8,128)(2,1)} %get-tuple-element.126), channel_id=1, source_target_pairs={{16,1},{1,16},{18,3},{3,18},{20,5},{5,20},{22,7},{7,22},{24,9},{9,... | collective-permute-start | bytes 2985992 | tf_op jit(solution)/shard_map/ppermute | solution.py:965
  14.9 36.9 %collective-permute-start = (bf16[648,768]{1,0:T(8,128)(2,1)S(1)}, bf16[648,768]{1,0:T(8,128)(2,1)S(1)}, u32[]{:S(2)}, u32[]{:S(2)}) collective-permute-start(bf16[648,768]{1,0:T(8,128)(2,1)S(1)} %get-tuple-element.127), channel_id=1, source_target_pairs={{0,16},{16,0},{1,17},{17,1},{2,18},{18,2},{3,19},{19,3},{4,20},{20... | collective-permute-start | bytes 2985992 | tf_op jit(solution)/shard_map/ppermute | solution.py:968
  51.8 1.9 copy-start.16
  51.8 2.0 copy-start.17
  51.8 2.0 copy-start.18
  53.9 0.9 copy-start.14
  54.7 342.7 %reduce-scatter.2.cloned.1.call-start = ((), (), s32[]{:S(2)}) async-start(), calls=%async_computation.1 | async-start | bytes 11280384 | tf_op jit(solution)/shard_map/reduce_scatter | solution.py:1050
  65.3 14.4 %copy-start.2 = (bf16[3,648,768]{2,1,0:T(8,128)(2,1)S(1)}, bf16[3,648,768]{2,1,0:T(8,128)(2,1)}, u32[]{:S(2)}) copy-start(bf16[3,648,768]{2,1,0:T(8,128)(2,1)} %param.18) | copy-start | bytes 8957956
  81.3 43.4 %collective-permute-start.4 = (bf16[648,768]{1,0:T(8,128)(2,1)}, bf16[648,768]{1,0:T(8,128)(2,1)}, u32[]{:S(2)}, u32[]{:S(2)}) collective-permute-start(bf16[648,768]{1,0:T(8,128)(2,1)} %get-tuple-element.123), channel_id=1, source_target_pairs={{16,1},{1,16},{18,3},{3,18},{20,5},{5,20},{22,7},{7,22},{24,9},{9,... | collective-permute-start | bytes 2985992 | tf_op jit(solution)/shard_map/ppermute | solution.py:965
  82.9 43.1 %collective-permute-start.3 = (bf16[648,768]{1,0:T(8,128)(2,1)}, bf16[648,768]{1,0:T(8,128)(2,1)}, u32[]{:S(2)}, u32[]{:S(2)}) collective-permute-start(bf16[648,768]{1,0:T(8,128)(2,1)} %get-tuple-element.124), channel_id=1, source_target_pairs={{0,16},{16,0},{1,17},{17,1},{2,18},{18,2},{3,19},{19,3},{4,20},{20... | collective-permute-start | bytes 2985992 | tf_op jit(solution)/shard_map/ppermute | solution.py:968
  85.1 44.1 %collective-permute-start.2 = (bf16[2,648,768]{2,1,0:T(8,128)(2,1)}, bf16[2,648,768]{2,1,0:T(8,128)(2,1)S(1)}, u32[]{:S(2)}, u32[]{:S(2)}) collective-permute-start(bf16[2,648,768]{2,1,0:T(8,128)(2,1)} %get-tuple-element.75), channel_id=1, source_target_pairs={{0,1},{1,0},{2,3},{3,2},{4,5},{5,4},{6,7},{7,6},{8,9},{9,8},{10,11... | collective-permute-start | bytes 5971976 | tf_op jit(solution)/shard_map/ppermute | solution.py:1019
  129.2 1.3 copy-start.1
  246.2 209.0 %all-gather.11.cloned.1.call-start = ((), (), s32[]{:S(2)}) async-start(), calls=%async_computation.4 | async-start | bytes 1671168 | tf_op jit(solution)/shard_map/all_gather | solution.py:1061
  246.3 34.1 %copy-start.3 = (bf16[3,648,768]{2,1,0:T(8,128)(2,1)S(1)}, bf16[3,648,768]{2,1,0:T(8,128)(2,1)}, u32[]{:S(2)}) copy-start(bf16[3,648,768]{2,1,0:T(8,128)(2,1)} %get-tuple-element.82) | copy-start | bytes 8957956
  280.1 71.0 %collective-permute-start.5 = (bf16[2,1,648,768]{3,2,1,0:T(8,128)(2,1)}, bf16[2,1,648,768]{3,2,1,0:T(8,128)(2,1)}, u32[]{:S(2)}, u32[]{:S(2)}) collective-permute-start(bf16[2,1,648,768]{3,2,1,0:T(8,128)(2,1)} %get-tuple-element.95), channel_id=1, source_target_pairs={{0,1},{1,0},{2,3},{3,2},{4,5},{5,4},{6,7},{7,6},{8,9},{9,8},{10,11... | collective-permute-start | bytes 5971976 | tf_op jit(solution)/shard_map/ppermute | solution.py:1052
  281.8 72.7 %collective-permute-start.6 = (bf16[648,768]{1,0:T(8,128)(2,1)}, bf16[648,768]{1,0:T(8,128)(2,1)S(1)}, u32[]{:S(2)}, u32[]{:S(2)}) collective-permute-start(bf16[648,768]{1,0:T(8,128)(2,1)} %get-tuple-element.121), channel_id=1, source_target_pairs={{0,16},{16,0},{1,17},{17,1},{2,18},{18,2},{3,19},{19,3},{4,20},{20... | collective-permute-start | bytes 2985992 | tf_op jit(solution)/shard_map/ppermute | solution.py:976
  283.3 71.3 %collective-permute-start.7 = (bf16[648,768]{1,0:T(8,128)(2,1)}, bf16[648,768]{1,0:T(8,128)(2,1)S(1)}, u32[]{:S(2)}, u32[]{:S(2)}) collective-permute-start(bf16[648,768]{1,0:T(8,128)(2,1)} %get-tuple-element.120), channel_id=1, source_target_pairs={{16,1},{1,16},{18,3},{3,18},{20,5},{5,20},{22,7},{7,22},{24,9},{9,... | collective-permute-start | bytes 2985992 | tf_op jit(solution)/shard_map/ppermute | solution.py:977
  284.0 67.1 %copy-start.8 = (bf16[2,1,648,768]{3,2,1,0:T(8,128)(2,1)S(1)}, bf16[2,1,648,768]{3,2,1,0:T(8,128)(2,1)}, u32[]{:S(2)}) copy-start(bf16[2,1,648,768]{3,2,1,0:T(8,128)(2,1)} %get-tuple-element.94) | copy-start | bytes 5971972
  354.5 17.7 %copy-start.10 = (bf16[648,768]{1,0:T(8,128)(2,1)}, bf16[648,768]{1,0:T(8,128)(2,1)S(1)}, u32[]{:S(2)}) copy-start(bf16[648,768]{1,0:T(8,128)(2,1)S(1)} %collective-permute-done.6) | copy-start | bytes 2985988
  354.5 17.7 %copy-start.12 = (bf16[648,768]{1,0:T(8,128)(2,1)}, bf16[648,768]{1,0:T(8,128)(2,1)S(1)}, u32[]{:S(2)}) copy-start(bf16[648,768]{1,0:T(8,128)(2,1)S(1)} %collective-permute-done.7) | copy-start | bytes 2985988
  385.9 8.5 %copy-start = (bf16[2,2,8,48,1152]{4,3,2,1,0:T(8,128)(2,1)S(1)}, bf16[2,2,8,48,1152]{4,3,2,1,0:T(8,128)(2,1)}, u32[]{:S(2)}) copy-start(bf16[2,2,8,48,1152]{4,3,2,1,0:T(8,128)(2,1)} %qkv_weight_grad.1) | copy-start | bytes 10616836
  388.9 5.5 %collective-permute-start.10 = (bf16[1,2,8,48,1152]{4,3,2,1,0:T(8,128)(2,1)}, bf16[1,2,8,48,1152]{4,3,2,1,0:T(8,128)(2,1)}, u32[]{:S(2)}, u32[]{:S(2)}) collective-permute-start(bf16[1,2,8,48,1152]{4,3,2,1,0:T(8,128)(2,1)} %constant_dynamic-slice_fusion.3), channel_id=1, source_target_pairs={{0,1},{1,0},{2,3},{3,2},{4,5},{5,4},{6,7},{7,6},{8,9},{9,8},{10,11... | collective-permute-start | bytes 5308424 | tf_op jit(solution)/shard_map/ppermute | solution.py:929
  390.7 64.6 %collective-permute-start.8 = (bf16[648,768]{1,0:T(8,128)(2,1)}, bf16[648,768]{1,0:T(8,128)(2,1)}, u32[]{:S(2)}, u32[]{:S(2)}) collective-permute-start(bf16[648,768]{1,0:T(8,128)(2,1)} %get-tuple-element.103), channel_id=1, source_target_pairs={{0,16},{16,0},{1,17},{17,1},{2,18},{18,2},{3,19},{19,3},{4,20},{20... | collective-permute-start | bytes 2985992 | tf_op jit(solution)/shard_map/ppermute | solution.py:976
  391.6 63.6 %collective-permute-start.9 = (bf16[648,768]{1,0:T(8,128)(2,1)}, bf16[648,768]{1,0:T(8,128)(2,1)}, u32[]{:S(2)}, u32[]{:S(2)}) collective-permute-start(bf16[648,768]{1,0:T(8,128)(2,1)} %get-tuple-element.104), channel_id=1, source_target_pairs={{16,1},{1,16},{18,3},{3,18},{20,5},{5,20},{22,7},{7,22},{24,9},{9,... | collective-permute-start | bytes 2985992 | tf_op jit(solution)/shard_map/ppermute | solution.py:977
  397.4 2.4 copy-start.4
  397.5 2.7 copy-start.11
  399.2 2.7 copy-start.15
  399.2 15.7 %collective-permute-start.15 = (bf16[4,48,1152]{2,1,0:T(8,128)(2,1)S(1)}, bf16[4,48,1152]{2,1,0:T(8,128)(2,1)S(1)}, u32[]{:S(2)}, u32[]{:S(2)}) collective-permute-start(bf16[4,48,1152]{2,1,0:T(8,128)(2,1)S(1)} %dynamic-slice_bitcast_fusion.2), channel_id=1, source_target_pairs={{0,4},{1,5},{2,6},{3,7},{4,0},{5,1},{6,2},{7,3},{8,12},{9,13},{10,... | collective-permute-start | bytes 1327112 | tf_op jit(solution)/shard_map/ppermute | solution.py:929
  401.9 37.8 %collective-permute-start.20 = (bf16[432,768]{1,0:T(8,128)(2,1)S(1)}, bf16[432,768]{1,0:T(8,128)(2,1)S(1)}, u32[]{:S(2)}, u32[]{:S(2)}) collective-permute-start(bf16[432,768]{1,0:T(8,128)(2,1)S(1)} %bitcast.136), channel_id=1, source_target_pairs={{0,16},{16,0},{1,17},{17,1},{2,18},{18,2},{3,19},{19,3},{4,20},{20... | collective-permute-start | bytes 1990664 | tf_op jit(solution)/shard_map/ppermute | solution.py:987
  404.4 12.2 %collective-permute-start.11 = (bf16[4,48,1152]{2,1,0:T(8,128)(2,1)S(1)}, bf16[4,48,1152]{2,1,0:T(8,128)(2,1)S(1)}, u32[]{:S(2)}, u32[]{:S(2)}) collective-permute-start(bf16[4,48,1152]{2,1,0:T(8,128)(2,1)S(1)} %dynamic-slice_bitcast_fusion.3), channel_id=1, source_target_pairs={{0,2},{1,3},{2,0},{3,1},{4,6},{5,7},{6,4},{7,5},{8,10},{9,11},{10,... | collective-permute-start | bytes 1327112 | tf_op jit(solution)/shard_map/ppermute | solution.py:929
  415.1 25.5 %collective-permute-start.16 = (bf16[2,48,1152]{2,1,0:T(8,128)(2,1)S(1)}, bf16[2,48,1152]{2,1,0:T(8,128)(2,1)S(1)}, u32[]{:S(2)}, u32[]{:S(2)}) collective-permute-start(bf16[2,48,1152]{2,1,0:T(8,128)(2,1)S(1)} %dynamic-slice_bitcast_fusion.4), channel_id=1, source_target_pairs={{0,8},{1,9},{2,10},{3,11},{4,12},{5,13},{6,14},{7,15},{8,0},{9,1},... | collective-permute-start | bytes 663560 | tf_op jit(solution)/shard_map/ppermute | solution.py:929
  416.8 25.3 %collective-permute-start.12 = (bf16[2,48,1152]{2,1,0:T(8,128)(2,1)S(1)}, bf16[2,48,1152]{2,1,0:T(8,128)(2,1)S(1)}, u32[]{:S(2)}, u32[]{:S(2)}) collective-permute-start(bf16[2,48,1152]{2,1,0:T(8,128)(2,1)S(1)} %dynamic-slice_bitcast_fusion.5), channel_id=1, source_target_pairs={{0,4},{1,5},{2,6},{3,7},{4,0},{5,1},{6,2},{7,3},{8,12},{9,13},{10,... | collective-permute-start | bytes 663560 | tf_op jit(solution)/shard_map/ppermute | solution.py:929
  440.7 17.7 %copy-start.9 = (bf16[648,768]{1,0:T(8,128)(2,1)S(1)}, bf16[648,768]{1,0:T(8,128)(2,1)}, u32[]{:S(2)}) copy-start(bf16[648,768]{1,0:T(8,128)(2,1)} %get-tuple-element.104) | copy-start | bytes 2985988
  440.7 4.8 %collective-permute-start.17 = (bf16[1,48,1152]{2,1,0:T(8,128)(2,1)S(1)}, bf16[1,48,1152]{2,1,0:T(8,128)(2,1)S(1)}, u32[]{:S(2)}, u32[]{:S(2)}) collective-permute-start(bf16[1,48,1152]{2,1,0:T(8,128)(2,1)S(1)} %constant_dynamic-slice_fusion.1), channel_id=1, source_target_pairs={{0,2},{1,3},{2,0},{3,1},{4,6},{5,7},{6,4},{7,5},{8,10},{9,11},{10,... | collective-permute-start | bytes 331784 | tf_op jit(solution)/shard_map/ppermute | solution.py:929
  442.3 16.2 %copy-start.13 = (bf16[648,768]{1,0:T(8,128)(2,1)S(1)}, bf16[648,768]{1,0:T(8,128)(2,1)}, u32[]{:S(2)}) copy-start(bf16[648,768]{1,0:T(8,128)(2,1)} %get-tuple-element.102) | copy-start | bytes 2985988
  443.1 7.0 %collective-permute-start.13 = (bf16[1,48,1152]{2,1,0:T(8,128)(2,1)S(1)}, bf16[1,48,1152]{2,1,0:T(8,128)(2,1)S(1)}, u32[]{:S(2)}, u32[]{:S(2)}) collective-permute-start(bf16[1,48,1152]{2,1,0:T(8,128)(2,1)S(1)} %constant_dynamic-slice_fusion.2), channel_id=1, source_target_pairs={{0,8},{1,9},{2,10},{3,11},{4,12},{5,13},{6,14},{7,15},{8,0},{9,1},... | collective-permute-start | bytes 331784 | tf_op jit(solution)/shard_map/ppermute | solution.py:929
  445.5 6.3 %collective-permute-start.18 = (bf16[48,1152]{1,0:T(8,128)(2,1)S(1)}, bf16[48,1152]{1,0:T(8,128)(2,1)S(1)}, u32[]{:S(2)}, u32[]{:S(2)}) collective-permute-start(bf16[48,1152]{1,0:T(8,128)(2,1)S(1)} %fusion.9), channel_id=1, source_target_pairs={{0,16},{16,0},{1,17},{17,1},{2,18},{18,2},{3,19},{19,3},{4,20},{20... | collective-permute-start | bytes 331784 | tf_op jit(solution)/shard_map/ppermute | solution.py:987
  450.1 5.1 %collective-permute-start.14 = (bf16[48,1152]{1,0:T(8,128)(2,1)S(1)}, bf16[48,1152]{1,0:T(8,128)(2,1)S(1)}, u32[]{:S(2)}, u32[]{:S(2)}) collective-permute-start(bf16[48,1152]{1,0:T(8,128)(2,1)S(1)} %fusion.8), channel_id=1, source_target_pairs={{0,16},{16,0},{1,17},{17,1},{2,18},{18,2},{3,19},{19,3},{4,20},{20... | collective-permute-start | bytes 331784 | tf_op jit(solution)/shard_map/ppermute | solution.py:987
  456.5 3.4 copy-start.5
  456.5 3.4 copy-start.6
  456.5 3.4 copy-start.7
  456.5 7.3 %collective-permute-start.19 = (f32[12,768]{1,0:T(8,128)S(1)}, f32[12,768]{1,0:T(8,128)S(1)}, u32[]{:S(2)}, u32[]{:S(2)}) collective-permute-start(f32[12,768]{1,0:T(8,128)S(1)} %slice_reduce_fusion), channel_id=1, source_target_pairs={{0,16},{16,0},{1,17},{17,1},{2,18},{18,2},{3,19},{19,3},{4,20},{20... | collective-permute-start | bytes 110600 | tf_op jit(solution)/shard_map/ppermute | solution.py:987
Sparse Core Ops, SparseCore 0:
  10.9 52.9 all-gather.6
  66.1 87.1 all-gather.8
  246.4 118.3 reduce-scatter.1
  393.4 42.8 all-gather.10

commit v5 on v4

--- a/solution.py
+++ b/solution.py
@@ -805,7 +805,7 @@
     return slot
 
 
-def qkv_weight_kernel(shards, normed_ref, dq_ref, dkv_ref, out_ref, left):
+def qkv_weight_kernel(shards, parity_ref, normed_ref, dq_ref, dkv_ref, own_ref, send_ref, left):
     step = pl.program_id(0)
     width = normed_ref.shape[-1]
     rows = width // shards
@@ -813,11 +813,16 @@
     orders = halving_orders(shards)
 
     def keep(side, start, grad):
-        for shard in range(shards):
-            slot = slot_of(shard, orders[side][1:])
-            out_ref[shard % 2, side, slot, :, start : start + grad.shape[1]] = grad[
-                shard * rows : (shard + 1) * rows
-            ]
+        for parity in range(2):
+
+            @pl.when(parity_ref[0] == parity)
+            def store():
+                for shard in range(shards):
+                    ref = own_ref if shard % 2 == parity else send_ref
+                    slot = slot_of(shard, orders[side][1:])
+                    ref[side, slot, :, start : start + grad.shape[1]] = grad[
+                        shard * rows : (shard + 1) * rows
+                    ]
 
     @pl.when(step == 0)
     def query_part():
@@ -835,24 +840,25 @@
         keep(1, half, mul(left[...], dkv_ref[0]).astype(BF16))
 
 
-def qkv_weight_grad(normed, dq, dkv, shards):
+def qkv_weight_grad(parity, normed, dq, dkv, shards):
     count, width = normed.shape
-    half = (2, 2, shards // 2, width // shards, 3 * width // 2)
+    half = (2, shards // 2, width // shards, 3 * width // 2)
     return pl.pallas_call(
         functools.partial(qkv_weight_kernel, shards),
         grid=(3,),
         in_specs=[
+            pl.BlockSpec(memory_space=pltpu.SMEM),
             whole(normed.shape),
             whole(dq.shape),
             pl.BlockSpec((1, count, width), lambda s: (jnp.maximum(s - 1, 0), 0, 0)),
         ],
-        out_specs=whole(half),
-        out_shape=shaped(half, BF16),
+        out_specs=[whole(half), whole(half)],
+        out_shape=[shaped(half, BF16), shaped(half, BF16)],
         scratch_shapes=[pltpu.VMEM((width, count), BF16)],
         compiler_params=params(1),
         cost_estimate=LATE,
         name="qkv_weight_grad",
-    )(normed, dq, dkv)
+    )(parity, normed, dq, dkv)
 
 
 def input_kernel(
@@ -1059,20 +1065,26 @@
     )
     got, centre = send_back(grad_units)
     everyone = lax.all_gather(sums, "fsdp", axis=0)
-    dq, dkv, sums = lax.optimization_barrier((dq, dkv, sums))
-    sides = qkv_weight_grad(flat(normed), flat(dq), dkv.reshape(2, row_count, width), fsdp_size)
+    dq, dkv, sums, shard_pack = lax.optimization_barrier((dq, dkv, sums, shard_pack))
+    pack_got = lax.ppermute(shard_pack, "seq", swap_sides)
+    own, send = qkv_weight_grad(
+        (place % 2).astype(jnp.int32)[None],
+        flat(normed),
+        flat(dq),
+        dkv.reshape(2, row_count, width),
+        fsdp_size,
+    )
     orders = halving_orders(fsdp_size)
-    sides = halving_sum(sides, "fsdp", fsdp_size, place, [1])[0]
-    sides, shard_pack = lax.optimization_barrier((sides, shard_pack))
-    shard_pack = both(shard_pack)
+    sides = (own.astype(F32) + lax.ppermute(send, "fsdp", swap_cores).astype(F32)).astype(BF16)
     shard_sides = [
         halving_sum(value, "fsdp", fsdp_size, place, order[1:])[0]
         for value, order in zip(sides, orders)
     ]
     shard_sides = [both(value) for value in shard_sides]
-    got, centre, shard_sides, everyone = lax.optimization_barrier(
-        (got, centre, shard_sides, everyone)
-    )
+    got, centre, shard_sides, everyone, pack_got = lax.optimization_barrier(
+        (got, centre, shard_sides, everyone, pack_got)
+    )
+    shard_pack = shard_pack.astype(F32) + pack_got.astype(F32)
     input_grad = in_place(grad_units, got, centre)
     totals = both(everyone[:, : 8 + parts].sum(0))
     mine = lax.dynamic_slice_in_dim(totals[:8], place * count, count, 1)

time: 480 us -> 479 us (level)
  Pallas kernels: 299 us -> 310 us
  waiting for transfers between devices: 86.4 us -> 78.2 us
  local copies, waits for them, and re-layouts: 18.9 us -> 13.9 us
    ppermute x4 -> x3, waiting for transfers between devices: 25.6 us -> 3.95 us  [both(): lax.ppermute(value, 'seq', swap_sides).astype(F32)]
    ppermute x7 -> x6, waiting for transfers between devices: 16.3 us -> 28.8 us  [halving_sum(): lax.ppermute(lax.dynamic_index_in_dim(halves, 1 - bit, 0, False), axis, p...]
    pallas_call x1, Pallas kernels: 35.2 us -> 46.9 us  [weight_grads(): pl.pallas_call(functools.partial(weight_kernel, parts, shards), grid=(2 *...]
  transfers between devices with their start and end apart: 25 -> 25, of which waited for: 9 -> 10; matrix products, arithmetic and copies ran while one was open for 8% -> 7% of each run, Pallas kernels for 43% -> 40%
where the time goes in v5:
time: 479 us; the launch traced here: 471 us
  Pallas kernels  310 us (65%)
  waiting for transfers between devices  78.2 us (16%)
  starting transfers between devices  28.2 us (6%)
  other arithmetic  26.2 us (5%)
  between operations  14.3 us (3%)
  local copies, waits for them, and re-layouts  13.9 us (3%)
    pallas_call x2, Pallas kernels, mix_back(): pl.pallas_call(functools.partial(mix_back_kernel, unit_count), grid=(pair...  101 us
    pallas_call x2, Pallas kernels, mix(): pl.pallas_call(mix_kernel, grid=(pairs, unit_count), in_specs=[pl.BlockSp...  57.9 us
    pallas_call x1, Pallas kernels, feed(): pl.pallas_call(feed_kernel, grid=(count,), in_specs=[rows(width), rows(wi...  57.3 us
    pallas_call x1, Pallas kernels, weight_grads(): pl.pallas_call(functools.partial(weight_kernel, parts, shards), grid=(2 *...  46.9 us
    ppermute x2, waiting for transfers between devices, gather_units(): lax.ppermute(lax.dynamic_index_in_dim(values, 2 * (1 - side), 0, False),...  32.3 us
    ppermute x6, waiting for transfers between devices, halving_sum(): lax.ppermute(lax.dynamic_index_in_dim(halves, 1 - bit, 0, False), axis, p...  28.8 us
    pallas_call x1, Pallas kernels, input_grads(): pl.pallas_call(input_kernel, grid=(count,), in_specs=[rows, rows, rows, p...  17.1 us
    pallas_call x1, Pallas kernels, project(): pl.pallas_call(project_kernel, grid=(count,), in_specs=[pl.BlockSpec((1,...  14.5 us
  transfers between devices with their start and end apart: 25, of which 10 were waited for; matrix products, arithmetic and copies ran while one was open for 7% of the time, Pallas kernels for 40%

profile of v5, /device:TPU:0, one launch (start us, length us, event | category | flops | bytes accessed | tf_op | source)
XLA Modules:
  0.0 470.9 jit_solution(18072929298415164800)
XLA Ops:
  7.2 1.2 broadcast_in_dim.33.hidden_ref
  8.4 1.7 head_pack.1
  10.3 3.0 constant_dynamic-slice_fusion.4
  13.2 1.6 collective-permute-start.1
  14.9 3.3 collective-permute-start
  18.1 1.3 select_bitcast_fusion.5
  19.4 32.3 %collective-permute-done = bf16[648,768]{1,0:T(8,128)(2,1)S(1)} collective-permute-done((bf16[648,768]{1,0:T(8,128)(2,1)S(1)}, bf16[648,768]{1,0:T(8,128)(2,1)S(1)}, u32[]{:S(2)}, u32[]{:S(2)}) %collective-permute-start) | collective-permute-done | bytes 995360 | tf_op jit(solution)/shard_map/ppermute | solution.py:974
  51.8 1.9 pad_maximum_fusion.x_ref
  54.8 9.1 %all-gather.7.cloned.1.call-done = bf16[896,2304]{1,0:T(8,128)(2,1)} async-done(((bf16[56,2304]{1,0:T(8,128)(2,1)}), bf16[896,2304]{1,0:T(8,128)(2,1)}) %all-gather.7.cloned.1.call-update) | async-done | bytes 4128784 | tf_op jit(solution)/shard_map/all_gather | solution.py:1008
  65.3 14.5 %project.1 = (bf16[3,3,648,768]{3,2,1,0:T(8,128)(2,1)}, bf16[3,648,768]{2,1,0:T(8,128)(2,1)}, bf16[2,648,768]{2,1,0:T(8,128)(2,1)}) custom-call(bf16[3,648,768]{2,1,0:T(8,128)(2,1)} %pad_maximum_fusion.x_ref, bf16[16,56,2304]{2,1,0:T(8,128)(2,1)} %bitcast.120, f32[8,768]{1,0:T(8,128)} %reshape.156.vectors_ref), custom_call_target="tpu_custom_call" | custom-call | flops 6879707136 | bytes 18468864 | tf_op jit(solution)/shard_map/project/pallas_call | solution.py:363
  79.8 1.5 constant_dynamic-slice_fusion.3
  81.3 1.7 collective-permute-start.4
  83.0 2.2 collective-permute-start.3
  85.2 38.0 %mix.2 = (bf16[3,648,768]{2,1,0:T(8,128)(2,1)}, f32[2,6,8,648]{3,2,1,0:T(8,128)}) custom-call(bf16[3,3,648,768]{3,2,1,0:T(8,128)(2,1)} %get-tuple-element.75.q_ref.ka_ref.va_ref.kb_ref.vb_ref, bf16[3,3,648,768]{3,2,1,0:T(8,128)(2,1)} %get-tuple-element.75.q_ref.ka_ref.va_ref.kb_ref.vb_ref, ...), custom_call_target="tpu_custom_call" | custom-call | flops 20639121408 | bytes 7962624 | tf_op jit(solution)/shard_map/mix/pallas_call | solution.py:463
  124.8 1.3 select_bitcast_fusion.4
  126.1 3.1 pad_maximum_fusion.1.cot_ref
  129.2 1.3 copy-done
  130.5 19.9 %mix.3 = (bf16[3,648,768]{2,1,0:T(8,128)(2,1)}, f32[1,6,8,648]{3,2,1,0:T(8,128)}) custom-call(bf16[3,3,648,768]{3,2,1,0:T(8,128)(2,1)} %get-tuple-element.75.q_ref.ka_ref.va_ref.kb_ref.vb_ref, bf16[3,3,648,768]{3,2,1,0:T(8,128)(2,1)} %get-tuple-element.75.q_ref.ka_ref.va_ref.kb_ref.vb_ref, ...), custom_call_target="tpu_custom_call", output_to_operand_aliasing={{0}: (5, {})} | custom-call | flops 10319560704 | bytes 3981312 | tf_op jit(solution)/shard_map/mix/pallas_call | solution.py:463
  150.4 2.9 all-gather.9.cloned.1.call-done
  153.3 57.3 %feed.1 = (bf16[3,648,768]{2,1,0:T(8,128)(2,1)}, bf16[3,648,768]{2,1,0:T(8,128)(2,1)}, bf16[3,648,768]{2,1,0:T(8,128)(2,1)}, bf16[3,648,3072]{2,1,0:T(8,128)(2,1...) custom-call(bf16[3,648,768]{2,1,0:T(8,128)(2,1)} %pad_maximum_fusion.x_r, ...), custom_call_target="tpu_custom_call" | custom-call | flops 41278242816 | bytes 53747712 | tf_op jit(solution)/shard_map/feed/pallas_call | solution.py:693
  210.7 46.9 %weight_grads.1 = bf16[16,432,768]{2,1,0:T(8,128)(2,1)} custom-call(bf16[1944,768]{1,0:T(8,128)(2,1)} %bitcast.149, bf16[1944,3072]{1,0:T(8,128)(2,1)} %bitcast.148, bf16[1944,3072]{1,0:T(8,128)(2,1)} %bitcast.147, bf16[1944,768]{1,0:T(8,128)(2,1)} %bitcast.129, bf16[1944,768]{1,0:T(8,128)(2,1)} %bitcast.114, bf16[1944,768]{1,0:T(8,128)(2,1)} %bitcast.128), custom_call_target="tpu_custom_call" | custom-call | flops 20639121408 | bytes 35831808 | tf_op jit(solution)/shard_map/weight_grads/pallas_call | solution.py:772
  257.6 33.8 %mix_back.2 = (bf16[3,648,768]{2,1,0:T(8,128)(2,1)}, bf16[2,1,648,768]{3,2,1,0:T(8,128)(2,1)}, bf16[2,1,648,768]{3,2,1,0:T(8,128)(2,1)}) custom-call(bf16[3,3,648,768]{3,2,1,0:T(8,128)(2,1)} %get-tuple-element.75.q_ref.ka_ref.va_ref.kb_ref.vb_ref, bf16[3,3,648,768]{3,2,1,0:T(8,128)(2,1)} %get-tuple-element.75.q_ref.ka_ref.va_ref.kb_ref.vb_ref, ...), custom_call_target="tpu_custom_call" | custom-call | flops 1000 | bytes 1000 | tf_op jit(solution)/shard_map/mix_back/pallas_call | solution.py:579
  291.7 1.4 slice_bitcast_fusion
  293.1 1.5 collective-permute-start.6
  294.6 1.6 collective-permute-start.7
  296.2 67.0 %mix_back.3 = (bf16[3,648,768]{2,1,0:T(8,128)(2,1)}, bf16[2,3,648,768]{3,2,1,0:T(8,128)(2,1)}, f32[8,128]{1,0:T(8,128)}) custom-call(bf16[3,3,648,768]{3,2,1,0:T(8,128)(2,1)} %get-tuple-element.75.q_ref.ka_ref.va_ref.kb_ref.vb_ref, bf16[3,3,648,768]{3,2,1,0:T(8,128)(2,1)} %get-tuple-element.75.q_ref.ka_ref.va_ref.kb_ref.vb_ref, ...), custom_call_target="tpu_custom_call", output_to_operand_aliasing={{0}: (8, {})} | custom-call | flops 1000 | bytes 1000 | tf_op jit(solution)/shard_map/mix_back/pallas_call | solution.py:579
  363.2 4.0 fusion.dkv_ref
  367.2 17.1 %input_grads.1 = (bf16[648,768]{1,0:T(8,128)(2,1)}, bf16[648,768]{1,0:T(8,128)(2,1)}, bf16[648,768]{1,0:T(8,128)(2,1)}, f32[32,768]{1,0:T(8,128)}) custom-call(bf16[3,648,768]{2,1,0:T(8,128)(2,1)} %pad_maximum_fusion.x_ref, bf16[3,648,768]{2,1,0:T(8,128)(2,1)} %get-tuple-element.89.dx_ref, bf16[3,648,768]{2,1,0:T(8,128)(2,1)} %get-tuple-element.110.dq_ref, ...), custom_call_target="tpu_custom_call" | custom-call | flops 1000 | bytes 1000 | tf_op jit(solution)/shard_map/input_grads/pallas_call | solution.py:909
  384.4 14.0 %qkv_weight_grad.1 = (bf16[2,8,48,1152]{3,2,1,0:T(8,128)(2,1)}, bf16[2,8,48,1152]{3,2,1,0:T(8,128)(2,1)}) custom-call(s32[1]{0:T(128)} %bitcast.32.parity_ref, bf16[1944,768]{1,0:T(8,128)(2,1)} %bitcast.127, bf16[1944,768]{1,0:T(8,128)(2,1)} %bitcast.112, bf16[2,1944,768]{2,1,0:T(8,128)(2,1)} %bitcast.113), custom_call_target="tpu_custom_call" | custom-call | flops 1000 | bytes 1000 | tf_op jit(solution)/shard_map/qkv_weight_grad/pallas_call | solution.py:846
  400.3 1.6 collective-permute-start.9
  402.9 2.5 add_convert_fusion.1
  406.1 1.4 fusion.1
  407.5 1.9 pad_maximum_fusion.2
  409.5 1.7 collective-permute-start.19
  411.9 9.0 %collective-permute-done.15 = bf16[4,48,1152]{2,1,0:T(8,128)(2,1)S(1)} collective-permute-done((bf16[4,48,1152]{2,1,0:T(8,128)(2,1)S(1)}, bf16[4,48,1152]{2,1,0:T(8,128)(2,1)S(1)}, u32[]{:S(2)}, u32[]{:S(2)}) %collective-permute-start.15) | collective-permute-done | bytes 442400 | tf_op jit(solution)/shard_map/ppermute | solution.py:935
  421.0 2.1 collective-permute-start.16
  423.3 1.1 collective-permute-start.12
  424.4 14.7 %collective-permute-done.16 = bf16[2,48,1152]{2,1,0:T(8,128)(2,1)S(1)} collective-permute-done((bf16[2,48,1152]{2,1,0:T(8,128)(2,1)S(1)}, bf16[2,48,1152]{2,1,0:T(8,128)(2,1)S(1)}, u32[]{:S(2)}, u32[]{:S(2)}) %collective-permute-start.16) | collective-permute-done | bytes 221216 | tf_op jit(solution)/shard_map/ppermute | solution.py:935
  439.2 2.3 collective-permute-start.17
  441.6 2.8 collective-permute-done.17
  444.5 1.3 collective-permute-start.18
  445.8 2.3 collective-permute-done.13
  449.1 1.7 collective-permute-done.18
  450.9 2.3 collective-permute-done.14
  453.2 1.4 convert_add_fusion
  455.4 1.6 collective-permute-start.20
  457.8 1.5 select_bitcast_fusion.2
  460.1 1.9 pad_maximum_fusion.3
  (91 shorter events, 15.0 us)
Async XLA Ops:
  7.2 56.7 %all-gather.7.cloned.1.call-start = ((), (), s32[]{:S(2)}) async-start(), calls=%async_computation.2 | async-start | bytes 4386816 | tf_op jit(solution)/shard_map/all_gather | solution.py:1008
  10.2 143.1 %all-gather.9.cloned.1.call-start = ((), (), s32[]{:S(2)}) async-start(), calls=%async_computation.3 | async-start | bytes 11280384 | tf_op jit(solution)/shard_map/all_gather | solution.py:1018
  13.2 4.9 %collective-permute-start.1 = (bf16[648,768]{1,0:T(8,128)(2,1)}, bf16[648,768]{1,0:T(8,128)(2,1)}, u32[]{:S(2)}, u32[]{:S(2)}) collective-permute-start(bf16[648,768]{1,0:T(8,128)(2,1)} %get-tuple-element.130), channel_id=1, source_target_pairs={{16,1},{1,16},{18,3},{3,18},{20,5},{5,20},{22,7},{7,22},{24,9},{9,... | collective-permute-start | bytes 2985992 | tf_op jit(solution)/shard_map/ppermute | solution.py:971
  14.9 36.9 %collective-permute-start = (bf16[648,768]{1,0:T(8,128)(2,1)S(1)}, bf16[648,768]{1,0:T(8,128)(2,1)S(1)}, u32[]{:S(2)}, u32[]{:S(2)}) collective-permute-start(bf16[648,768]{1,0:T(8,128)(2,1)S(1)} %get-tuple-element.131), channel_id=1, source_target_pairs={{0,16},{16,0},{1,17},{17,1},{2,18},{18,2},{3,19},{19,3},{4,20},{20... | collective-permute-start | bytes 2985992 | tf_op jit(solution)/shard_map/ppermute | solution.py:974
  51.8 1.9 copy-start.8
  51.8 2.0 copy-start.9
  51.8 2.0 copy-start.10
  53.9 0.8 copy-start.5
  54.7 329.6 %reduce-scatter.2.cloned.1.call-start = ((), (), s32[]{:S(2)}) async-start(), calls=%async_computation.1 | async-start | bytes 11280384 | tf_op jit(solution)/shard_map/reduce_scatter | solution.py:1056
  65.3 14.5 %copy-start.1 = (bf16[3,648,768]{2,1,0:T(8,128)(2,1)S(1)}, bf16[3,648,768]{2,1,0:T(8,128)(2,1)}, u32[]{:S(2)}) copy-start(bf16[3,648,768]{2,1,0:T(8,128)(2,1)} %param.18) | copy-start | bytes 8957956
  81.3 43.4 %collective-permute-start.4 = (bf16[648,768]{1,0:T(8,128)(2,1)}, bf16[648,768]{1,0:T(8,128)(2,1)}, u32[]{:S(2)}, u32[]{:S(2)}) collective-permute-start(bf16[648,768]{1,0:T(8,128)(2,1)} %get-tuple-element.127), channel_id=1, source_target_pairs={{16,1},{1,16},{18,3},{3,18},{20,5},{5,20},{22,7},{7,22},{24,9},{9,... | collective-permute-start | bytes 2985992 | tf_op jit(solution)/shard_map/ppermute | solution.py:971
  83.0 43.1 %collective-permute-start.3 = (bf16[648,768]{1,0:T(8,128)(2,1)}, bf16[648,768]{1,0:T(8,128)(2,1)}, u32[]{:S(2)}, u32[]{:S(2)}) collective-permute-start(bf16[648,768]{1,0:T(8,128)(2,1)} %get-tuple-element.128), channel_id=1, source_target_pairs={{0,16},{16,0},{1,17},{17,1},{2,18},{18,2},{3,19},{19,3},{4,20},{20... | collective-permute-start | bytes 2985992 | tf_op jit(solution)/shard_map/ppermute | solution.py:974
  85.2 44.0 %collective-permute-start.2 = (bf16[2,648,768]{2,1,0:T(8,128)(2,1)}, bf16[2,648,768]{2,1,0:T(8,128)(2,1)S(1)}, u32[]{:S(2)}, u32[]{:S(2)}) collective-permute-start(bf16[2,648,768]{2,1,0:T(8,128)(2,1)} %get-tuple-element.77), channel_id=1, source_target_pairs={{0,1},{1,0},{2,3},{3,2},{4,5},{5,4},{6,7},{7,6},{8,9},{9,8},{10,11... | collective-permute-start | bytes 5971976 | tf_op jit(solution)/shard_map/ppermute | solution.py:1025
  129.2 1.3 copy-start
  257.6 195.7 %all-gather.11.cloned.1.call-start = ((), (), s32[]{:S(2)}) async-start(), calls=%async_computation.4 | async-start | bytes 1671168 | tf_op jit(solution)/shard_map/all_gather | solution.py:1067
  257.6 34.1 %copy-start.2 = (bf16[3,648,768]{2,1,0:T(8,128)(2,1)S(1)}, bf16[3,648,768]{2,1,0:T(8,128)(2,1)}, u32[]{:S(2)}) copy-start(bf16[3,648,768]{2,1,0:T(8,128)(2,1)} %get-tuple-element.84) | copy-start | bytes 8957956
  291.4 71.8 %collective-permute-start.5 = (bf16[2,1,648,768]{3,2,1,0:T(8,128)(2,1)}, bf16[2,1,648,768]{3,2,1,0:T(8,128)(2,1)}, u32[]{:S(2)}, u32[]{:S(2)}) collective-permute-start(bf16[2,1,648,768]{3,2,1,0:T(8,128)(2,1)} %get-tuple-element.97), channel_id=1, source_target_pairs={{0,1},{1,0},{2,3},{3,2},{4,5},{5,4},{6,7},{7,6},{8,9},{9,8},{10,11... | collective-permute-start | bytes 5971976 | tf_op jit(solution)/shard_map/ppermute | solution.py:1058
  293.1 74.2 %collective-permute-start.6 = (bf16[648,768]{1,0:T(8,128)(2,1)}, bf16[648,768]{1,0:T(8,128)(2,1)}, u32[]{:S(2)}, u32[]{:S(2)}) collective-permute-start(bf16[648,768]{1,0:T(8,128)(2,1)} %get-tuple-element.125), channel_id=1, source_target_pairs={{0,16},{16,0},{1,17},{17,1},{2,18},{18,2},{3,19},{19,3},{4,20},{20... | collective-permute-start | bytes 2985992 | tf_op jit(solution)/shard_map/ppermute | solution.py:982
  294.6 72.7 %collective-permute-start.7 = (bf16[648,768]{1,0:T(8,128)(2,1)}, bf16[648,768]{1,0:T(8,128)(2,1)}, u32[]{:S(2)}, u32[]{:S(2)}) collective-permute-start(bf16[648,768]{1,0:T(8,128)(2,1)} %get-tuple-element.124), channel_id=1, source_target_pairs={{16,1},{1,16},{18,3},{3,18},{20,5},{5,20},{22,7},{7,22},{24,9},{9,... | collective-permute-start | bytes 2985992 | tf_op jit(solution)/shard_map/ppermute | solution.py:983
  398.4 4.6 collective-permute-start.10
  399.3 53.9 %collective-permute-start.8 = (bf16[648,768]{1,0:T(8,128)(2,1)}, bf16[648,768]{1,0:T(8,128)(2,1)}, u32[]{:S(2)}, u32[]{:S(2)}) collective-permute-start(bf16[648,768]{1,0:T(8,128)(2,1)} %get-tuple-element.105), channel_id=1, source_target_pairs={{0,16},{16,0},{1,17},{17,1},{2,18},{18,2},{3,19},{19,3},{4,20},{20... | collective-permute-start | bytes 2985992 | tf_op jit(solution)/shard_map/ppermute | solution.py:982
  400.3 52.8 %collective-permute-start.9 = (bf16[648,768]{1,0:T(8,128)(2,1)}, bf16[648,768]{1,0:T(8,128)(2,1)}, u32[]{:S(2)}, u32[]{:S(2)}) collective-permute-start(bf16[648,768]{1,0:T(8,128)(2,1)} %get-tuple-element.106), channel_id=1, source_target_pairs={{16,1},{1,16},{18,3},{3,18},{20,5},{5,20},{22,7},{7,22},{24,9},{9,... | collective-permute-start | bytes 2985992 | tf_op jit(solution)/shard_map/ppermute | solution.py:983
  405.6 15.3 %collective-permute-start.15 = (bf16[4,48,1152]{2,1,0:T(8,128)(2,1)S(1)}, bf16[4,48,1152]{2,1,0:T(8,128)(2,1)S(1)}, u32[]{:S(2)}, u32[]{:S(2)}) collective-permute-start(bf16[4,48,1152]{2,1,0:T(8,128)(2,1)S(1)} %dynamic-slice_bitcast_fusion.2), channel_id=1, source_target_pairs={{0,4},{1,5},{2,6},{3,7},{4,0},{5,1},{6,2},{7,3},{8,12},{9,13},{10,... | collective-permute-start | bytes 1327112 | tf_op jit(solution)/shard_map/ppermute | solution.py:935
  407.5 1.9 copy-start.6
  409.5 43.8 %collective-permute-start.19 = (bf16[432,768]{1,0:T(8,128)(2,1)S(1)}, bf16[432,768]{1,0:T(8,128)(2,1)}, u32[]{:S(2)}, u32[]{:S(2)}) collective-permute-start(bf16[432,768]{1,0:T(8,128)(2,1)S(1)} %bitcast.135), channel_id=1, source_target_pairs={{0,16},{16,0},{1,17},{17,1},{2,18},{18,2},{3,19},{19,3},{4,20},{20... | collective-permute-start | bytes 1990664 | tf_op jit(solution)/shard_map/ppermute | solution.py:1069
  411.2 11.9 %collective-permute-start.11 = (bf16[4,48,1152]{2,1,0:T(8,128)(2,1)S(1)}, bf16[4,48,1152]{2,1,0:T(8,128)(2,1)S(1)}, u32[]{:S(2)}, u32[]{:S(2)}) collective-permute-start(bf16[4,48,1152]{2,1,0:T(8,128)(2,1)S(1)} %dynamic-slice_bitcast_fusion.3), channel_id=1, source_target_pairs={{0,2},{1,3},{2,0},{3,1},{4,6},{5,7},{6,4},{7,5},{8,10},{9,11},{10,... | collective-permute-start | bytes 1327112 | tf_op jit(solution)/shard_map/ppermute | solution.py:935
  421.0 18.1 %collective-permute-start.16 = (bf16[2,48,1152]{2,1,0:T(8,128)(2,1)S(1)}, bf16[2,48,1152]{2,1,0:T(8,128)(2,1)S(1)}, u32[]{:S(2)}, u32[]{:S(2)}) collective-permute-start(bf16[2,48,1152]{2,1,0:T(8,128)(2,1)S(1)} %dynamic-slice_bitcast_fusion.4), channel_id=1, source_target_pairs={{0,8},{1,9},{2,10},{3,11},{4,12},{5,13},{6,14},{7,15},{8,0},{9,1},... | collective-permute-start | bytes 663560 | tf_op jit(solution)/shard_map/ppermute | solution.py:935
  423.3 18.2 %collective-permute-start.12 = (bf16[2,48,1152]{2,1,0:T(8,128)(2,1)S(1)}, bf16[2,48,1152]{2,1,0:T(8,128)(2,1)S(1)}, u32[]{:S(2)}, u32[]{:S(2)}) collective-permute-start(bf16[2,48,1152]{2,1,0:T(8,128)(2,1)S(1)} %dynamic-slice_bitcast_fusion.5), channel_id=1, source_target_pairs={{0,4},{1,5},{2,6},{3,7},{4,0},{5,1},{6,2},{7,3},{8,12},{9,13},{10,... | collective-permute-start | bytes 663560 | tf_op jit(solution)/shard_map/ppermute | solution.py:935
  439.2 5.3 %collective-permute-start.17 = (bf16[1,48,1152]{2,1,0:T(8,128)(2,1)S(1)}, bf16[1,48,1152]{2,1,0:T(8,128)(2,1)S(1)}, u32[]{:S(2)}, u32[]{:S(2)}) collective-permute-start(bf16[1,48,1152]{2,1,0:T(8,128)(2,1)S(1)} %constant_dynamic-slice_fusion.1), channel_id=1, source_target_pairs={{0,2},{1,3},{2,0},{3,1},{4,6},{5,7},{6,4},{7,5},{8,10},{9,11},{10,... | collective-permute-start | bytes 331784 | tf_op jit(solution)/shard_map/ppermute | solution.py:935
  441.6 6.6 %collective-permute-start.13 = (bf16[1,48,1152]{2,1,0:T(8,128)(2,1)S(1)}, bf16[1,48,1152]{2,1,0:T(8,128)(2,1)S(1)}, u32[]{:S(2)}, u32[]{:S(2)}) collective-permute-start(bf16[1,48,1152]{2,1,0:T(8,128)(2,1)S(1)} %constant_dynamic-slice_fusion.2), channel_id=1, source_target_pairs={{0,8},{1,9},{2,10},{3,11},{4,12},{5,13},{6,14},{7,15},{8,0},{9,1},... | collective-permute-start | bytes 331784 | tf_op jit(solution)/shard_map/ppermute | solution.py:935
  444.5 6.4 %collective-permute-start.18 = (bf16[48,1152]{1,0:T(8,128)(2,1)S(1)}, bf16[48,1152]{1,0:T(8,128)(2,1)S(1)}, u32[]{:S(2)}, u32[]{:S(2)}) collective-permute-start(bf16[48,1152]{1,0:T(8,128)(2,1)S(1)} %fusion.8), channel_id=1, source_target_pairs={{0,16},{16,0},{1,17},{17,1},{2,18},{18,2},{3,19},{19,3},{4,20},{20... | collective-permute-start | bytes 331784 | tf_op jit(solution)/shard_map/ppermute | solution.py:993
  448.2 5.0 %collective-permute-start.14 = (bf16[48,1152]{1,0:T(8,128)(2,1)S(1)}, bf16[48,1152]{1,0:T(8,128)(2,1)S(1)}, u32[]{:S(2)}, u32[]{:S(2)}) collective-permute-start(bf16[48,1152]{1,0:T(8,128)(2,1)S(1)} %fusion.7), channel_id=1, source_target_pairs={{0,16},{16,0},{1,17},{17,1},{2,18},{18,2},{3,19},{19,3},{4,20},{20... | collective-permute-start | bytes 331784 | tf_op jit(solution)/shard_map/ppermute | solution.py:993
  453.2 4.6 copy-start.3
  453.2 4.6 copy-start.4
  453.2 2.1 copy-start.7
  455.4 7.5 %collective-permute-start.20 = (f32[12,768]{1,0:T(8,128)S(1)}, f32[12,768]{1,0:T(8,128)S(1)}, u32[]{:S(2)}, u32[]{:S(2)}) collective-permute-start(f32[12,768]{1,0:T(8,128)S(1)} %slice_reduce_fusion), channel_id=1, source_target_pairs={{0,16},{16,0},{1,17},{17,1},{2,18},{18,2},{3,19},{19,3},{4,20},{20... | collective-permute-start | bytes 110600 | tf_op jit(solution)/shard_map/ppermute | solution.py:993
Sparse Core Ops, SparseCore 0:
  10.9 52.9 all-gather.6
  66.1 87.1 all-gather.8
  257.7 118.3 reduce-scatter.1
  399.4 42.4 all-gather.10

commit v6 on v5

--- a/solution.py
+++ b/solution.py
@@ -1065,8 +1065,7 @@
     )
     got, centre = send_back(grad_units)
     everyone = lax.all_gather(sums, "fsdp", axis=0)
-    dq, dkv, sums, shard_pack = lax.optimization_barrier((dq, dkv, sums, shard_pack))
-    pack_got = lax.ppermute(shard_pack, "seq", swap_sides)
+    dq, dkv, sums = lax.optimization_barrier((dq, dkv, sums))
     own, send = qkv_weight_grad(
         (place % 2).astype(jnp.int32)[None],
         flat(normed),
@@ -1076,6 +1075,8 @@
     )
     orders = halving_orders(fsdp_size)
     sides = (own.astype(F32) + lax.ppermute(send, "fsdp", swap_cores).astype(F32)).astype(BF16)
+    sides, shard_pack = lax.optimization_barrier((sides, shard_pack))
+    pack_got = lax.ppermute(shard_pack, "seq", swap_sides)
     shard_sides = [
         halving_sum(value, "fsdp", fsdp_size, place, order[1:])[0]
         for value, order in zip(sides, orders)

time: 479 us -> 478 us (level)
  starting transfers between devices: 28.2 us -> 23 us
  transfers between devices with their start and end apart: 25 -> 25, of which waited for: 10 -> 11; matrix products, arithmetic and copies ran while one was open for 7% -> 7% of each run, Pallas kernels for 40% -> 44%
where the time goes in v6:
time: 478 us; the launch traced here: 469 us
  Pallas kernels  311 us (65%)
  waiting for transfers between devices  82.2 us (17%)
  starting transfers between devices  23 us (5%)
  other arithmetic  22.8 us (5%)
  local copies, waits for them, and re-layouts  15.8 us (3%)
  between operations  14.4 us (3%)
    pallas_call x2, Pallas kernels, mix_back(): pl.pallas_call(functools.partial(mix_back_kernel, unit_count), grid=(pair...  101 us
    pallas_call x2, Pallas kernels, mix(): pl.pallas_call(mix_kernel, grid=(pairs, unit_count), in_specs=[pl.BlockSp...  57.9 us
    pallas_call x1, Pallas kernels, feed(): pl.pallas_call(feed_kernel, grid=(count,), in_specs=[rows(width), rows(wi...  57.4 us
    pallas_call x1, Pallas kernels, weight_grads(): pl.pallas_call(functools.partial(weight_kernel, parts, shards), grid=(2 *...  46.8 us
    ppermute x2, waiting for transfers between devices, gather_units(): lax.ppermute(lax.dynamic_index_in_dim(values, 2 * (1 - side), 0, False),...  32.3 us
    ppermute x6, waiting for transfers between devices, halving_sum(): lax.ppermute(lax.dynamic_index_in_dim(halves, 1 - bit, 0, False), axis, p...  30.6 us
    pallas_call x1, Pallas kernels, input_grads(): pl.pallas_call(input_kernel, grid=(count,), in_specs=[rows, rows, rows, p...  17.7 us
    pallas_call x1, Pallas kernels, project(): pl.pallas_call(project_kernel, grid=(count,), in_specs=[pl.BlockSpec((1,...  14.4 us
  transfers between devices with their start and end apart: 25, of which 11 were waited for; matrix products, arithmetic and copies ran while one was open for 7% of the time, Pallas kernels for 44%

profile of v6, /device:TPU:0, one launch (start us, length us, event | category | flops | bytes accessed | tf_op | source)
XLA Modules:
  0.0 469.1 jit_solution(13848432255571767890)
XLA Ops:
  7.2 1.2 broadcast_in_dim.33.hidden_ref
  8.4 1.7 head_pack.1
  10.3 3.0 constant_dynamic-slice_fusion.4
  13.2 1.6 collective-permute-start.1
  14.9 3.3 collective-permute-start
  18.1 1.3 select_bitcast_fusion.5
  19.4 32.3 %collective-permute-done = bf16[648,768]{1,0:T(8,128)(2,1)S(1)} collective-permute-done((bf16[648,768]{1,0:T(8,128)(2,1)S(1)}, bf16[648,768]{1,0:T(8,128)(2,1)S(1)}, u32[]{:S(2)}, u32[]{:S(2)}) %collective-permute-start) | collective-permute-done | bytes 995360 | tf_op jit(solution)/shard_map/ppermute | solution.py:974
  51.8 1.9 pad_maximum_fusion.x_ref
  54.8 9.1 %all-gather.7.cloned.1.call-done = bf16[896,2304]{1,0:T(8,128)(2,1)} async-done(((bf16[56,2304]{1,0:T(8,128)(2,1)}), bf16[896,2304]{1,0:T(8,128)(2,1)}) %all-gather.7.cloned.1.call-update) | async-done | bytes 4128784 | tf_op jit(solution)/shard_map/all_gather | solution.py:1008
  65.3 14.4 %project.1 = (bf16[3,3,648,768]{3,2,1,0:T(8,128)(2,1)}, bf16[3,648,768]{2,1,0:T(8,128)(2,1)}, bf16[2,648,768]{2,1,0:T(8,128)(2,1)}) custom-call(bf16[3,648,768]{2,1,0:T(8,128)(2,1)} %pad_maximum_fusion.x_ref, bf16[16,56,2304]{2,1,0:T(8,128)(2,1)} %bitcast.120, f32[8,768]{1,0:T(8,128)} %reshape.156.vectors_ref), custom_call_target="tpu_custom_call" | custom-call | flops 6879707136 | bytes 18468864 | tf_op jit(solution)/shard_map/project/pallas_call | solution.py:363
  79.8 1.5 constant_dynamic-slice_fusion.3
  81.3 1.6 collective-permute-start.4
  82.9 2.2 collective-permute-start.3
  85.1 38.0 %mix.2 = (bf16[3,648,768]{2,1,0:T(8,128)(2,1)}, f32[2,6,8,648]{3,2,1,0:T(8,128)}) custom-call(bf16[3,3,648,768]{3,2,1,0:T(8,128)(2,1)} %get-tuple-element.76.q_ref.ka_ref.va_ref.kb_ref.vb_ref, bf16[3,3,648,768]{3,2,1,0:T(8,128)(2,1)} %get-tuple-element.76.q_ref.ka_ref.va_ref.kb_ref.vb_ref, ...), custom_call_target="tpu_custom_call" | custom-call | flops 20639121408 | bytes 7962624 | tf_op jit(solution)/shard_map/mix/pallas_call | solution.py:463
  123.2 0.9 fusion.9
  124.7 1.3 select_bitcast_fusion.4
  126.0 3.1 pad_maximum_fusion.1.cot_ref
  129.2 1.3 copy-done
  130.5 19.9 %mix.3 = (bf16[3,648,768]{2,1,0:T(8,128)(2,1)}, f32[1,6,8,648]{3,2,1,0:T(8,128)}) custom-call(bf16[3,3,648,768]{3,2,1,0:T(8,128)(2,1)} %get-tuple-element.76.q_ref.ka_ref.va_ref.kb_ref.vb_ref, bf16[3,3,648,768]{3,2,1,0:T(8,128)(2,1)} %get-tuple-element.76.q_ref.ka_ref.va_ref.kb_ref.vb_ref, ...), custom_call_target="tpu_custom_call", output_to_operand_aliasing={{0}: (5, {})} | custom-call | flops 10319560704 | bytes 3981312 | tf_op jit(solution)/shard_map/mix/pallas_call | solution.py:463
  150.4 3.0 all-gather.9.cloned.1.call-done
  153.3 57.4 %feed.1 = (bf16[3,648,768]{2,1,0:T(8,128)(2,1)}, bf16[3,648,768]{2,1,0:T(8,128)(2,1)}, bf16[3,648,768]{2,1,0:T(8,128)(2,1)}, bf16[3,648,3072]{2,1,0:T(8,128)(2,1...) custom-call(bf16[3,648,768]{2,1,0:T(8,128)(2,1)} %pad_maximum_fusion.x_r, ...), custom_call_target="tpu_custom_call" | custom-call | flops 41278242816 | bytes 53747712 | tf_op jit(solution)/shard_map/feed/pallas_call | solution.py:693
  210.8 46.8 %weight_grads.1 = bf16[16,432,768]{2,1,0:T(8,128)(2,1)} custom-call(bf16[1944,768]{1,0:T(8,128)(2,1)} %bitcast.149, bf16[1944,3072]{1,0:T(8,128)(2,1)} %bitcast.148, bf16[1944,3072]{1,0:T(8,128)(2,1)} %bitcast.147, bf16[1944,768]{1,0:T(8,128)(2,1)} %bitcast.129, bf16[1944,768]{1,0:T(8,128)(2,1)} %bitcast.114, bf16[1944,768]{1,0:T(8,128)(2,1)} %bitcast.128), custom_call_target="tpu_custom_call" | custom-call | flops 20639121408 | bytes 35831808 | tf_op jit(solution)/shard_map/weight_grads/pallas_call | solution.py:772
  257.7 33.8 %mix_back.2 = (bf16[3,648,768]{2,1,0:T(8,128)(2,1)}, bf16[2,1,648,768]{3,2,1,0:T(8,128)(2,1)}, bf16[2,1,648,768]{3,2,1,0:T(8,128)(2,1)}) custom-call(bf16[3,3,648,768]{3,2,1,0:T(8,128)(2,1)} %get-tuple-element.76.q_ref.ka_ref.va_ref.kb_ref.vb_ref, bf16[3,3,648,768]{3,2,1,0:T(8,128)(2,1)} %get-tuple-element.76.q_ref.ka_ref.va_ref.kb_ref.vb_ref, ...), custom_call_target="tpu_custom_call" | custom-call | flops 1000 | bytes 1000 | tf_op jit(solution)/shard_map/mix_back/pallas_call | solution.py:579
  291.7 1.4 slice_bitcast_fusion
  293.1 1.4 collective-permute-start.6
  295.3 67.2 %mix_back.3 = (bf16[3,648,768]{2,1,0:T(8,128)(2,1)}, bf16[2,3,648,768]{3,2,1,0:T(8,128)(2,1)}, f32[8,128]{1,0:T(8,128)}) custom-call(bf16[3,3,648,768]{3,2,1,0:T(8,128)(2,1)} %get-tuple-element.76.q_ref.ka_ref.va_ref.kb_ref.vb_ref, bf16[3,3,648,768]{3,2,1,0:T(8,128)(2,1)} %get-tuple-element.76.q_ref.ka_ref.va_ref.kb_ref.vb_ref, ...), custom_call_target="tpu_custom_call", output_to_operand_aliasing={{0}: (8, {})} | custom-call | flops 1000 | bytes 1000 | tf_op jit(solution)/shard_map/mix_back/pallas_call | solution.py:579
  362.4 3.4 fusion.dkv_ref
  365.9 17.7 %input_grads.1 = (bf16[648,768]{1,0:T(8,128)(2,1)}, bf16[648,768]{1,0:T(8,128)(2,1)}, bf16[648,768]{1,0:T(8,128)(2,1)}, f32[32,768]{1,0:T(8,128)}) custom-call(bf16[3,648,768]{2,1,0:T(8,128)(2,1)} %pad_maximum_fusion.x_ref, bf16[3,648,768]{2,1,0:T(8,128)(2,1)} %get-tuple-element.90.dx_ref, bf16[3,648,768]{2,1,0:T(8,128)(2,1)} %get-tuple-element.110.dq_ref, ...), custom_call_target="tpu_custom_call" | custom-call | flops 1000 | bytes 1000 | tf_op jit(solution)/shard_map/input_grads/pallas_call | solution.py:909
  383.6 14.0 %qkv_weight_grad.1 = (bf16[2,8,48,1152]{3,2,1,0:T(8,128)(2,1)}, bf16[2,8,48,1152]{3,2,1,0:T(8,128)(2,1)}) custom-call(s32[1]{0:T(128)} %bitcast.32.parity_ref, bf16[1944,768]{1,0:T(8,128)(2,1)} %bitcast.127, bf16[1944,768]{1,0:T(8,128)(2,1)} %bitcast.112, bf16[2,1944,768]{2,1,0:T(8,128)(2,1)} %bitcast.113), custom_call_target="tpu_custom_call" | custom-call | flops 1000 | bytes 1000 | tf_op jit(solution)/shard_map/qkv_weight_grad/pallas_call | solution.py:846
  397.6 1.8 collective-permute-start.10
  399.4 1.0 collective-permute-start.8
  400.4 1.6 collective-permute-start.9
  402.0 0.9 collective-permute-done.10
  402.9 1.9 add_convert_fusion.1
  406.0 1.0 copy-done.3
  407.2 1.9 pad_maximum_fusion.2
  409.8 2.5 collective-permute-start.19
  412.4 7.8 %collective-permute-done.15 = bf16[4,48,1152]{2,1,0:T(8,128)(2,1)S(1)} collective-permute-done((bf16[4,48,1152]{2,1,0:T(8,128)(2,1)S(1)}, bf16[4,48,1152]{2,1,0:T(8,128)(2,1)S(1)}, u32[]{:S(2)}, u32[]{:S(2)}) %collective-permute-start.15) | collective-permute-done | bytes 442400 | tf_op jit(solution)/shard_map/ppermute | solution.py:935
  420.4 2.1 collective-permute-start.16
  422.6 1.1 collective-permute-start.12
  423.7 13.2 %collective-permute-done.16 = bf16[2,48,1152]{2,1,0:T(8,128)(2,1)S(1)} collective-permute-done((bf16[2,48,1152]{2,1,0:T(8,128)(2,1)S(1)}, bf16[2,48,1152]{2,1,0:T(8,128)(2,1)S(1)}, u32[]{:S(2)}, u32[]{:S(2)}) %collective-permute-start.16) | collective-permute-done | bytes 221216 | tf_op jit(solution)/shard_map/ppermute | solution.py:935
  437.1 3.3 collective-permute-done.12
  440.6 1.5 collective-permute-done.17
  442.1 4.8 %collective-permute-done.13 = bf16[1,48,1152]{2,1,0:T(8,128)(2,1)S(1)} collective-permute-done((bf16[1,48,1152]{2,1,0:T(8,128)(2,1)S(1)}, bf16[1,48,1152]{2,1,0:T(8,128)(2,1)S(1)}, u32[]{:S(2)}, u32[]{:S(2)}) %collective-permute-start.13) | collective-permute-done | bytes 110624 | tf_op jit(solution)/shard_map/ppermute | solution.py:935
  447.0 5.0 %collective-permute-done.18 = bf16[48,1152]{1,0:T(8,128)(2,1)S(1)} collective-permute-done((bf16[48,1152]{1,0:T(8,128)(2,1)S(1)}, bf16[48,1152]{1,0:T(8,128)(2,1)S(1)}, u32[]{:S(2)}, u32[]{:S(2)}) %collective-permute-start.18) | collective-permute-done | bytes 110624 | tf_op jit(solution)/shard_map/ppermute | solution.py:993
  452.0 1.2 collective-permute-done.14
  455.7 1.7 select_bitcast_fusion.2
  458.3 1.9 pad_maximum_fusion.3
  (99 shorter events, 12.6 us)
Async XLA Ops:
  7.2 56.7 %all-gather.7.cloned.1.call-start = ((), (), s32[]{:S(2)}) async-start(), calls=%async_computation.2 | async-start | bytes 4386816 | tf_op jit(solution)/shard_map/all_gather | solution.py:1008
  10.2 143.1 %all-gather.9.cloned.1.call-start = ((), (), s32[]{:S(2)}) async-start(), calls=%async_computation.3 | async-start | bytes 11280384 | tf_op jit(solution)/shard_map/all_gather | solution.py:1018
  13.2 4.9 %collective-permute-start.1 = (bf16[648,768]{1,0:T(8,128)(2,1)}, bf16[648,768]{1,0:T(8,128)(2,1)}, u32[]{:S(2)}, u32[]{:S(2)}) collective-permute-start(bf16[648,768]{1,0:T(8,128)(2,1)} %get-tuple-element.132), channel_id=1, source_target_pairs={{16,1},{1,16},{18,3},{3,18},{20,5},{5,20},{22,7},{7,22},{24,9},{9,... | collective-permute-start | bytes 2985992 | tf_op jit(solution)/shard_map/ppermute | solution.py:971
  14.9 36.9 %collective-permute-start = (bf16[648,768]{1,0:T(8,128)(2,1)S(1)}, bf16[648,768]{1,0:T(8,128)(2,1)S(1)}, u32[]{:S(2)}, u32[]{:S(2)}) collective-permute-start(bf16[648,768]{1,0:T(8,128)(2,1)S(1)} %get-tuple-element.133), channel_id=1, source_target_pairs={{0,16},{16,0},{1,17},{17,1},{2,18},{18,2},{3,19},{19,3},{4,20},{20... | collective-permute-start | bytes 2985992 | tf_op jit(solution)/shard_map/ppermute | solution.py:974
  51.8 1.9 copy-start.12
  51.8 2.0 copy-start.13
  51.8 2.0 copy-start.14
  53.9 0.8 copy-start.9
  54.7 350.1 %reduce-scatter.2.cloned.1.call-start = ((), (), s32[]{:S(2)}) async-start(), calls=%async_computation.1 | async-start | bytes 11280384 | tf_op jit(solution)/shard_map/reduce_scatter | solution.py:1056
  65.3 14.4 %copy-start.1 = (bf16[3,648,768]{2,1,0:T(8,128)(2,1)S(1)}, bf16[3,648,768]{2,1,0:T(8,128)(2,1)}, u32[]{:S(2)}) copy-start(bf16[3,648,768]{2,1,0:T(8,128)(2,1)} %param.18) | copy-start | bytes 8957956
  81.3 43.4 %collective-permute-start.4 = (bf16[648,768]{1,0:T(8,128)(2,1)}, bf16[648,768]{1,0:T(8,128)(2,1)}, u32[]{:S(2)}, u32[]{:S(2)}) collective-permute-start(bf16[648,768]{1,0:T(8,128)(2,1)} %get-tuple-element.129), channel_id=1, source_target_pairs={{16,1},{1,16},{18,3},{3,18},{20,5},{5,20},{22,7},{7,22},{24,9},{9,... | collective-permute-start | bytes 2985992 | tf_op jit(solution)/shard_map/ppermute | solution.py:971
  82.9 43.1 %collective-permute-start.3 = (bf16[648,768]{1,0:T(8,128)(2,1)}, bf16[648,768]{1,0:T(8,128)(2,1)}, u32[]{:S(2)}, u32[]{:S(2)}) collective-permute-start(bf16[648,768]{1,0:T(8,128)(2,1)} %get-tuple-element.130), channel_id=1, source_target_pairs={{0,16},{16,0},{1,17},{17,1},{2,18},{18,2},{3,19},{19,3},{4,20},{20... | collective-permute-start | bytes 2985992 | tf_op jit(solution)/shard_map/ppermute | solution.py:974
  85.1 44.0 %collective-permute-start.2 = (bf16[2,648,768]{2,1,0:T(8,128)(2,1)}, bf16[2,648,768]{2,1,0:T(8,128)(2,1)S(1)}, u32[]{:S(2)}, u32[]{:S(2)}) collective-permute-start(bf16[2,648,768]{2,1,0:T(8,128)(2,1)} %get-tuple-element.78), channel_id=1, source_target_pairs={{0,1},{1,0},{2,3},{3,2},{4,5},{5,4},{6,7},{7,6},{8,9},{9,8},{10,11... | collective-permute-start | bytes 5971976 | tf_op jit(solution)/shard_map/ppermute | solution.py:1025
  129.2 1.3 copy-start
  257.6 195.6 %all-gather.11.cloned.1.call-start = ((), (), s32[]{:S(2)}) async-start(), calls=%async_computation.4 | async-start | bytes 1671168 | tf_op jit(solution)/shard_map/all_gather | solution.py:1067
  257.7 34.0 %copy-start.2 = (bf16[3,648,768]{2,1,0:T(8,128)(2,1)S(1)}, bf16[3,648,768]{2,1,0:T(8,128)(2,1)}, u32[]{:S(2)}) copy-start(bf16[3,648,768]{2,1,0:T(8,128)(2,1)} %get-tuple-element.85) | copy-start | bytes 8957956
  291.4 71.0 %collective-permute-start.5 = (bf16[2,1,648,768]{3,2,1,0:T(8,128)(2,1)}, bf16[2,1,648,768]{3,2,1,0:T(8,128)(2,1)}, u32[]{:S(2)}, u32[]{:S(2)}) collective-permute-start(bf16[2,1,648,768]{3,2,1,0:T(8,128)(2,1)} %get-tuple-element.98), channel_id=1, source_target_pairs={{0,1},{1,0},{2,3},{3,2},{4,5},{5,4},{6,7},{7,6},{8,9},{9,8},{10,11... | collective-permute-start | bytes 5971976 | tf_op jit(solution)/shard_map/ppermute | solution.py:1058
  293.1 72.8 %collective-permute-start.6 = (bf16[648,768]{1,0:T(8,128)(2,1)}, bf16[648,768]{1,0:T(8,128)(2,1)S(1)}, u32[]{:S(2)}, u32[]{:S(2)}) collective-permute-start(bf16[648,768]{1,0:T(8,128)(2,1)} %get-tuple-element.127), channel_id=1, source_target_pairs={{0,16},{16,0},{1,17},{17,1},{2,18},{18,2},{3,19},{19,3},{4,20},{20... | collective-permute-start | bytes 2985992 | tf_op jit(solution)/shard_map/ppermute | solution.py:982
  294.5 71.3 %collective-permute-start.7 = (bf16[648,768]{1,0:T(8,128)(2,1)}, bf16[648,768]{1,0:T(8,128)(2,1)S(1)}, u32[]{:S(2)}, u32[]{:S(2)}) collective-permute-start(bf16[648,768]{1,0:T(8,128)(2,1)} %get-tuple-element.126), channel_id=1, source_target_pairs={{16,1},{1,16},{18,3},{3,18},{20,5},{5,20},{22,7},{7,22},{24,9},{9,... | collective-permute-start | bytes 2985992 | tf_op jit(solution)/shard_map/ppermute | solution.py:983
  295.3 67.2 %copy-start.4 = (bf16[2,1,648,768]{3,2,1,0:T(8,128)(2,1)S(1)}, bf16[2,1,648,768]{3,2,1,0:T(8,128)(2,1)}, u32[]{:S(2)}) copy-start(bf16[2,1,648,768]{3,2,1,0:T(8,128)(2,1)} %get-tuple-element.97) | copy-start | bytes 5971972
  365.9 17.7 %copy-start.6 = (bf16[648,768]{1,0:T(8,128)(2,1)}, bf16[648,768]{1,0:T(8,128)(2,1)S(1)}, u32[]{:S(2)}) copy-start(bf16[648,768]{1,0:T(8,128)(2,1)S(1)} %collective-permute-done.6) | copy-start | bytes 2985988
  365.9 17.7 %copy-start.8 = (bf16[648,768]{1,0:T(8,128)(2,1)}, bf16[648,768]{1,0:T(8,128)(2,1)S(1)}, u32[]{:S(2)}) copy-start(bf16[648,768]{1,0:T(8,128)(2,1)S(1)} %collective-permute-done.7) | copy-start | bytes 2985988
  397.6 5.3 %collective-permute-start.10 = (bf16[2,8,48,1152]{3,2,1,0:T(8,128)(2,1)}, bf16[2,8,48,1152]{3,2,1,0:T(8,128)(2,1)S(1)}, u32[]{:S(2)}, u32[]{:S(2)}) collective-permute-start(bf16[2,8,48,1152]{3,2,1,0:T(8,128)(2,1)} %get-tuple-element.113), channel_id=1, source_target_pairs={{0,1},{1,0},{2,3},{3,2},{4,5},{5,4},{6,7},{7,6},{8,9},{9,8},{10,11... | collective-permute-start | bytes 5308424 | tf_op jit(solution)/shard_map/ppermute | solution.py:1077
  399.4 53.8 %collective-permute-start.8 = (bf16[648,768]{1,0:T(8,128)(2,1)}, bf16[648,768]{1,0:T(8,128)(2,1)}, u32[]{:S(2)}, u32[]{:S(2)}) collective-permute-start(bf16[648,768]{1,0:T(8,128)(2,1)} %get-tuple-element.106), channel_id=1, source_target_pairs={{0,16},{16,0},{1,17},{17,1},{2,18},{18,2},{3,19},{19,3},{4,20},{20... | collective-permute-start | bytes 2985992 | tf_op jit(solution)/shard_map/ppermute | solution.py:982
  400.4 52.8 %collective-permute-start.9 = (bf16[648,768]{1,0:T(8,128)(2,1)}, bf16[648,768]{1,0:T(8,128)(2,1)}, u32[]{:S(2)}, u32[]{:S(2)}) collective-permute-start(bf16[648,768]{1,0:T(8,128)(2,1)} %get-tuple-element.107), channel_id=1, source_target_pairs={{16,1},{1,16},{18,3},{3,18},{20,5},{5,20},{22,7},{7,22},{24,9},{9,... | collective-permute-start | bytes 2985992 | tf_op jit(solution)/shard_map/ppermute | solution.py:983
  404.8 1.2 copy-start.7
  404.9 2.1 copy-start.3
  405.1 15.1 %collective-permute-start.15 = (bf16[4,48,1152]{2,1,0:T(8,128)(2,1)S(1)}, bf16[4,48,1152]{2,1,0:T(8,128)(2,1)S(1)}, u32[]{:S(2)}, u32[]{:S(2)}) collective-permute-start(bf16[4,48,1152]{2,1,0:T(8,128)(2,1)S(1)} %dynamic-slice_bitcast_fusion.2), channel_id=1, source_target_pairs={{0,4},{1,5},{2,6},{3,7},{4,0},{5,1},{6,2},{7,3},{8,12},{9,13},{10,... | collective-permute-start | bytes 1327112 | tf_op jit(solution)/shard_map/ppermute | solution.py:935
  407.2 2.6 copy-start.10
  409.2 13.3 %collective-permute-start.11 = (bf16[4,48,1152]{2,1,0:T(8,128)(2,1)S(1)}, bf16[4,48,1152]{2,1,0:T(8,128)(2,1)S(1)}, u32[]{:S(2)}, u32[]{:S(2)}) collective-permute-start(bf16[4,48,1152]{2,1,0:T(8,128)(2,1)S(1)} %dynamic-slice_bitcast_fusion.3), channel_id=1, source_target_pairs={{0,2},{1,3},{2,0},{3,1},{4,6},{5,7},{6,4},{7,5},{8,10},{9,11},{10,... | collective-permute-start | bytes 1327112 | tf_op jit(solution)/shard_map/ppermute | solution.py:935
  409.8 43.4 %collective-permute-start.19 = (bf16[432,768]{1,0:T(8,128)(2,1)S(1)}, bf16[432,768]{1,0:T(8,128)(2,1)S(1)}, u32[]{:S(2)}, u32[]{:S(2)}) collective-permute-start(bf16[432,768]{1,0:T(8,128)(2,1)S(1)} %bitcast.135), channel_id=1, source_target_pairs={{0,16},{16,0},{1,17},{17,1},{2,18},{18,2},{3,19},{19,3},{4,20},{20... | collective-permute-start | bytes 1990664 | tf_op jit(solution)/shard_map/ppermute | solution.py:1079
  420.4 16.6 %collective-permute-start.16 = (bf16[2,48,1152]{2,1,0:T(8,128)(2,1)S(1)}, bf16[2,48,1152]{2,1,0:T(8,128)(2,1)S(1)}, u32[]{:S(2)}, u32[]{:S(2)}) collective-permute-start(bf16[2,48,1152]{2,1,0:T(8,128)(2,1)S(1)} %dynamic-slice_bitcast_fusion.4), channel_id=1, source_target_pairs={{0,8},{1,9},{2,10},{3,11},{4,12},{5,13},{6,14},{7,15},{8,0},{9,1},... | collective-permute-start | bytes 663560 | tf_op jit(solution)/shard_map/ppermute | solution.py:935
  422.6 17.8 %collective-permute-start.12 = (bf16[2,48,1152]{2,1,0:T(8,128)(2,1)S(1)}, bf16[2,48,1152]{2,1,0:T(8,128)(2,1)S(1)}, u32[]{:S(2)}, u32[]{:S(2)}) collective-permute-start(bf16[2,48,1152]{2,1,0:T(8,128)(2,1)S(1)} %dynamic-slice_bitcast_fusion.5), channel_id=1, source_target_pairs={{0,4},{1,5},{2,6},{3,7},{4,0},{5,1},{6,2},{7,3},{8,12},{9,13},{10,... | collective-permute-start | bytes 663560 | tf_op jit(solution)/shard_map/ppermute | solution.py:935
  437.0 5.0 %collective-permute-start.17 = (bf16[1,48,1152]{2,1,0:T(8,128)(2,1)S(1)}, bf16[1,48,1152]{2,1,0:T(8,128)(2,1)S(1)}, u32[]{:S(2)}, u32[]{:S(2)}) collective-permute-start(bf16[1,48,1152]{2,1,0:T(8,128)(2,1)S(1)} %constant_dynamic-slice_fusion.1), channel_id=1, source_target_pairs={{0,2},{1,3},{2,0},{3,1},{4,6},{5,7},{6,4},{7,5},{8,10},{9,11},{10,... | collective-permute-start | bytes 331784 | tf_op jit(solution)/shard_map/ppermute | solution.py:935
  440.5 6.4 %collective-permute-start.13 = (bf16[1,48,1152]{2,1,0:T(8,128)(2,1)S(1)}, bf16[1,48,1152]{2,1,0:T(8,128)(2,1)S(1)}, u32[]{:S(2)}, u32[]{:S(2)}) collective-permute-start(bf16[1,48,1152]{2,1,0:T(8,128)(2,1)S(1)} %constant_dynamic-slice_fusion.2), channel_id=1, source_target_pairs={{0,8},{1,9},{2,10},{3,11},{4,12},{5,13},{6,14},{7,15},{8,0},{9,1},... | collective-permute-start | bytes 331784 | tf_op jit(solution)/shard_map/ppermute | solution.py:935
  442.1 9.9 %collective-permute-start.18 = (bf16[48,1152]{1,0:T(8,128)(2,1)S(1)}, bf16[48,1152]{1,0:T(8,128)(2,1)S(1)}, u32[]{:S(2)}, u32[]{:S(2)}) collective-permute-start(bf16[48,1152]{1,0:T(8,128)(2,1)S(1)} %fusion.8), channel_id=1, source_target_pairs={{0,16},{16,0},{1,17},{17,1},{2,18},{18,2},{3,19},{19,3},{4,20},{20... | collective-permute-start | bytes 331784 | tf_op jit(solution)/shard_map/ppermute | solution.py:993
  446.9 6.2 %collective-permute-start.14 = (bf16[48,1152]{1,0:T(8,128)(2,1)S(1)}, bf16[48,1152]{1,0:T(8,128)(2,1)S(1)}, u32[]{:S(2)}, u32[]{:S(2)}) collective-permute-start(bf16[48,1152]{1,0:T(8,128)(2,1)S(1)} %fusion.7), channel_id=1, source_target_pairs={{0,16},{16,0},{1,17},{17,1},{2,18},{18,2},{3,19},{19,3},{4,20},{20... | collective-permute-start | bytes 331784 | tf_op jit(solution)/shard_map/ppermute | solution.py:993
  453.2 2.5 copy-start.5
  453.2 1.5 copy-start.11
  454.8 6.3 %collective-permute-start.20 = (f32[12,768]{1,0:T(8,128)S(1)}, f32[12,768]{1,0:T(8,128)S(1)}, u32[]{:S(2)}, u32[]{:S(2)}) collective-permute-start(f32[12,768]{1,0:T(8,128)S(1)} %slice_reduce_fusion), channel_id=1, source_target_pairs={{0,16},{16,0},{1,17},{17,1},{2,18},{18,2},{3,19},{19,3},{4,20},{20... | collective-permute-start | bytes 110600 | tf_op jit(solution)/shard_map/ppermute | solution.py:993
Sparse Core Ops, SparseCore 0:
  10.9 52.9 all-gather.6
  66.1 87.1 all-gather.8
  257.7 118.3 reduce-scatter.1
  402.1 44.7 all-gather.10
